TPU v7x, 256 devices: a whole 4x4x8 slice. The times are simulated.
256 devices in a mesh: dp: 4 (over x_hi, core), rows: 64 (over y, x_lo, z).
Axes of the slice: x: 4 (x_hi: 2, x_lo: 2; x = x_hi * 2 + x_lo), y: 4, z: 8, core: 2. Of those that a mesh axis runs over, the one named last changes fastest.
Arguments:
- image: bfloat16 [4, 192, 48, 512], P('dp', 'rows'), may hold values from -6 to 6
- out_grad: bfloat16 [4, 192, 48, 512], P('dp', 'rows'), may hold values from -1 to 1
- w_qkv: bfloat16 [2, 512, 768], replicated
- w_proj: bfloat16 [2, 256, 512], replicated, may hold values from -0.375 to 0.375
- norm_gain: float32 [2, 512], replicated, may hold values from 0.25 to 1.75
- norm_bias: float32 [2, 512], replicated, may hold values from -3 to 3
- logit_scale: float32 [2, 8], replicated, may hold values from 1.6 to 2.8
- row_band: int32 [192], replicated, may hold values from 0 to 2, as said below
- col_band: int32 [48], replicated, may hold values from 0 to 2, as said below
Outputs:
- grad_image: bfloat16 [4, 192, 48, 512], P('dp', 'rows')
- grad_qkv: float32 [2, 512, 768], P(None, 'rows')
- grad_proj: float32 [2, 256, 512], P(None, None, 'rows')
- grad_gain: float32 [2, 512], P(None, 'rows')
- grad_bias: float32 [2, 512], P(None, 'rows')
Inputs may be any that keep to these rules, and one draw needn't show every extreme that they name: `row_band`: labels never fall from one row to the next, and every label 0, 1, 2 occurs. `col_band`: labels never fall from one column to the next, and every label 0, 1, 2 occurs.
All inputs are finite; a program needn't handle non-finite values.
Results may differ from a plain program's by a relative error of at most 0.025.
Values may be sent and summed in bfloat16 or wider, within the bound.
No kernel may reach another device: no remote copies, remote signals or barrier semaphores. Data moves between devices by JAX's collectives and lax.ppermute only.
A program may use at most 64 MiB of HBM per device.

v0:
```python
import jax
import jax.numpy as jnp
from jax import lax
from jax.sharding import PartitionSpec as P

C = 512
HEADS = 8
HD = 32
WIN = 24
HH = 256
SHIFT = 12


norm_eps = 1e-05
mask_value = -100.0


def swapped(block, axis, apart):
    count = lax.axis_size(axis)
    route = []
    for low in range(count):
        high = low | 1 << apart
        if high != low and high < count:
            route += [(low, high), (high, low)]
    return lax.ppermute(block, axis, route)


def shifted(shard, axis, by):
    size = lax.axis_size(axis)
    return lax.ppermute(shard, axis, [(i, (i + by) % size) for i in range(size)])


def project(tokens, weight, log_scale):
    token_count = tokens.shape[0]
    projected = jnp.dot(tokens, weight, preferred_element_type=jnp.float32)
    queries = projected[:, :HH].reshape(token_count, HEADS, HD)
    key_part = projected[:, HH : 2 * HH].reshape(token_count, HEADS, HD)
    temper = jnp.exp(log_scale)[None, :, None]
    q_factor = lax.rsqrt(1.0 + jnp.sum(queries * queries, -1, keepdims=True))
    k_factor = lax.rsqrt(1.0 + jnp.sum(key_part * key_part, -1, keepdims=True))
    q_hat = (queries * q_factor * temper).reshape(token_count, HH).astype(jnp.bfloat16)
    k_hat = (key_part * k_factor).reshape(token_count, HH).astype(jnp.bfloat16)
    return (q_hat, k_hat, projected[:, 2 * HH :].astype(jnp.bfloat16))


def project_back(tokens, weight, log_scale, grad_q, grad_k, grad_v):
    token_count = tokens.shape[0]
    projected = jnp.dot(tokens, weight, preferred_element_type=jnp.float32)
    queries = projected[:, :HH].reshape(token_count, HEADS, HD)
    key_part = projected[:, HH : 2 * HH].reshape(token_count, HEADS, HD)
    temper = jnp.exp(log_scale)[None, :, None]
    q_factor = lax.rsqrt(1.0 + jnp.sum(queries * queries, -1, keepdims=True))
    k_factor = lax.rsqrt(1.0 + jnp.sum(key_part * key_part, -1, keepdims=True))
    q_unit = queries * q_factor
    k_unit = key_part * k_factor
    scaled = grad_q.reshape(token_count, HEADS, HD) * temper
    d_query = q_factor * (scaled - q_unit * jnp.sum(q_unit * scaled, -1, keepdims=True))
    k_grad = grad_k.reshape(token_count, HEADS, HD)
    d_key = k_factor * (k_grad - k_unit * jnp.sum(k_unit * k_grad, -1, keepdims=True))
    d_projected = jnp.concatenate(
        [d_query.reshape(token_count, HH), d_key.reshape(token_count, HH), grad_v], 1
    ).astype(jnp.bfloat16)
    grad_weight = lax.dot_general(
        tokens, d_projected, (((0,), (0,)), ((), ())), preferred_element_type=jnp.float32
    )
    grad_tokens = lax.dot_general(
        d_projected, weight, (((1,), (1,)), ((), ())), preferred_element_type=jnp.float32
    )
    return (grad_tokens, grad_weight)


def normalized(attended, weight):
    outputs = jnp.dot(attended, weight, preferred_element_type=jnp.float32)
    centered = outputs - jnp.mean(outputs, -1, keepdims=True)
    inverse = lax.rsqrt(jnp.mean(centered * centered, -1, keepdims=True) + norm_eps)
    return (centered * inverse, inverse)


def finish(tokens, attended, weight, gain_row, offset):
    y_hat, inverse = normalized(attended, weight)
    return (tokens.astype(jnp.float32) + y_hat * gain_row + offset).astype(jnp.bfloat16)


def finish_back(attended, weight, gain_row, grad_out):
    y_hat, inverse = normalized(attended, weight)
    grad_gain = jnp.sum(grad_out * y_hat, 0)
    grad_offset = jnp.sum(grad_out, 0)
    scaled = grad_out * gain_row
    grad_y = inverse * (
        scaled
        - jnp.mean(scaled, -1, keepdims=True)
        - y_hat * jnp.mean(scaled * y_hat, -1, keepdims=True)
    )
    grad_y = grad_y.astype(jnp.bfloat16)
    grad_weight = lax.dot_general(
        attended, grad_y, (((0,), (0,)), ((), ())), preferred_element_type=jnp.float32
    )
    grad_attended = lax.dot_general(
        grad_y, weight, (((1,), (1,)), ((), ())), preferred_element_type=jnp.float32
    ).astype(jnp.bfloat16)
    return (grad_attended, grad_weight, grad_gain, grad_offset)


def heads_first(array):
    return array.transpose(2, 0, 1, 3)


def attend_heads(q_win, k_win, v_win, allowed):

    def one_head(head_item):
        q_head, k_head, v_head = head_item
        scores = jnp.einsum("wqd,wkd->wqk", q_head, k_head, preferred_element_type=jnp.float32)
        if allowed is not None:
            scores = scores + jnp.where(allowed, 0.0, mask_value)
        highest = jnp.max(scores, -1, keepdims=True)
        weights = jnp.exp(scores - highest)
        softmaxed = (weights / jnp.sum(weights, -1, keepdims=True)).astype(jnp.bfloat16)
        attended = jnp.einsum(
            "wqk,wkd->wqd", softmaxed, v_head, preferred_element_type=jnp.float32
        ).astype(jnp.bfloat16)
        return (attended, softmaxed)

    attended, softmaxed = lax.map(
        one_head, (heads_first(q_win), heads_first(k_win), heads_first(v_win))
    )
    return (attended.transpose(1, 2, 0, 3), softmaxed)


def attend_heads_back(q_win, k_win, v_win, softmaxed, grad_attended):

    def one_head(head_item):
        q_head, k_head, v_head, soft_head, grad_head = head_item
        grad_soft = jnp.einsum(
            "wqd,wkd->wqk", grad_head, v_head, preferred_element_type=jnp.float32
        )
        soft_float = soft_head.astype(jnp.float32)
        row_total = jnp.sum(soft_float * grad_soft, -1, keepdims=True)
        grad_scores = (soft_float * (grad_soft - row_total)).astype(jnp.bfloat16)
        grad_q = jnp.einsum("wqk,wkd->wqd", grad_scores, k_head, preferred_element_type=jnp.float32)
        grad_k = jnp.einsum("wqk,wqd->wkd", grad_scores, q_head, preferred_element_type=jnp.float32)
        grad_v = jnp.einsum(
            "wqk,wqd->wkd", soft_head, grad_head, preferred_element_type=jnp.float32
        )
        return (grad_q, grad_k, grad_v)

    grad_q, grad_k, grad_v = lax.map(
        one_head,
        (
            heads_first(q_win),
            heads_first(k_win),
            heads_first(v_win),
            softmaxed,
            heads_first(grad_attended),
        ),
    )
    return (
        grad_q.transpose(1, 2, 0, 3),
        grad_k.transpose(1, 2, 0, 3),
        grad_v.transpose(1, 2, 0, 3),
    )


def query_windows(flat_rows, rows_dev, windows_across):
    return (
        flat_rows.reshape(rows_dev, windows_across, WIN, HEADS, HD)
        .transpose(1, 0, 2, 3, 4)
        .reshape(windows_across, rows_dev * WIN, HEADS, HD)
    )


def query_flat(windows, rows_dev, windows_across):
    return (
        windows.reshape(windows_across, rows_dev, WIN, HH)
        .transpose(1, 0, 2, 3)
        .reshape(rows_dev * windows_across * WIN, HH)
    )


def key_windows(gathered, windows_across):
    return (
        gathered.reshape(WIN, windows_across, WIN, 2, HEADS, HD)
        .transpose(1, 0, 2, 3, 4, 5)
        .reshape(windows_across, WIN * WIN, 2, HEADS, HD)
    )


def key_map(windows, group_size, rows_dev, windows_across):
    return (
        windows.reshape(windows_across, WIN, WIN, 2 * HH)
        .transpose(1, 0, 2, 3)
        .reshape(group_size, rows_dev, windows_across * WIN, 2 * HH)
    )


def layout_order(bit_order, levels):
    return [levels - 1 - bit_order.index(levels - 1 - axis_index) for axis_index in range(levels)]


def collect(local, bit_order, position):
    levels = len(bit_order)
    gathered = local[None]
    for bit_index in bit_order:
        partner = swapped(gathered, "rows", bit_index)
        is_lower = position >> bit_index & 1 == 0
        gathered = jnp.where(
            is_lower,
            jnp.concatenate([gathered, partner], 0),
            jnp.concatenate([partner, gathered], 0),
        )
    shape_rest = local.shape
    axis_order = layout_order(bit_order, levels)
    gathered = gathered.reshape((2,) * levels + shape_rest)
    gathered = gathered.transpose(
        tuple(axis_order) + tuple(range(levels, levels + len(shape_rest)))
    )
    return gathered.reshape((1 << levels,) + shape_rest)


def spread(partials, bit_order, position):
    levels = len(bit_order)
    axis_order = layout_order(bit_order, levels)
    inverse = [axis_order.index(axis_index) for axis_index in range(levels)]
    shape_rest = partials.shape[1:]
    summed = partials.reshape((2,) * levels + shape_rest)
    summed = summed.transpose(tuple(inverse) + tuple(range(levels, levels + len(shape_rest))))
    summed = summed.reshape((1 << levels,) + shape_rest)
    for bit_index in reversed(bit_order):
        half_size = summed.shape[0] // 2
        is_lower = position >> bit_index & 1 == 0
        kept_half = jnp.where(is_lower, summed[:half_size], summed[half_size:])
        sent_half = jnp.where(is_lower, summed[half_size:], summed[:half_size])
        summed = kept_half + swapped(sent_half.astype(jnp.bfloat16), "rows", bit_index).astype(
            sent_half.dtype
        )
    return summed[0]


def roll_rows(local, steps):
    return shifted(local, "rows", steps)


def block_forward(tokens, params, allowed, layout):
    w_mix, w_out, gain_row, offset, log_scale = params
    rows_dev, windows_across, group_size, bit_order, position = layout
    flat_tokens = tokens.reshape(-1, C)
    q_hat, k_hat, values = project(flat_tokens, w_mix, log_scale)
    joined = jnp.concatenate([k_hat, values], 1).reshape(rows_dev, windows_across * WIN, 2 * HH)
    window_keys = key_windows(collect(joined, bit_order, position), windows_across)
    q_win = query_windows(q_hat, rows_dev, windows_across)
    attended_win, softmaxed = attend_heads(
        q_win, window_keys[:, :, 0], window_keys[:, :, 1], allowed
    )
    attended = query_flat(attended_win, rows_dev, windows_across)
    return (flat_tokens, attended, q_win, window_keys, softmaxed)


def block_backward(saved_state, params, grad_in, layout):
    flat_tokens, attended, q_win, window_keys, softmaxed = saved_state
    w_mix, w_out, gain_row, offset, log_scale = params
    rows_dev, windows_across, group_size, bit_order, position = layout
    grad_att, grad_proj, grad_gain, grad_offset = finish_back(attended, w_out, gain_row, grad_in)
    grad_att_win = query_windows(grad_att, rows_dev, windows_across)
    grad_q, grad_k, grad_v = attend_heads_back(
        q_win, window_keys[:, :, 0], window_keys[:, :, 1], softmaxed, grad_att_win
    )
    partials = key_map(jnp.stack([grad_k, grad_v], 2), group_size, rows_dev, windows_across)
    own_grads = spread(partials, bit_order, position).reshape(-1, 2 * HH)
    grad_from, grad_mix = project_back(
        flat_tokens,
        w_mix,
        log_scale,
        query_flat(grad_q, rows_dev, windows_across),
        own_grads[:, :HH],
        own_grads[:, HH:],
    )
    return (grad_in + grad_from, (grad_mix, grad_proj, grad_gain, grad_offset))


def body(image, out_grad, w_qkv, w_proj, norm_gain, norm_bias, logit_scale, row_band, col_band):
    rows_dev = image.shape[1]
    map_width = image.shape[2]
    windows_across = map_width // WIN
    group_size = WIN // rows_dev
    levels = group_size.bit_length() - 1
    half_group = group_size // 2
    position = lax.axis_index("rows")
    bit_order = list(range(levels))
    layout = (rows_dev, windows_across, group_size, bit_order, position)
    first_params = (w_qkv[0], w_proj[0], norm_gain[0], norm_bias[0], logit_scale[0])
    second_params = (w_qkv[1], w_proj[1], norm_gain[1], norm_bias[1], logit_scale[1])
    own_rows = lax.dynamic_slice_in_dim(row_band, position * rows_dev, rows_dev, 0)
    window_rows = lax.dynamic_slice_in_dim(row_band, position // group_size * WIN, WIN, 0)
    q_labels = (3 * own_rows[:, None] + col_band[None, :]).reshape(rows_dev, windows_across, WIN)
    q_labels = q_labels.transpose(1, 0, 2).reshape(windows_across, rows_dev * WIN)
    k_labels = (3 * window_rows[:, None] + col_band[None, :]).reshape(WIN, windows_across, WIN)
    k_labels = k_labels.transpose(1, 0, 2).reshape(windows_across, WIN * WIN)
    allowed = q_labels[:, :, None] == k_labels[:, None, :]
    saved_first = block_forward(image[0], first_params, None, layout)
    out_first = finish(
        saved_first[0], saved_first[1], w_proj[0], norm_gain[0], norm_bias[0]
    ).reshape(rows_dev, map_width, C)
    rolled = jnp.roll(roll_rows(out_first, -half_group), -SHIFT, 1)
    saved_second = block_forward(rolled, second_params, allowed, layout)
    grad_rolled = jnp.roll(roll_rows(out_grad[0], -half_group), -SHIFT, 1)
    grad_second, grads_second = block_backward(
        saved_second, second_params, grad_rolled.reshape(-1, C).astype(jnp.float32), layout
    )
    grad_back = grad_second.astype(jnp.bfloat16).reshape(rows_dev, map_width, C)
    grad_first_in = roll_rows(jnp.roll(grad_back, SHIFT, 1), half_group)
    grad_input, grads_first = block_backward(
        saved_first, first_params, grad_first_in.reshape(-1, C).astype(jnp.float32), layout
    )
    grad_image = grad_input.astype(jnp.bfloat16).reshape(1, rows_dev, map_width, C)
    weight_grads = tuple(
        (
            jnp.stack([early_grad, late_grad])
            for early_grad, late_grad in zip(grads_first, grads_second)
        )
    )
    share_rows = C // lax.axis_size("rows")
    totals = lax.psum(
        (weight_grads[0], weight_grads[1], weight_grads[2], weight_grads[3]), ("dp", "rows")
    )
    first_row = position * share_rows
    result = (
        lax.dynamic_slice_in_dim(totals[0], first_row, share_rows, 1),
        lax.dynamic_slice_in_dim(totals[1], first_row, share_rows, 2),
        lax.dynamic_slice_in_dim(totals[2], first_row, share_rows, 1),
        lax.dynamic_slice_in_dim(totals[3], first_row, share_rows, 1),
    )
    return (grad_image, result[0], result[1], result[2], result[3])


def solution(mesh):
    placed = (
        P("dp", "rows", None, None),
        P("dp", "rows", None, None),
        P(),
        P(),
        P(),
        P(),
        P(),
        P(),
        P(),
    )
    return jax.shard_map(
        body,
        mesh=mesh,
        in_specs=placed,
        out_specs=(
            P("dp", "rows", None, None),
            P(None, "rows", None),
            P(None, None, "rows"),
            P(None, "rows"),
            P(None, "rows"),
        ),
        check_vma=False,
    )
```

profile of v0, /device:TPU:1, one launch (start us, length us, event | category | flops | bytes accessed | tf_op | source)
XLA Modules:
  0.0 757.8 jit_solution(4765835421974957139)
XLA Ops:
  7.2 1.5 fusion.127
  10.7 2.6 collective-permute-start.1
  13.3 2.5 collective-permute-done.1
  15.9 4.0 collective-permute-start.2
  19.9 12.7 %collective-permute-done.2 = bf16[2,3,48,512]{3,2,1,0:T(8,128)(2,1)S(1)} collective-permute-done((bf16[2,3,48,512]{3,2,1,0:T(8,128)(2,1)S(1)}, bf16[2,3,48,512]{3,2,1,0:T(8,128)(2,1)S(1)}, u32[]{:S(2)}, u32[]{:S(2)}) %collective-permute-start.2) | collective-permute-done | bytes 294944 | tf_op jit(solution)/shard_map/ppermute | solution.py:25
  32.7 6.5 collective-permute-start.3
  40.3 24.6 %collective-permute-done.3 = bf16[4,3,48,512]{3,2,1,0:T(8,128)(2,1)} collective-permute-done((bf16[4,3,48,512]{3,2,1,0:T(8,128)(2,1)S(1)}, bf16[4,3,48,512]{3,2,1,0:T(8,128)(2,1)}, u32[]{:S(2)}, u32[]{:S(2)}) %collective-permute-start.3) | collective-permute-done | bytes 589856 | tf_op jit(solution)/shard_map/ppermute | solution.py:25
  64.9 1.5 maximum_select_fusion
  66.3 4.1 select_n.139
  70.5 11.3 %copy.81 = bf16[2,24,24,2,8,32]{2,1,5,4,3,0:T(8,128)(2,1)} copy(bf16[2,24,24,2,8,32]{5,4,3,2,0,1:T(8,128)(2,1)} %bitcast.443) | data formatting | bytes 2359296 | tf_op jit(solution)/shard_map/transpose | solution.py:182
  81.8 7.5 reshape.300
  90.6 16.0 %while.53 = (s32[]{:T(128)}, bf16[8,2,72,32]{2,3,1,0:T(8,128)(2,1)S(1)}, bf16[8,2,72,576]{3,2,1,0:T(8,128)(2,1)S(1)}, bf16[8,2,72,32]{2,3,1,0:T(8,128)(2,1)S(1)}...) while((s32[]{:T(128)}, bf16[8,2,72,32]{2,3,1,0:T(8,128)(2,1)S(1)}, ...), condition=%wide.region_5.6_spmd, body=%wide.region_2.5_spmd.sunk | while | flops 16511760 | bytes 1185425 | solution.py:123
  109.5 6.0 collective-permute-start.4
  115.6 3.3 collective-permute-done.4
  119.1 1.5 fusion.124
  122.6 7.5 collective-permute-start
  130.5 4.8 collective-permute-start.6
  136.2 17.2 %collective-permute-done.6 = bf16[2,3,48,512]{3,2,1,0:T(8,128)(2,1)S(1)} collective-permute-done((bf16[2,3,48,512]{3,2,1,0:T(8,128)(2,1)S(1)}, bf16[2,3,48,512]{3,2,1,0:T(8,128)(2,1)S(1)}, u32[]{:S(2)}, u32[]{:S(2)}) %collective-permute-start.6) | collective-permute-done | bytes 294944 | tf_op jit(solution)/shard_map/ppermute | solution.py:25
  157.6 24.6 %collective-permute-done.7 = bf16[4,3,48,512]{3,2,1,0:T(8,128)(2,1)} collective-permute-done((bf16[4,3,48,512]{3,2,1,0:T(8,128)(2,1)S(1)}, bf16[4,3,48,512]{3,2,1,0:T(8,128)(2,1)}, u32[]{:S(2)}, u32[]{:S(2)}) %collective-permute-start.7) | collective-permute-done | bytes 589856 | tf_op jit(solution)/shard_map/ppermute | solution.py:25
  182.2 1.5 maximum_select_fusion.1
  183.7 4.1 select_n.143
  187.8 11.3 %copy.92 = bf16[2,24,24,2,8,32]{2,1,5,4,3,0:T(8,128)(2,1)} copy(bf16[2,24,24,2,8,32]{5,4,3,2,0,1:T(8,128)(2,1)} %bitcast.444) | data formatting | bytes 2359296 | tf_op jit(solution)/shard_map/transpose | solution.py:182
  199.1 7.5 reshape.309
  208.8 23.8 %while.56 = (s32[]{:T(128)}, bf16[8,2,72,32]{2,3,1,0:T(8,128)(2,1)S(1)}, bf16[8,2,72,576]{3,2,1,0:T(8,128)(2,1)S(1)}, bf16[8,2,72,32]{2,3,1,0:T(8,128)(2,1)}, bf...) while((s32[]{:T(128)}, ...), condition=%wide.region_13.14_spmd.clone, body=%wide.region_10.13_spmd.clone.sunk | while | flops 17009424 | bytes 1196769 | solution.py:123
  213.3 1.5 fusion.278
  222.2 1.5 fusion.278
  225.2 1.5 fusion.278
  228.1 1.5 fusion.278
  233.6 1.8 fusion.134
  238.7 38.5 %while.54 = (s32[]{:T(128)}, f32[8,2,72,32]{2,3,1,0:T(8,128)S(1)}, f32[8,2,576,32]{2,3,1,0:T(8,128)}, f32[8,2,576,32]{2,3,1,0:T(8,128)}, bf16[8,2,72,576]{3,2,1,...) while((s32[]{:T(128)}, f32[8,2,72,32]{2,3,1,0:T(8,128)S(1)}, ...), condition=%wide.region_20.21_spmd, body=%wide.region_18.20_spmd.sunk | while | flops 21814128 | bytes 2293993 | solution.py:146
  240.1 1.5 fusion.259
  244.9 1.5 fusion.259
  249.7 1.5 fusion.259
  254.5 1.6 fusion.259
  259.3 1.6 fusion.259
  264.2 1.5 fusion.259
  269.0 1.6 fusion.259
  273.8 1.5 fusion.259
  277.9 1.9 pad_maximum_fusion.1
  279.9 5.2 copy.109
  285.1 6.7 reshape.315
  292.0 3.3 collective-permute-start.8
  295.6 22.5 %collective-permute-done.8 = bf16[4,3,48,512]{3,2,1,0:T(8,128)(2,1)S(1)} collective-permute-done((bf16[4,3,48,512]{3,2,1,0:T(8,128)(2,1)S(1)}, bf16[4,3,48,512]{3,2,1,0:T(8,128)(2,1)S(1)}, u32[]{:S(2)}, u32[]{:S(2)}) %collective-permute-start.8) | collective-permute-done | bytes 589856 | tf_op jit(solution)/shard_map/ppermute | solution.py:25
  322.2 12.5 %collective-permute-done.9 = bf16[2,3,48,512]{3,2,1,0:T(8,128)(2,1)S(1)} collective-permute-done((bf16[2,3,48,512]{3,2,1,0:T(8,128)(2,1)}, bf16[2,3,48,512]{3,2,1,0:T(8,128)(2,1)S(1)}, u32[]{:S(2)}, u32[]{:S(2)}) %collective-permute-start.9) | collective-permute-done | bytes 294944 | tf_op jit(solution)/shard_map/ppermute | solution.py:25
  336.8 2.4 collective-permute-done.10
  340.7 1.8 fusion.119
  346.3 5.6 collective-permute-start.11
  352.0 5.5 collective-permute-done.11
  359.7 43.5 %while.55 = (s32[]{:T(128)}, f32[8,2,72,32]{2,3,1,0:T(8,128)S(1)}, f32[8,2,576,32]{2,3,1,0:T(8,128)S(1)}, f32[8,2,576,32]{2,3,1,0:T(8,128)S(1)}, bf16[8,2,72,576...) while((s32[]{:T(128)}, f32[8,2,72,32]{2,3,1,0:T(8,128)S(1)}, ...), condition=%wide.region_27.28_spmd, body=%wide.region_25.27_spmd.sunk | while | flops 21814128 | bytes 2312425 | solution.py:146
  404.7 1.9 pad_maximum_fusion.2
  406.7 5.2 copy.126
  411.9 6.7 reshape.321
  418.8 2.6 collective-permute-start.12
  422.9 11.3 %collective-permute-done.12 = bf16[4,3,48,512]{3,2,1,0:T(8,128)(2,1)S(1)} collective-permute-done((bf16[4,3,48,512]{3,2,1,0:T(8,128)(2,1)S(1)}, bf16[4,3,48,512]{3,2,1,0:T(8,128)(2,1)S(1)}, u32[]{:S(2)}, u32[]{:S(2)}) %collective-permute-start.12) | collective-permute-done | bytes 589856 | tf_op jit(solution)/shard_map/ppermute | solution.py:25
  435.2 18.7 %collective-permute-start.13 = (bf16[2,3,48,512]{3,2,1,0:T(8,128)(2,1)}, bf16[2,3,48,512]{3,2,1,0:T(8,128)(2,1)}, u32[]{:S(2)}, u32[]{:S(2)}) collective-permute-start(bf16[2,3,48,512]{3,2,1,0:T(8,128)(2,1)} %select_convert_fusion.2), channel_id=1, source_target_pairs={{0,2},{2,0},{1,3},{3,1},{4,6},{6,4},{5,7},{7,5},{8,10},{10,8},{9,1... | collective-permute-start | bytes 884744 | tf_op jit(solution)/shard_map/ppermute | solution.py:25
  454.3 2.0 copy.120
  458.8 2.3 reshape.327
  461.1 1.8 fusion.118
  463.0 4.4 collective-permute-done.13
  472.5 1.8 copy.124
  474.2 2.1 pad_maximum_fusion.3
  481.0 2.0 pad_maximum_fusion
  483.7 74.0 %all-reduce = (f32[2,512]{1,0:T(2,128)S(1)}, f32[2,512]{1,0:T(2,128)S(1)}) all-reduce(f32[2,512]{1,0:T(2,128)S(1)} %pad_maximum_fusion.15, f32[2,512]{1,0:T(2,128)S(1)} %pad_maximum_fusion.16), channel_id=1, replica_groups=mesh['dp'=4,'rows'=64] {'dp','rows'}, use_global_device_ids=true, to_apply=%region_34.35 | all-reduce | flops 2048 | bytes 16384 | tf_op jit(solution)/shard_map/psum | solution.py:321
  559.5 187.5 %all-reduce.4.cloned.1.call-done = (f32[2,512,768]{1,2,0:T(8,128)}, f32[2,256,512]{2,1,0:T(8,128)}) async-done(((f32[2,512,768]{1,2,0:T(8,128)}, f32[2,256,512]{2,1,0:T(8,128)}), (f32[2,512,768]{1,2,0:T(8,128)}, f32[2,256,512]{2,1,0:T(8,128)})) %all-reduce.4.cloned.1.call-update) | async-done | bytes 4194320 | tf_op jit(solution)/shard_map/psum | solution.py:321
  (462 shorter events, 161.0 us)
Async XLA Ops:
  7.2 739.8 %all-reduce.4.cloned.1.call-start = ((), (), s32[]{:S(2)}) async-start(), calls=%async_computation | async-start | bytes 8388608 | tf_op jit(solution)/shard_map/psum | solution.py:321
  9.6 6.3 copy-start.20
  9.7 10.1 %copy-start.8 = (f32[144,256]{0,1:T(8,128)}, f32[144,256]{0,1:T(8,128)S(1)}, u32[]{:S(2)}) copy-start(f32[144,256]{0,1:T(8,128)S(1)} %copy.79) | copy-start | bytes 442372
  10.0 22.8 %copy-start.22 = (f32[144,256]{1,0:T(8,128)}, f32[144,256]{1,0:T(8,128)S(1)}, u32[]{:S(2)}) copy-start(f32[144,256]{1,0:T(8,128)S(1)} %copy.80) | copy-start | bytes 442372
  10.0 105.5 %copy-start.73 = (f32[8]{0:T(128)}, f32[8]{0:T(128)S(1)}, u32[]{:S(2)}) copy-start(f32[8]{0:T(128)S(1)} %get-tuple-element.386) | copy-start | bytes 100
  10.7 22.1 %copy-start.64 = (f32[256]{0:T(256)}, f32[256]{0:T(256)S(1)}, u32[]{:S(2)}) copy-start(f32[256]{0:T(256)S(1)} %mul.357) | copy-start | bytes 3076
  10.7 5.1 collective-permute-start.1
  15.9 23.8 %copy-start.76 = (f32[2,512]{1,0:T(2,128)S(1)}, f32[2,512]{1,0:T(2,128)}, u32[]{:S(2)}) copy-start(f32[2,512]{1,0:T(2,128)} %param.21) | copy-start | bytes 12292
  15.9 16.7 %collective-permute-start.2 = (bf16[2,3,48,512]{3,2,1,0:T(8,128)(2,1)S(1)}, bf16[2,3,48,512]{3,2,1,0:T(8,128)(2,1)S(1)}, u32[]{:S(2)}, u32[]{:S(2)}) collective-permute-start(bf16[2,3,48,512]{3,2,1,0:T(8,128)(2,1)S(1)} %maximum_select_fusion.4), channel_id=1, source_target_pairs={{0,2},{2,0},{1,3},{3,1},{4,6},{6,4},{5,7},{7,5},{8,10},{10,8},{9,1... | collective-permute-start | bytes 884744 | tf_op jit(solution)/shard_map/ppermute | solution.py:25
  32.7 32.1 %collective-permute-start.3 = (bf16[4,3,48,512]{3,2,1,0:T(8,128)(2,1)S(1)}, bf16[4,3,48,512]{3,2,1,0:T(8,128)(2,1)}, u32[]{:S(2)}, u32[]{:S(2)}) collective-permute-start(bf16[4,3,48,512]{3,2,1,0:T(8,128)(2,1)S(1)} %maximum_select_fusion.2), channel_id=1, source_target_pairs={{0,4},{4,0},{1,5},{5,1},{2,6},{6,2},{3,7},{7,3},{8,12},{12,8},{9,1... | collective-permute-start | bytes 1769480 | tf_op jit(solution)/shard_map/ppermute | solution.py:25
  40.3 69.0 %copy-start.56 = (f32[1,512]{1,0:T(1,128)}, f32[1,512]{1,0:T(1,128)S(1)}, u32[]{:S(2)}) copy-start(f32[1,512]{1,0:T(1,128)S(1)} %get-tuple-element.384) | copy-start | bytes 6148
  106.7 12.3 %copy-start = (bf16[8,2,72,576]{3,2,1,0:T(8,128)(2,1)}, bf16[8,2,72,576]{3,2,1,0:T(8,128)(2,1)S(1)}, u32[]{:S(2)}) copy-start(bf16[8,2,72,576]{3,2,1,0:T(8,128)(2,1)S(1)} %get-tuple-element.687) | copy-start | bytes 3981316
  106.7 12.3 %copy-start.7 = (bf16[8,2,576,32]{2,3,1,0:T(8,128)(2,1)}, bf16[8,2,576,32]{2,3,1,0:T(8,128)(2,1)S(1)}, u32[]{:S(2)}) copy-start(bf16[8,2,576,32]{2,3,1,0:T(8,128)(2,1)S(1)} %get-tuple-element.720) | copy-start | bytes 1769476
  107.7 12.8 %copy-start.37 = (bf16[3,2,24,256]{3,2,1,0:T(8,128)(2,1)}, bf16[3,2,24,256]{3,2,1,0:T(8,128)(2,1)S(1)}, u32[]{:S(2)}) copy-start(bf16[3,2,24,256]{3,2,1,0:T(8,128)(2,1)S(1)} %copy.86) | copy-start | bytes 221188
  109.0 11.5 %copy-start.60 = (f32[144]{0:T(256)}, f32[144]{0:T(256)S(1)}, u32[]{:S(2)}) copy-start(f32[144]{0:T(256)S(1)} %broadcast_multiply_fusion.5) | copy-start | bytes 1732
  109.3 11.3 %copy-start.62 = (f32[144]{0:T(256)}, f32[144]{0:T(256)S(1)}, u32[]{:S(2)}) copy-start(f32[144]{0:T(256)S(1)} %add_rsqrt_fusion.5) | copy-start | bytes 1732
  109.5 9.5 %collective-permute-start.4 = (bf16[3,48,512]{2,1,0:T(8,128)(2,1)S(1)}, bf16[3,48,512]{2,1,0:T(8,128)(2,1)S(1)}, u32[]{:S(2)}, u32[]{:S(2)}) collective-permute-start(bf16[3,48,512]{2,1,0:T(8,128)(2,1)S(1)} %bitcast.506), channel_id=1, source_target_pairs={{0,60},{1,61},{2,62},{3,63},{4,0},{5,1},{6,2},{7,3},{8,4},{9,5},{1... | collective-permute-start | bytes 442376 | tf_op jit(solution)/shard_map/ppermute | solution.py:30
  115.6 6.4 copy-start.66
  121.6 8.9 %copy-start.23 = (f32[144,256]{1,0:T(8,128)}, f32[144,256]{1,0:T(8,128)S(1)}, u32[]{:S(2)}) copy-start(f32[144,256]{1,0:T(8,128)S(1)} %copy.108) | copy-start | bytes 442372
  121.6 8.4 %copy-start.80 = (s32[192]{0:T(256)S(1)}, s32[192]{0:T(256)}, u32[]{:S(2)}) copy-start(s32[192]{0:T(256)} %param.24) | copy-start | bytes 2308
  121.6 8.7 %copy-start.81 = (s32[48]{0:T(128)S(1)}, s32[48]{0:T(128)}, u32[]{:S(2)}) copy-start(s32[48]{0:T(128)} %param.25) | copy-start | bytes 580
  121.8 8.8 %copy-start.10 = (f32[144,256]{0,1:T(8,128)}, f32[144,256]{0,1:T(8,128)S(1)}, u32[]{:S(2)}) copy-start(f32[144,256]{0,1:T(8,128)S(1)} %copy.90) | copy-start | bytes 442372
  122.0 31.6 %copy-start.25 = (f32[144,256]{1,0:T(8,128)}, f32[144,256]{1,0:T(8,128)S(1)}, u32[]{:S(2)}) copy-start(f32[144,256]{1,0:T(8,128)S(1)} %copy.91) | copy-start | bytes 442372
  122.1 32.4 %copy-start.58 = (f32[1,512]{1,0:T(1,128)S(1)}, f32[1,512]{1,0:T(1,128)}, u32[]{:S(2)}) copy-start(f32[1,512]{1,0:T(1,128)} %get-tuple-element.383) | copy-start | bytes 6148
  122.1 8.4 %collective-permute-start.5 = (bf16[1,3,48,512]{3,2,1,0:T(8,128)(2,1)S(1)}, bf16[1,3,48,512]{3,2,1,0:T(8,128)(2,1)S(1)}, u32[]{:S(2)}, u32[]{:S(2)}) collective-permute-start(bf16[1,3,48,512]{3,2,1,0:T(8,128)(2,1)S(1)} %bitcast.495), channel_id=1, source_target_pairs={{0,1},{1,0},{2,3},{3,2},{4,5},{5,4},{6,7},{7,6},{8,9},{9,8},{10,11... | collective-permute-start | bytes 442376 | tf_op jit(solution)/shard_map/ppermute | solution.py:25
  122.6 31.8 %collective-permute-start = (bf16[3,48,512]{2,1,0:T(8,128)(2,1)S(1)}, bf16[3,48,512]{2,1,0:T(8,128)(2,1)S(1)}, u32[]{:S(2)}, u32[]{:S(2)}) collective-permute-start(bf16[3,48,512]{2,1,0:T(8,128)(2,1)S(1)} %bitcast.519), channel_id=1, source_target_pairs={{0,60},{1,61},{2,62},{3,63},{4,0},{5,1},{6,2},{7,3},{8,4},{9,5},{1... | collective-permute-start | bytes 442376 | tf_op jit(solution)/shard_map/ppermute | solution.py:30
  130.5 22.9 %collective-permute-start.6 = (bf16[2,3,48,512]{3,2,1,0:T(8,128)(2,1)S(1)}, bf16[2,3,48,512]{3,2,1,0:T(8,128)(2,1)S(1)}, u32[]{:S(2)}, u32[]{:S(2)}) collective-permute-start(bf16[2,3,48,512]{3,2,1,0:T(8,128)(2,1)S(1)} %maximum_select_fusion.5), channel_id=1, source_target_pairs={{0,2},{2,0},{1,3},{3,1},{4,6},{6,4},{5,7},{7,5},{8,10},{10,8},{9,1... | collective-permute-start | bytes 884744 | tf_op jit(solution)/shard_map/ppermute | solution.py:25
  153.6 28.6 %collective-permute-start.7 = (bf16[4,3,48,512]{3,2,1,0:T(8,128)(2,1)S(1)}, bf16[4,3,48,512]{3,2,1,0:T(8,128)(2,1)}, u32[]{:S(2)}, u32[]{:S(2)}) collective-permute-start(bf16[4,3,48,512]{3,2,1,0:T(8,128)(2,1)S(1)} %maximum_select_fusion.3), channel_id=1, source_target_pairs={{0,4},{4,0},{1,5},{5,1},{2,6},{6,2},{3,7},{7,3},{8,12},{12,8},{9,1... | collective-permute-start | bytes 1769480 | tf_op jit(solution)/shard_map/ppermute | solution.py:25
  208.8 24.3 %copy-start.15 = (bf16[2,256,512]{2,1,0:T(8,128)(2,1)S(1)}, bf16[2,256,512]{2,1,0:T(8,128)(2,1)}, u32[]{:S(2)}) copy-start(bf16[2,256,512]{2,1,0:T(8,128)(2,1)} %param.20) | copy-start | bytes 1572868
  292.0 26.1 %collective-permute-start.8 = (bf16[4,3,48,512]{3,2,1,0:T(8,128)(2,1)S(1)}, bf16[4,3,48,512]{3,2,1,0:T(8,128)(2,1)S(1)}, u32[]{:S(2)}, u32[]{:S(2)}) collective-permute-start(bf16[4,3,48,512]{3,2,1,0:T(8,128)(2,1)S(1)} %bitcast.494), channel_id=1, source_target_pairs={{0,4},{4,0},{1,5},{5,1},{2,6},{6,2},{3,7},{7,3},{8,12},{12,8},{9,1... | collective-permute-start | bytes 1769480 | tf_op jit(solution)/shard_map/ppermute | solution.py:25
  319.2 15.5 %collective-permute-start.9 = (bf16[2,3,48,512]{3,2,1,0:T(8,128)(2,1)}, bf16[2,3,48,512]{3,2,1,0:T(8,128)(2,1)S(1)}, u32[]{:S(2)}, u32[]{:S(2)}) collective-permute-start(bf16[2,3,48,512]{3,2,1,0:T(8,128)(2,1)} %select_convert_fusion.3), channel_id=1, source_target_pairs={{0,2},{2,0},{1,3},{3,1},{4,6},{6,4},{5,7},{7,5},{8,10},{10,8},{9,1... | collective-permute-start | bytes 884744 | tf_op jit(solution)/shard_map/ppermute | solution.py:25
  322.1 13.1 %copy-start.14 = (f32[144,256]{0,1:T(8,128)S(1)}, f32[144,256]{0,1:T(8,128)}, u32[]{:S(2)}) copy-start(f32[144,256]{0,1:T(8,128)} %copy-done.13) | copy-start | bytes 442372
  322.2 13.1 %copy-start.55 = (f32[144,8]{0,1:T(8,128)S(1)}, f32[144,8]{0,1:T(8,128)}, u32[]{:S(2)}) copy-start(f32[144,8]{0,1:T(8,128)} %copy-done.54) | copy-start | bytes 13828
  322.2 13.0 %copy-start.74 = (f32[8]{0:T(128)S(1)}, f32[8]{0:T(128)}, u32[]{:S(2)}) copy-start(f32[8]{0:T(128)} %copy-done.73) | copy-start | bytes 100
  334.9 4.3 collective-permute-start.10
  336.0 4.8 copy-start.11
  336.8 6.9 copy-start.4
  336.8 6.9 copy-start.24
  336.8 6.9 copy-start.67
  340.7 4.1 copy-start.18
  344.9 12.6 %copy-start.57 = (f32[1,512]{1,0:T(1,128)S(1)}, f32[1,512]{1,0:T(1,128)}, u32[]{:S(2)}) copy-start(f32[1,512]{1,0:T(1,128)} %copy-done.56) | copy-start | bytes 6148
  344.9 12.6 %copy-start.61 = (f32[144]{0:T(256)S(1)}, f32[144]{0:T(256)}, u32[]{:S(2)}) copy-start(f32[144]{0:T(256)} %copy-done.60) | copy-start | bytes 1732
  344.9 12.6 %copy-start.63 = (f32[144]{0:T(256)S(1)}, f32[144]{0:T(256)}, u32[]{:S(2)}) copy-start(f32[144]{0:T(256)} %copy-done.62) | copy-start | bytes 1732
  346.2 11.9 %copy-start.16 = (bf16[2,256,512]{2,1,0:T(8,128)(2,1)S(1)}, bf16[2,256,512]{2,1,0:T(8,128)(2,1)}, u32[]{:S(2)}) copy-start(bf16[2,256,512]{2,1,0:T(8,128)(2,1)} %param.20) | copy-start | bytes 1572868
  346.3 11.1 %collective-permute-start.11 = (bf16[3,48,512]{2,1,0:T(8,128)(2,1)S(1)}, bf16[3,48,512]{2,1,0:T(8,128)(2,1)S(1)}, u32[]{:S(2)}, u32[]{:S(2)}) collective-permute-start(bf16[3,48,512]{2,1,0:T(8,128)(2,1)S(1)} %pad_maximum_fusion.10), channel_id=1, source_target_pairs={{0,4},{1,5},{2,6},{3,7},{4,8},{5,9},{6,10},{7,11},{8,12},{9,13},{1... | collective-permute-start | bytes 442376 | tf_op jit(solution)/shard_map/ppermute | solution.py:30
  403.3 3.4 copy-start.34
  418.8 15.3 %collective-permute-start.12 = (bf16[4,3,48,512]{3,2,1,0:T(8,128)(2,1)S(1)}, bf16[4,3,48,512]{3,2,1,0:T(8,128)(2,1)S(1)}, u32[]{:S(2)}, u32[]{:S(2)}) collective-permute-start(bf16[4,3,48,512]{3,2,1,0:T(8,128)(2,1)S(1)} %bitcast.493), channel_id=1, source_target_pairs={{0,4},{4,0},{1,5},{5,1},{2,6},{6,2},{3,7},{7,3},{8,12},{12,8},{9,1... | collective-permute-start | bytes 1769480 | tf_op jit(solution)/shard_map/ppermute | solution.py:25
  434.1 19.7 %copy-start.31 = (bf16[3,48,512]{2,1,0:T(8,128)(2,1)S(1)}, bf16[3,48,512]{2,1,0:T(8,128)(2,1)}, u32[]{:S(2)}) copy-start(bf16[3,48,512]{2,1,0:T(8,128)(2,1)} %copy-done.30) | copy-start | bytes 442372
  434.2 19.7 %copy-start.44 = (bf16[144,256]{1,0:T(8,128)(2,1)S(1)}, bf16[144,256]{1,0:T(8,128)(2,1)}, u32[]{:S(2)}) copy-start(bf16[144,256]{1,0:T(8,128)(2,1)} %copy-done.43) | copy-start | bytes 221188
  434.2 19.7 %copy-start.46 = (bf16[144,256]{1,0:T(8,128)(2,1)S(1)}, bf16[144,256]{1,0:T(8,128)(2,1)}, u32[]{:S(2)}) copy-start(bf16[144,256]{1,0:T(8,128)(2,1)} %copy-done.45) | copy-start | bytes 221188
  434.2 19.7 %copy-start.51 = (bf16[144,256]{1,0:T(8,128)(2,1)S(1)}, bf16[144,256]{1,0:T(8,128)(2,1)}, u32[]{:S(2)}) copy-start(bf16[144,256]{1,0:T(8,128)(2,1)} %slice.319) | copy-start | bytes 221188
  435.2 32.2 %collective-permute-start.13 = (bf16[2,3,48,512]{3,2,1,0:T(8,128)(2,1)}, bf16[2,3,48,512]{3,2,1,0:T(8,128)(2,1)}, u32[]{:S(2)}, u32[]{:S(2)}) collective-permute-start(bf16[2,3,48,512]{3,2,1,0:T(8,128)(2,1)} %select_convert_fusion.2), channel_id=1, source_target_pairs={{0,2},{2,0},{1,3},{3,1},{4,6},{6,4},{5,7},{7,5},{8,10},{10,8},{9,1... | collective-permute-start | bytes 884744 | tf_op jit(solution)/shard_map/ppermute | solution.py:25
  456.3 4.8 copy-start.72
  462.9 7.8 %copy-start.29 = (bf16[144,512]{1,0:T(8,128)(2,1)S(1)}, bf16[144,512]{1,0:T(8,128)(2,1)}, u32[]{:S(2)}) copy-start(bf16[144,512]{1,0:T(8,128)(2,1)} %copy-done.28) | copy-start | bytes 442372
  463.0 7.8 %copy-start.38 = (bf16[3,2,24,256]{3,2,1,0:T(8,128)(2,1)S(1)}, bf16[3,2,24,256]{3,2,1,0:T(8,128)(2,1)}, u32[]{:S(2)}) copy-start(bf16[3,2,24,256]{3,2,1,0:T(8,128)(2,1)} %copy-done.37) | copy-start | bytes 221188
  469.4 4.9 copy-start.17
  470.0 6.3 collective-permute-start.14
  472.5 3.9 copy-start.6
  476.3 3.1 copy-start.65
  477.4 3.2 copy-start.52
  483.0 75.4 %copy-start.19 = (bf16[2,512,768]{2,1,0:T(8,128)(2,1)S(1)}, bf16[2,512,768]{2,1,0:T(8,128)(2,1)}, u32[]{:S(2)}) copy-start(bf16[2,512,768]{2,1,0:T(8,128)(2,1)} %param.19) | copy-start | bytes 4718596
  483.1 75.3 %copy-start.48 = (bf16[144,256]{1,0:T(8,128)(2,1)S(1)}, bf16[144,256]{1,0:T(8,128)(2,1)}, u32[]{:S(2)}) copy-start(bf16[144,256]{1,0:T(8,128)(2,1)} %copy-done.47) | copy-start | bytes 221188
  483.1 75.3 %copy-start.50 = (bf16[144,256]{1,0:T(8,128)(2,1)S(1)}, bf16[144,256]{1,0:T(8,128)(2,1)}, u32[]{:S(2)}) copy-start(bf16[144,256]{1,0:T(8,128)(2,1)} %copy-done.49) | copy-start | bytes 221188
  483.1 75.3 %copy-start.53 = (bf16[144,256]{1,0:T(8,128)(2,1)S(1)}, bf16[144,256]{1,0:T(8,128)(2,1)}, u32[]{:S(2)}) copy-start(bf16[144,256]{1,0:T(8,128)(2,1)} %copy-done.52) | copy-start | bytes 221188
  (35 other events, 56.4 us)
Sparse Core Ops, SparseCore 0:
  483.2 263.6 all-reduce.3
where the time goes:
time: 764 us; the launch traced here: 758 us
  waiting for transfers between devices  331 us (43%)
  matrix products  120 us (16%)
  local copies, waits for them, and re-layouts  111 us (15%)
  blocking collectives  74 us (10%)
  starting transfers between devices  62.9 us (8%)
  other arithmetic  42.4 us (6%)
  between operations  15.8 us (2%)
    psum x1, waiting for transfers between devices, body(): lax.psum((weight_grads[0], weight_grads[1], weight_grads[2], weight_grads...  187 us
    ppermute x12, waiting for transfers between devices, swapped(): return lax.ppermute(block, axis, route)  135 us
    psum x1, blocking collectives, body(): lax.psum((weight_grads[0], weight_grads[1], weight_grads[2], weight_grads...  74 us
    ppermute x12, starting transfers between devices, swapped(): return lax.ppermute(block, axis, route)  43.7 us
    dot_general x16, matrix products, one_head(): jnp.einsum('wqk,wkd->wqd', softmaxed, v_head, preferred_element_type=jnp....  22.9 us
    transpose x2, local copies, waits for them, and re-layouts, key_windows(): return gathered.reshape(WIN, windows_across, WIN, 2, HEADS, HD).transpose...  22.6 us
    dot_general x16, matrix products, one_head(): jnp.einsum('wqd,wkd->wqk', grad_head, v_head, preferred_element_type=jnp....  20.5 us
    dot_general x16, matrix products, one_head(): jnp.einsum('wqk,wqd->wkd', grad_scores, q_head, preferred_element_type=jn...  19.4 us
  transfers between devices with their start and end apart: 16, of which 13 were waited for; matrix products, arithmetic and copies ran while one was open for 4% of the time, Pallas kernels for 0%

commit v1 on v0

v1 whole, which is shorter than its diff:
```python
import functools

import jax
import jax.numpy as jnp
from jax import lax
from jax.experimental import pallas as pl
from jax.experimental.pallas import tpu as pltpu
from jax.sharding import PartitionSpec as P

C = 512
HEADS = 8
HD = 32
WIN = 24
HH = 256
SHIFT = 12
GROUP = 8
TOK = 144
CELLS = WIN * WIN
ROWS_DEV = 3
PACK = 48
DEVS = 64

norm_eps = 1e-05
mask_value = 100.0
f32 = jnp.float32
bf16 = jnp.bfloat16


def dot(a, b):
    return jnp.dot(a, b, preferred_element_type=f32)


def dot_t(a, b):
    return lax.dot_general(a, b, (((1,), (1,)), ((), ())), preferred_element_type=f32)


def dot_0(a, b):
    return lax.dot_general(a, b, (((0,), (0,)), ((), ())), preferred_element_type=f32)


def iota(shape, axis):
    return lax.broadcasted_iota(jnp.int32, shape, axis)


def head_sums(x):
    width = x.shape[1]
    ones = (iota((width, width), 0) // HD == iota((width, width), 1) // HD).astype(f32).astype(bf16)
    high = x.astype(bf16)
    low = (x - high.astype(f32)).astype(bf16)
    return dot(high, ones) + dot(low, ones)


def split_two(x):
    high = x.astype(bf16).astype(f32)
    return high, x - high


def lane_slice(x, at):
    return x[:, at : at + HD]


def send_projected(tokens, weight, scale_ref, block, out_ref):
    projected = dot(tokens, weight)
    query, key, value = projected[:, :HH], projected[:, HH : 2 * HH], projected[:, 2 * HH :]
    lane = iota((1, HH), 1)
    scale = jnp.zeros((1, HH), f32)
    for h in range(HEADS):
        scale = jnp.where(lane // HD == h, scale_ref[block, h], scale)
    q_factor = lax.rsqrt(1.0 + head_sums(query * query))
    k_factor = lax.rsqrt(1.0 + head_sums(key * key))
    q_hat = query * q_factor * jnp.exp(scale)
    k_hat = key * k_factor
    q_high, q_low = split_two(q_factor)
    k_high, k_low = split_two(k_factor)
    slot = iota(q_hat.shape, 1) % HD
    extra = jnp.where(
        slot == 0,
        q_high,
        jnp.where(slot == 1, q_low, jnp.where(slot == 2, k_high, jnp.where(slot == 3, k_low, 0.0))),
    )
    for h in range(HEADS):
        at = h * HD
        out_ref[h] = jnp.concatenate(
            [lane_slice(q_hat, at), lane_slice(k_hat, at), lane_slice(value, at), lane_slice(extra, at)], 1
        ).astype(bf16)


def unpack_heads(packed_ref):
    packed = [packed_ref[h].astype(f32) for h in range(HEADS)]
    rows = [
        jnp.concatenate([lane_slice(packed[h], r * HD) for h in range(HEADS)], 1)
        for r in range(ROWS_DEV)
    ]
    return jnp.concatenate(rows, 0).astype(bf16)


def pack_heads(array, out_ref):
    zeros = jnp.zeros((PACK, HD), f32)
    for h in range(HEADS):
        out_ref[h] = jnp.concatenate(
            [lane_slice(array[r * PACK : (r + 1) * PACK], h * HD) for r in range(ROWS_DEV)] + [zeros], 1
        ).astype(bf16)


def to_windows(array):
    split = array.reshape(GROUP, ROWS_DEV, 2, WIN, array.shape[-1])
    return [split[:, :, w].reshape(CELLS, array.shape[-1]) for w in range(2)]


def from_windows(pair):
    depth = pair[0].shape[-1]
    parts = [part.reshape(GROUP, ROWS_DEV, 1, WIN, depth) for part in pair]
    return jnp.concatenate(parts, 2).reshape(GROUP, TOK, depth)


def roll_tokens(array, by):
    by = by % TOK
    return jnp.concatenate([array[TOK - by :], array[: TOK - by]], 0)


def normalized(attended, weight):
    outputs = dot(attended, weight)
    centered = outputs - jnp.mean(outputs, -1, keepdims=True)
    inverse = lax.rsqrt(jnp.mean(centered * centered, -1, keepdims=True) + norm_eps)
    return centered * inverse, inverse


def finish_back(attended, weight, gain_row, grad_out):
    y_hat, inverse = normalized(attended, weight)
    grad_gain = jnp.sum(grad_out * y_hat, 0, keepdims=True)
    grad_bias = jnp.sum(grad_out, 0, keepdims=True)
    scaled = grad_out * gain_row
    grad_y = inverse * (
        scaled
        - jnp.mean(scaled, -1, keepdims=True)
        - y_hat * jnp.mean(scaled * y_hat, -1, keepdims=True)
    )
    grad_y = grad_y.astype(bf16)
    gains = jnp.concatenate([grad_gain, grad_bias, jnp.zeros((6, C), f32)], 0)
    return grad_y, dot_t(grad_y, weight), gains


def labels_of(axis, window, first_row, row_ref, col_ref):
    shape = (CELLS, 1) if axis == 0 else (1, CELLS)
    at = iota(shape, axis)
    source = at // (ROWS_DEV * WIN)
    rest = at - source * (ROWS_DEV * WIN)
    local_row = rest // WIN
    column = rest - local_row * WIN + window * WIN
    local_row = local_row + (column >= 36).astype(jnp.int32)
    local_row = jnp.where(local_row >= ROWS_DEV, local_row - ROWS_DEV, local_row)
    row = first_row + source * ROWS_DEV + local_row
    row_label = jnp.zeros(shape, jnp.int32)
    col_label = jnp.zeros(shape, jnp.int32)
    for label in (1, 2):
        row_cut = jnp.sum((row_ref[...] < label).astype(jnp.int32), 1, keepdims=True)
        col_cut = jnp.sum((col_ref[...] < label).astype(jnp.int32), 1, keepdims=True)
        row_label = row_label + (row >= row_cut).astype(jnp.int32)
        col_label = col_label + (column >= col_cut).astype(jnp.int32)
    return 3 * row_label + col_label


def masked(scores, window, mask_refs):
    if mask_refs is None:
        return scores
    first_row = mask_refs[0][0]
    one = labels_of(0, window, first_row, *mask_refs[1:])
    two = labels_of(1, window, first_row, *mask_refs[1:])
    return scores - jnp.where(one == two, 0.0, mask_value)


def attend_kernel(masks, x_ref, *refs):
    mask_refs = refs[:3] if masks else None
    out_ref, saved_ref = refs[-2:]
    lane = iota((CELLS, 128), 1)
    per_window = []
    for w, cells in enumerate(to_windows(x_ref[...].astype(f32))):
        query = cells[:, :HD].astype(bf16)
        key = cells[:, HD : 2 * HD].astype(bf16)
        value = jnp.where(lane < HD, pltpu.roll(cells, 64, 1), jnp.where(lane == HD, 1.0, 0.0)).astype(bf16)
        scores = masked(dot_t(query, key), w, mask_refs)
        weights = jnp.exp(scores).astype(bf16)
        summed = dot(weights, value)
        inverse = 1.0 / summed[:, HD : HD + 1]
        attended = jnp.where(lane < HD, summed * inverse, 0.0)
        saved_ref[w] = jnp.where(lane == HD, inverse, attended)
        per_window.append(attended.reshape(GROUP, ROWS_DEV, WIN, 128))
    total = 0.0
    for r in range(ROWS_DEV):
        rows = jnp.concatenate([part[:, r] for part in per_window], 1).reshape(GROUP * PACK, 128)
        total = total + (rows if r == 0 else pltpu.roll(rows, r * HD, 1))
    out_ref[...] = total.astype(bf16).reshape(GROUP, PACK, 128)


def attend_back_kernel(block, masks, head_ref, scale_ref, x_ref, saved_ref, grad_ref, *refs):
    mask_refs = refs[:3] if masks else None
    out_ref = refs[-1]
    lane = iota((CELLS, 128), 1)
    scale_row = jnp.exp(jnp.full((1, 128), scale_ref[block, head_ref[0]], f32))
    packed = grad_ref[...].astype(f32).reshape(GROUP * PACK, 128)
    rolled = [packed if r == 0 else pltpu.roll(packed, 128 - r * HD, 1) for r in range(ROWS_DEV)]
    rolled = [part.reshape(GROUP, 1, 2, WIN, 128) for part in rolled]
    grads = jnp.concatenate(rolled, 1)
    results = []
    for w, cells in enumerate(to_windows(x_ref[...].astype(f32))):
        saved = saved_ref[w]
        grad = grads[:, :, w].reshape(CELLS, 128)
        inverse = saved[:, HD : HD + 1]
        grad = jnp.where(lane < HD, grad * inverse, 0.0).astype(bf16).astype(f32)
        row = jnp.sum(grad * saved, 1, keepdims=True)
        row_high, row_low = split_two(row)
        grad_ext = jnp.where(lane == HD, -row_high, jnp.where(lane == HD + 1, -row_low, grad)).astype(bf16)
        ones = jnp.where((lane == HD) | (lane == HD + 1), 1.0, 0.0)
        value_ext = jnp.where(lane < HD, pltpu.roll(cells, 64, 1), ones).astype(bf16)
        query = cells[:, :HD].astype(bf16)
        key = cells[:, HD : 2 * HD].astype(bf16)
        scores = masked(dot_t(key, query), w, mask_refs)
        weights = jnp.exp(scores).astype(bf16)
        grad_scores = (weights.astype(f32) * dot_t(value_ext, grad_ext)).astype(bf16)
        query_at = jnp.where((lane >= HD) & (lane < 2 * HD), pltpu.roll(cells, HD, 1), 0.0).astype(bf16)
        grad_at = pltpu.roll(grad, 2 * HD, 1).astype(bf16)
        grad_kv = dot(grad_scores, query_at) + dot(weights, grad_at)
        key_at = jnp.where(lane < HD, pltpu.roll(cells, 128 - HD, 1), 0.0).astype(bf16)
        grad_q = dot_0(grad_scores, key_at)
        total = jnp.where(lane < HD, grad_q * scale_row, grad_kv)
        unit = jnp.where(lane < HD, cells / scale_row, jnp.where(lane < 2 * HD, cells, 0.0))
        q_factor = cells[:, 96:97] + cells[:, 97:98]
        k_factor = cells[:, 98:99] + cells[:, 99:100]
        factor = jnp.where(lane < HD, q_factor, jnp.where(lane < 2 * HD, k_factor, 1.0))
        result = factor * (total - unit * head_sums(unit * total))
        results.append(jnp.where(lane >= 96, pltpu.roll(saved, 96, 1), result))
    out_ref[...] = from_windows(results).astype(bf16)


def first_kernel(scale_ref, tokens_ref, w_ref, out_ref):
    send_projected(tokens_ref[...], w_ref[...], scale_ref, 0, out_ref)


def middle_kernel(scale_ref, packed_ref, tokens_ref, w_proj_ref, gain_ref, bias_ref, w_ref, rolled_ref, out_ref):
    attended = unpack_heads(packed_ref)
    y_hat, _ = normalized(attended, w_proj_ref[...])
    out = (tokens_ref[...].astype(f32) + y_hat * gain_ref[0:1] + bias_ref[0:1]).astype(bf16).astype(f32)
    rolled = roll_tokens(out, -SHIFT).astype(bf16)
    rolled_ref[...] = rolled
    send_projected(rolled, w_ref[...], scale_ref, 1, out_ref)


def turn_kernel(packed_ref, grad_ref, w_proj_ref, gain_ref, out_ref, grad_y_ref, gains_ref):
    attended = unpack_heads(packed_ref)
    grad = roll_tokens(grad_ref[...].astype(f32), -SHIFT)
    grad_y, grad_att, gains = finish_back(attended, w_proj_ref[...], gain_ref[1:2], grad)
    pack_heads(grad_att, out_ref)
    grad_y_ref[...] = grad_y
    gains_ref[...] = gains


def gather_qkv(qkv_ref):
    parts = [qkv_ref[h].astype(f32) for h in range(HEADS)]
    return jnp.concatenate(
        [lane_slice(parts[h], kind * HD) for kind in range(3) for h in range(HEADS)], 1
    ).astype(bf16)


def back_kernel(
    qkv_ref, w_ref, grad_ref, packed_ref, w_proj_ref, gain_ref, out_ref, grad0_ref, grad_proj_ref, gains_ref
):
    from_qkv = roll_tokens(dot_t(gather_qkv(qkv_ref), w_ref[...]), SHIFT)
    grad = (grad_ref[...].astype(f32) + from_qkv).astype(bf16)
    grad0_ref[...] = grad
    attended = unpack_heads(packed_ref)
    grad_y, grad_att, gains = finish_back(attended, w_proj_ref[...], gain_ref[0:1], grad.astype(f32))
    pack_heads(grad_att, out_ref)
    grad_proj_ref[...] = dot_0(grad_y, attended)
    gains_ref[...] = gains


def last_kernel(qkv_ref, w_ref, grad_ref, out_ref):
    from_qkv = dot_t(gather_qkv(qkv_ref), w_ref[...])
    out_ref[...] = (grad_ref[...].astype(f32) + from_qkv).astype(bf16)


def weights_kernel(
    qkv0_ref, qkv1_ref, tokens0_ref, tokens1_ref, grad_y1_ref, grad_proj0_ref, gains0_ref, gains1_ref, out_ref
):
    qkv0 = qkv0_ref[...].reshape(GROUP * TOK, 128)
    qkv1 = qkv1_ref[...].reshape(GROUP * TOK, 128)
    grad0 = dot_0(qkv0, tokens0_ref[...])
    grad1 = dot_0(qkv1, tokens1_ref[...])
    proj1 = dot_0(qkv1, grad_y1_ref[...])
    pieces = []
    for ref in (gains0_ref, gains1_ref):
        for row in (0, 1):
            pieces += split_two(ref[row : row + 1])
    grad0 = jnp.concatenate([grad0[:96]] + [jnp.concatenate(pieces, 0), jnp.zeros((24, C), f32)], 0)
    grad1 = jnp.concatenate([grad1[:96], proj1[96:]], 0)
    upper = jnp.concatenate([grad1.T, grad0.T], 1).reshape(DEVS, 8, 256)
    lower = grad_proj0_ref[...].reshape(DEVS, 8, 256)
    out_ref[...] = jnp.concatenate([upper, lower], 1).astype(bf16)


def reduce_kernel(parts_ref, out_ref):
    summed = jnp.sum(parts_ref[...].astype(f32).reshape(8, 8, 16, 256), 0)
    late = [summed[(h + GROUP // 2) % GROUP, :8, :128] for h in range(HEADS)]
    early = [summed[h, :8, 128:] for h in range(HEADS)]
    proj0 = jnp.sum(summed[:, 8:], 0)
    gains = jnp.sum(summed[:, :8, 128:], 0)
    pieces = [lane_slice(part, kind * HD) for kind in range(3) for part in early]
    pieces += [lane_slice(part, kind * HD) for kind in range(3) for part in late]
    pieces += [proj0]
    pieces += [lane_slice(part, 96) for part in late]
    pieces += [gains]
    out_ref[...] = jnp.concatenate(pieces, 1)


def final_kernel(a_ref, b_ref, c_ref, d_ref, qkv_ref, proj_ref, gains_ref):
    total = (a_ref[...] + b_ref[...]) + (c_ref[...] + d_ref[...])
    qkv_ref[0] = total[:, :768]
    qkv_ref[1] = total[:, 768:1536]
    proj_ref[0] = total[:, 1536:1792].T
    proj_ref[1] = total[:, 1792:2048].T
    gains_ref[...] = total[:, 2048:2176].T


def call(kernel, outs, smem, *args):
    specs = [pl.BlockSpec(memory_space=pltpu.SMEM)] * smem
    specs += [pl.BlockSpec(memory_space=pltpu.VMEM)] * (len(args) - smem)
    return pl.pallas_call(
        kernel,
        out_shape=[jax.ShapeDtypeStruct(shape, dtype) for shape, dtype in outs],
        in_specs=specs,
        out_specs=[pl.BlockSpec(memory_space=pltpu.VMEM)] * len(outs),
        compiler_params=pltpu.CompilerParams(vmem_limit_bytes=40 * 2**20),
    )(*args)


def body(image, out_grad, w_qkv, w_proj, norm_gain, norm_bias, logit_scale, row_band, col_band):
    position = lax.axis_index("rows")
    aligned = [[GROUP * g + i for i in range(GROUP)] for g in range(DEVS // GROUP)]
    half = GROUP // 2
    moved = [[(GROUP * g + half + i) % DEVS for i in range(GROUP)] for g in range(DEVS // GROUP)]
    moved_position = (position + DEVS - half) % DEVS
    head0 = (position % GROUP).reshape(1)
    head1 = (moved_position % GROUP).reshape(1)
    first_row = (moved_position // GROUP * WIN).reshape(1)
    masks = (first_row, row_band.reshape(1, -1), col_band.reshape(1, -1))

    def exchange(array, groups):
        return lax.all_to_all(array, "rows", 0, 0, axis_index_groups=groups, tiled=True)

    def gather(array, groups):
        return lax.all_gather(array, "rows", axis_index_groups=groups, tiled=True)

    tokens0 = image.reshape(TOK, C)
    grad_out = out_grad.reshape(TOK, C)
    wide = ((GROUP, TOK, 128), bf16)
    narrow = ((GROUP, PACK, 128), bf16)
    saved = ((2, CELLS, 128), f32)
    cells = ((TOK, C), bf16)
    gains = ((8, C), f32)

    tokens0_all = gather(tokens0, aligned)
    (x0,) = call(first_kernel, [wide], 1, logit_scale, tokens0, w_qkv[0])
    x0 = exchange(x0, aligned)
    a0, saved0 = call(functools.partial(attend_kernel, False), [narrow, saved], 0, x0)
    a0 = exchange(a0, aligned)
    tokens1, x1 = call(
        middle_kernel, [cells, wide], 1, logit_scale, a0, tokens0, w_proj[0], norm_gain, norm_bias, w_qkv[1]
    )
    tokens1_all = gather(tokens1, moved)
    x1 = exchange(x1, moved)
    mask_specs = 1

    def masked_call(kernel, outs, scalars, arrays):
        specs = [pl.BlockSpec(memory_space=pltpu.SMEM)] * len(scalars)
        specs += [pl.BlockSpec(memory_space=pltpu.VMEM)] * len(arrays)
        specs += [pl.BlockSpec(memory_space=pltpu.SMEM)] * mask_specs
        specs += [pl.BlockSpec(memory_space=pltpu.VMEM)] * 2
        return pl.pallas_call(
            kernel,
            out_shape=[jax.ShapeDtypeStruct(shape, dtype) for shape, dtype in outs],
            in_specs=specs,
            out_specs=[pl.BlockSpec(memory_space=pltpu.VMEM)] * len(outs),
            compiler_params=pltpu.CompilerParams(vmem_limit_bytes=40 * 2**20),
        )(*scalars, *arrays, *masks)

    a1, saved1 = masked_call(functools.partial(attend_kernel, True), [narrow, saved], (), (x1,))
    a1 = exchange(a1, moved)
    d1, grad_y1, gains1 = call(turn_kernel, [narrow, cells, gains], 0, a1, grad_out, w_proj[1], norm_gain)
    grad_y1_all = gather(grad_y1, moved)
    d1 = exchange(d1, moved)
    (qkv1,) = masked_call(
        functools.partial(attend_back_kernel, 1, True), [wide], (head1, logit_scale), (x1, saved1, d1)
    )
    d_qkv1 = exchange(qkv1, moved)
    d0, grad0, grad_proj0, gains0 = call(
        back_kernel,
        [narrow, cells, ((C, HH), f32), gains],
        0,
        d_qkv1,
        w_qkv[1],
        grad_out,
        a0,
        w_proj[0],
        norm_gain,
    )
    d0 = exchange(d0, aligned)
    (qkv0,) = call(
        functools.partial(attend_back_kernel, 0, False), [wide], 2, head0, logit_scale, x0, saved0, d0
    )
    (parts,) = call(
        weights_kernel,
        [((DEVS, 16, 256), bf16)],
        0,
        qkv0,
        qkv1,
        tokens0_all,
        tokens1_all,
        grad_y1_all,
        grad_proj0,
        gains0,
        gains1,
    )
    parts = lax.all_to_all(parts, "rows", 0, 0, tiled=True)
    (share,) = call(reduce_kernel, [((8, 2176), f32)], 0, parts)
    others = [lax.ppermute(share, "dp", [(i, i ^ k) for i in range(4)]) for k in (1, 2, 3)]
    d_qkv0 = exchange(qkv0, aligned)
    (grad_image,) = call(last_kernel, [cells], 0, d_qkv0, w_qkv[0], grad0)
    grad_qkv, grad_proj, small = call(
        final_kernel, [((2, 8, 768), f32), ((2, HH, 8), f32), ((128, 8), f32)], 0, share, *others
    )
    small = small[96:104].reshape(2, 2, 2, 8).sum(2)
    return (grad_image.reshape(image.shape), grad_qkv, grad_proj, small[:, 0], small[:, 1])


def solution(mesh):
    placed = (P("dp", "rows", None, None), P("dp", "rows", None, None)) + (P(),) * 7
    return jax.shard_map(
        body,
        mesh=mesh,
        in_specs=placed,
        out_specs=(
            P("dp", "rows", None, None),
            P(None, "rows", None),
            P(None, None, "rows"),
            P(None, "rows"),
            P(None, "rows"),
        ),
        check_vma=False,
    )
```

time: 764 us -> 204 us (0.27)
  waiting for transfers between devices: 331 us -> 44.3 us
  matrix products: 120 us -> 0 us
  local copies, waits for them, and re-layouts: 111 us -> 11.3 us
  other arithmetic: 42.4 us -> 0.02 us
  Pallas kernels: 0 us -> 25.4 us
  starting transfers between devices: 62.9 us -> 41.5 us
  blocking collectives: 74 us -> 65.3 us
    psum x1 -> x0, waiting for transfers between devices: 187 us -> none  [body(): lax.psum((weight_grads[0], weight_grads[1], weight_grads[2], weight_grads...]
    ppermute x15 -> x3, waiting for transfers between devices: 144 us -> 4.01 us  [body(): lax.ppermute(share, 'dp', [(i, i ^ k) for i in range(4)])]
    dot_general x92 -> x0, matrix products: 106 us -> none  [the longest x16 22.9 us: one_head(): jnp.einsum('wqk,wkd->wqd', softmaxed, v_head, preferred_element_type=jnp....]
    psum x1 -> x0, blocking collectives: 74 us -> none  [body(): lax.psum((weight_grads[0], weight_grads[1], weight_grads[2], weight_grads...]
    all_to_all x0 -> x4, blocking collectives: none -> 65.3 us  [the longest x3 46.3 us: exchange(): lax.all_to_all(array, 'rows', 0, 0, axis_index_groups=groups, tiled=True)]
    ppermute x15 -> x3, starting transfers between devices: 62.9 us -> 9.94 us  [body(): lax.ppermute(share, 'dp', [(i, i ^ k) for i in range(4)])]
    all_to_all x0 -> x5, starting transfers between devices: none -> 31.5 us  [exchange(): lax.all_to_all(array, 'rows', 0, 0, axis_index_groups=groups, tiled=True)]
    reshape x16 -> x0, local copies, waits for them, and re-layouts: 31.1 us -> none  [the longest x2 15.1 us: key_windows(): return gathered.reshape(WIN, windows_across, WIN, 2, HEADS, HD).transpose...]
  transfers between devices with their start and end apart: 16 -> 11, of which waited for: 13 -> 7; matrix products, arithmetic and copies ran while one was open for 4% -> 1% of each run, Pallas kernels for 0% -> 11%
where the time goes in v1:
time: 204 us; the launch traced here: 202 us
  blocking collectives  65.3 us (32%)
  waiting for transfers between devices  44.3 us (22%)
  starting transfers between devices  41.5 us (20%)
  Pallas kernels  25.4 us (12%)
  between operations  13.9 us (7%)
  local copies, waits for them, and re-layouts  11.3 us (6%)
    all_to_all x3, blocking collectives, exchange(): lax.all_to_all(array, 'rows', 0, 0, axis_index_groups=groups, tiled=True)  46.3 us
    all_to_all x5, starting transfers between devices, exchange(): lax.all_to_all(array, 'rows', 0, 0, axis_index_groups=groups, tiled=True)  31.5 us
    all_to_all x5, waiting for transfers between devices, exchange(): lax.all_to_all(array, 'rows', 0, 0, axis_index_groups=groups, tiled=True)  23.8 us
    all_to_all x1, blocking collectives, body(): parts = lax.all_to_all(parts, 'rows', 0, 0, tiled=True)  19.1 us
    pallas_call x10, Pallas kernels, call(): pl.pallas_call(kernel, out_shape=[jax.ShapeDtypeStruct(shape, dtype) for...  17.8 us
    all_gather x3, waiting for transfers between devices, gather(): return lax.all_gather(array, 'rows', axis_index_groups=groups, tiled=True)  15.7 us
    ppermute x3, starting transfers between devices, body(): lax.ppermute(share, 'dp', [(i, i ^ k) for i in range(4)])  9.94 us
    unnamed x35, local copies, waits for them, and re-layouts  9.14 us
  transfers between devices with their start and end apart: 11, of which 7 were waited for; matrix products, arithmetic and copies ran while one was open for 1% of the time, Pallas kernels for 11%

profile of v1, /device:TPU:1, one launch (start us, length us, event | category | flops | bytes accessed | tf_op | source)
XLA Modules:
  0.0 201.7 jit_solution(2831100378659844905)
XLA Ops:
  7.2 0.0 all-gather.4.cloned.1.call-start
  7.2 0.7 all-gather.4.cloned.1.call-update
  7.9 0.0 copy-start
  7.9 0.0 copy-start.12
  7.9 1.5 slice_bitcast_fusion
  9.4 0.0 copy-start.16
  9.4 0.0 copy-done
  9.5 0.0 copy-done.12
  9.5 1.2 shard_map.128
  10.6 0.0 copy-start.11
  10.7 0.0 copy-start.13
  10.7 19.6 %all_to_all.45.x_ref = bf16[8,144,128]{2,1,0:T(8,128)(2,1)S(1)} all-to-all(bf16[8,144,128]{2,1,0:T(8,128)(2,1)S(1)} %shard_map.128), channel_id=1, replica_groups={{0,1,2,3,4,5,6,7},{8,9,10,11,12,13,14,15},{16,17,18,19,20,21,22,23},{24..., dimensions={0} | all-to-all | bytes 589824 | tf_op jit(solution)/shard_map/all_to_all | solution.py:348
  30.3 1.9 shard_map.129
  32.2 0.8 copy-done.5
  33.1 3.9 %all-to-all-start.1 = ((bf16[8,48,128]{2,1,0:T(8,128)(2,1)}), bf16[8,48,128]{2,1,0:T(8,128)(2,1)S(1)}, u32[]{:S(2)}, u32[]{:S(2)}) async-start(bf16[8,48,128]{2,1,0:T(8,128)(2,1)} %get-tuple-element.22), calls=%async_computation.1 | async-start | bytes 196608 | tf_op jit(solution)/shard_map/all_to_all | solution.py:348
  36.9 0.0 all-gather.6.cloned.1.call-start
  37.0 0.0 copy-done.16
  37.0 0.0 copy-start.14
  37.0 0.0 copy-start.15
  37.1 8.0 %all-to-all-done.1.packed_ref = bf16[8,48,128]{2,1,0:T(8,128)(2,1)S(1)} async-done(((bf16[8,48,128]{2,1,0:T(8,128)(2,1)}), bf16[8,48,128]{2,1,0:T(8,128)(2,1)S(1)}, u32[]{:S(2)}, u32[]{:S(2)}) %all-to-all-start.1) | async-done | bytes 98336 | tf_op jit(solution)/shard_map/all_to_all | solution.py:348
  45.1 0.0 copy-done.11
  45.1 0.0 copy-done.13
  45.1 2.4 %shard_map.130 = (bf16[144,512]{1,0:T(8,128)(2,1)}, bf16[8,144,128]{2,1,0:T(8,128)(2,1)}) custom-call(f32[2,8]{1,0:T(2,128)S(1)} %copy-done.12, bf16[8,48,128]{2,1,0:T(8,128)(2,1)S(1)} %all-to-all-done.1.packed_ref, bf16[144,512]{1,0:T(8,128)(2,1)S(1)} %bitcast.21, bf16[256,512]{1,0:T(8,128)(2,1)S(1)} %get-tuple-element.50.w_proj_ref, ...), custom_call_target="tpu_custom_call" | custom-call | tf_op jit(solution)/shard_map/pallas_call | solution.py:327
  47.5 0.0 all-gather.6.cloned.1.call-update
  47.5 9.7 %all-to-all-start.2 = ((bf16[8,144,128]{2,1,0:T(8,128)(2,1)}), bf16[8,144,128]{2,1,0:T(8,128)(2,1)S(1)}, u32[]{:S(2)}, u32[]{:S(2)}) async-start(bf16[8,144,128]{2,1,0:T(8,128)(2,1)} %get-tuple-element.23), calls=%async_computation.2 | async-start | bytes 589824 | tf_op jit(solution)/shard_map/all_to_all | solution.py:348
  57.2 0.0 all-gather.8.cloned.1.call-start
  57.2 4.6 %all-to-all-done.2.x_ref = bf16[8,144,128]{2,1,0:T(8,128)(2,1)S(1)} async-done(((bf16[8,144,128]{2,1,0:T(8,128)(2,1)}), bf16[8,144,128]{2,1,0:T(8,128)(2,1)S(1)}, u32[]{:S(2)}, u32[]{:S(2)}) %all-to-all-start.2) | async-done | bytes 294944 | tf_op jit(solution)/shard_map/all_to_all | solution.py:348
  61.8 0.0 copy-done.14
  61.8 0.0 copy-done.15
  61.8 1.9 shard_map.131
  63.7 0.8 copy-done.7
  64.5 12.2 %all_to_all.46.packed_ref = bf16[8,48,128]{2,1,0:T(8,128)(2,1)S(1)} all-to-all(bf16[8,48,128]{2,1,0:T(8,128)(2,1)S(1)} %get-tuple-element.25), channel_id=1, replica_groups={{4,5,6,7,8,9,10,11},{12,13,14,15,16,17,18,19},{20,21,22,23,24,25,26,27}..., dimensions={0} | all-to-all | bytes 196608 | tf_op jit(solution)/shard_map/all_to_all | solution.py:348
  76.7 1.4 shard_map.132
  78.1 0.0 all-gather.8.cloned.1.call-update
  78.1 10.8 %all-to-all-start.4 = ((bf16[8,48,128]{2,1,0:T(8,128)(2,1)}), bf16[8,48,128]{2,1,0:T(8,128)(2,1)S(1)}, u32[]{:S(2)}, u32[]{:S(2)}) async-start(bf16[8,48,128]{2,1,0:T(8,128)(2,1)} %get-tuple-element.26), calls=%async_computation.4 | async-start | bytes 196608 | tf_op jit(solution)/shard_map/all_to_all | solution.py:348
  88.9 2.8 %all-to-all-done.4.grad_ref = bf16[8,48,128]{2,1,0:T(8,128)(2,1)S(1)} async-done(((bf16[8,48,128]{2,1,0:T(8,128)(2,1)}), bf16[8,48,128]{2,1,0:T(8,128)(2,1)S(1)}, u32[]{:S(2)}, u32[]{:S(2)}) %all-to-all-start.4) | async-done | bytes 98336 | tf_op jit(solution)/shard_map/all_to_all | solution.py:348
  91.7 1.1 copy-done.8
  92.8 5.6 %shard_map.133.qkv1_ref = bf16[8,144,128]{2,1,0:T(8,128)(2,1)S(1)} custom-call(s32[1]{0:T(128)} %bitcast.3.head_ref, f32[2,8]{1,0:T(2,128)S(1)} %copy-done.12, bf16[8,144,128]{2,1,0:T(8,128)(2,1)S(1)} %all-to-all-done.2.x_ref, f32[2,576,128]{2,1,0:T(8,128)S(1)} %copy-done.8, bf16[8,48,128]{2,1,0:T(8,128)(2,1)S(1)} %all-to-all-done.4.grad_ref, ...), custom_call_target="tpu_custom_call" | custom-call | tf_op jit(solution)/shard_map/pallas_call | solution.py:378
  98.4 14.5 %all_to_all.47.qkv_ref = bf16[8,144,128]{2,1,0:T(8,128)(2,1)S(1)} all-to-all(bf16[8,144,128]{2,1,0:T(8,128)(2,1)S(1)} %shard_map.133.qkv1_ref), channel_id=1, replica_groups={{4,5,6,7,8,9,10,11},{12,13,14,15,16,17,18,19},{20,21,22,23,24,25,26,27}..., dimensions={0} | all-to-all | bytes 589824 | tf_op jit(solution)/shard_map/all_to_all | solution.py:348
  112.8 1.7 shard_map.134
  114.5 0.8 copy-done.9
  115.3 3.7 %all-to-all-start.6 = ((bf16[8,48,128]{2,1,0:T(8,128)(2,1)}), bf16[8,48,128]{2,1,0:T(8,128)(2,1)S(1)}, u32[]{:S(2)}, u32[]{:S(2)}) async-start(bf16[8,48,128]{2,1,0:T(8,128)(2,1)} %get-tuple-element.27), calls=%async_computation.6 | async-start | bytes 196608 | tf_op jit(solution)/shard_map/all_to_all | solution.py:348
  119.0 8.4 %all-to-all-done.6.grad_ref = bf16[8,48,128]{2,1,0:T(8,128)(2,1)S(1)} async-done(((bf16[8,48,128]{2,1,0:T(8,128)(2,1)}), bf16[8,48,128]{2,1,0:T(8,128)(2,1)S(1)}, u32[]{:S(2)}, u32[]{:S(2)}) %all-to-all-start.6) | async-done | bytes 98336 | tf_op jit(solution)/shard_map/all_to_all | solution.py:348
  127.4 1.1 copy-done.6
  128.5 5.5 %shard_map.135.qkv0_ref = bf16[8,144,128]{2,1,0:T(8,128)(2,1)} custom-call(s32[1]{0:T(128)} %bitcast.head_ref, f32[2,8]{1,0:T(2,128)S(1)} %copy-done.12, bf16[8,144,128]{2,1,0:T(8,128)(2,1)S(1)} %all_to_all.45.x_ref, f32[2,576,128]{2,1,0:T(8,128)S(1)} %copy-done.6, bf16[8,48,128]{2,1,0:T(8,128)(2,1)S(1)} %all-to-all-done.6.grad_ref), custom_call_target="tpu_custom_call" | custom-call | tf_op jit(solution)/shard_map/pallas_call | solution.py:327
  134.0 15.7 %all-gather.8.cloned.1.call-done.grad_y1_ref = bf16[1152,512]{1,0:T(8,128)(2,1)} async-done(((bf16[144,512]{1,0:T(8,128)(2,1)}), bf16[1152,512]{1,0:T(8,128)(2,1)}) %all-gather.8.cloned.1.call-update) | async-done | bytes 1179664 | tf_op jit(solution)/shard_map/all_gather | solution.py:351
  149.8 1.3 copy-done.1
  151.1 1.3 copy-done.2
  152.3 1.3 copy-done.3
  153.6 1.8 shard_map.137
  155.4 19.1 %all_to_all.48.parts_ref = bf16[64,16,256]{2,1,0:T(8,128)(2,1)S(1)} all-to-all(bf16[64,16,256]{2,1,0:T(8,128)(2,1)S(1)} %shard_map.137), channel_id=1, replica_groups=mesh['dp'=4,'rows'=64] {'rows'}, dimensions={0} | all-to-all | bytes 1048576 | tf_op jit(solution)/shard_map/all_to_all | solution.py:423
  174.5 3.4 %all-to-all-start.7 = ((bf16[8,144,128]{2,1,0:T(8,128)(2,1)}), bf16[8,144,128]{2,1,0:T(8,128)(2,1)S(1)}, u32[]{:S(2)}, u32[]{:S(2)}) async-start(bf16[8,144,128]{2,1,0:T(8,128)(2,1)} %shard_map.135.qkv0_ref), calls=%async_computation.7 | async-start | bytes 589824 | tf_op jit(solution)/shard_map/all_to_all | solution.py:348
  177.9 0.2 shard_map.138.a_ref
  178.1 6.7 %collective-permute-start = (f32[8,2176]{1,0:T(8,128)S(1)}, f32[8,2176]{1,0:T(8,128)S(1)}, u32[]{:S(2)}, u32[]{:S(2)}) collective-permute-start(f32[8,2176]{1,0:T(8,128)S(1)} %shard_map.138.a_ref), channel_id=1, source_target_pairs={{0,64},{64,0},{128,192},{192,128},{1,65},{65,1},{129,193},{193,129... | collective-permute-start | bytes 208904 | tf_op jit(solution)/shard_map/ppermute | solution.py:425
  184.8 2.7 %collective-permute-start.1 = (f32[8,2176]{1,0:T(8,128)S(1)}, f32[8,2176]{1,0:T(8,128)S(1)}, u32[]{:S(2)}, u32[]{:S(2)}) collective-permute-start(f32[8,2176]{1,0:T(8,128)S(1)} %shard_map.138.a_ref), channel_id=1, source_target_pairs={{0,128},{64,192},{128,0},{192,64},{1,129},{65,193},{129,1},{193,65... | collective-permute-start | bytes 208904 | tf_op jit(solution)/shard_map/ppermute | solution.py:425
  187.5 0.5 collective-permute-start.2
  188.0 0.0 all-to-all-done.7.qkv_ref
  188.0 1.1 shard_map.136
  189.1 0.0 collective-permute-done.b_ref
  189.1 0.9 collective-permute-done.1.c_ref
  190.0 3.1 %collective-permute-done.2.d_ref = f32[8,2176]{1,0:T(8,128)S(1)} collective-permute-done((f32[8,2176]{1,0:T(8,128)S(1)}, f32[8,2176]{1,0:T(8,128)S(1)}, u32[]{:S(2)}, u32[]{:S(2)}) %collective-permute-start.2) | collective-permute-done | bytes 69664 | tf_op jit(solution)/shard_map/ppermute | solution.py:425
  193.1 0.7 shard_map.139
  193.8 0.7 copy.15
  194.6 0.6 fusion
  (17 shorter events, 0.1 us)
Async XLA Ops:
  7.2 126.9 %all-gather.4.cloned.1.call-start = ((), (), s32[]{:S(2)}) async-start(), calls=%async_computation.9 | async-start | bytes 1327104 | tf_op jit(solution)/shard_map/all_gather | solution.py:351
  7.9 1.5 copy-start
  7.9 1.5 copy-start.12
  9.4 27.6 %copy-start.16 = (bf16[2,256,512]{2,1,0:T(8,128)(2,1)S(1)}, bf16[2,256,512]{2,1,0:T(8,128)(2,1)}, u32[]{:S(2)}) copy-start(bf16[2,256,512]{2,1,0:T(8,128)(2,1)} %param.12) | copy-start | bytes 1572868
  10.6 34.5 %copy-start.11 = (f32[2,512]{1,0:T(2,128)S(1)}, f32[2,512]{1,0:T(2,128)}, u32[]{:S(2)}) copy-start(f32[2,512]{1,0:T(2,128)} %gain_ref.5) | copy-start | bytes 12292
  10.7 34.4 %copy-start.13 = (f32[2,512]{1,0:T(2,128)S(1)}, f32[2,512]{1,0:T(2,128)}, u32[]{:S(2)}) copy-start(f32[2,512]{1,0:T(2,128)} %bias_ref.1) | copy-start | bytes 12292
  32.2 0.8 copy-start.5
  33.1 12.0 %all-to-all-start.1 = ((bf16[8,48,128]{2,1,0:T(8,128)(2,1)}), bf16[8,48,128]{2,1,0:T(8,128)(2,1)S(1)}, u32[]{:S(2)}, u32[]{:S(2)}) async-start(bf16[8,48,128]{2,1,0:T(8,128)(2,1)} %get-tuple-element.22), calls=%async_computation.1 | async-start | bytes 196608 | tf_op jit(solution)/shard_map/all_to_all | solution.py:348
  36.9 97.1 %all-gather.6.cloned.1.call-start = ((), (), s32[]{:S(2)}) async-start(), calls=%async_computation.10 | async-start | bytes 1327104 | tf_op jit(solution)/shard_map/all_gather | solution.py:351
  37.0 24.7 %copy-start.14 = (s32[192]{0:T(256)S(1)}, s32[192]{0:T(256)}, u32[]{:S(2)}) copy-start(s32[192]{0:T(256)} %param.16) | copy-start | bytes 2308
  37.0 24.7 %copy-start.15 = (s32[48]{0:T(128)S(1)}, s32[48]{0:T(128)}, u32[]{:S(2)}) copy-start(s32[48]{0:T(128)} %param.17) | copy-start | bytes 580
  45.1 31.6 %copy-start.4 = (bf16[1,3,48,512]{3,2,1,0:T(8,128)(2,1)S(1)}, bf16[1,3,48,512]{3,2,1,0:T(8,128)(2,1)}, u32[]{:S(2)}) copy-start(bf16[1,3,48,512]{3,2,1,0:T(8,128)(2,1)} %param.10) | copy-start | bytes 442372
  47.5 14.3 %all-to-all-start.2 = ((bf16[8,144,128]{2,1,0:T(8,128)(2,1)}), bf16[8,144,128]{2,1,0:T(8,128)(2,1)S(1)}, u32[]{:S(2)}, u32[]{:S(2)}) async-start(bf16[8,144,128]{2,1,0:T(8,128)(2,1)} %get-tuple-element.23), calls=%async_computation.2 | async-start | bytes 589824 | tf_op jit(solution)/shard_map/all_to_all | solution.py:348
  57.2 92.6 %all-gather.8.cloned.1.call-start = ((), (), s32[]{:S(2)}) async-start(), calls=%async_computation.11 | async-start | bytes 1327104 | tf_op jit(solution)/shard_map/all_gather | solution.py:351
  63.7 0.8 copy-start.7
  78.1 13.6 %all-to-all-start.4 = ((bf16[8,48,128]{2,1,0:T(8,128)(2,1)}), bf16[8,48,128]{2,1,0:T(8,128)(2,1)S(1)}, u32[]{:S(2)}, u32[]{:S(2)}) async-start(bf16[8,48,128]{2,1,0:T(8,128)(2,1)} %get-tuple-element.26), calls=%async_computation.4 | async-start | bytes 196608 | tf_op jit(solution)/shard_map/all_to_all | solution.py:348
  91.7 1.1 copy-start.8
  114.5 0.8 copy-start.9
  115.3 12.1 %all-to-all-start.6 = ((bf16[8,48,128]{2,1,0:T(8,128)(2,1)}), bf16[8,48,128]{2,1,0:T(8,128)(2,1)S(1)}, u32[]{:S(2)}, u32[]{:S(2)}) async-start(bf16[8,48,128]{2,1,0:T(8,128)(2,1)} %get-tuple-element.27), calls=%async_computation.6 | async-start | bytes 196608 | tf_op jit(solution)/shard_map/all_to_all | solution.py:348
  127.4 1.1 copy-start.6
  128.5 21.3 %copy-start.10 = (f32[512,256]{1,0:T(8,128)S(1)}, f32[512,256]{1,0:T(8,128)}, u32[]{:S(2)}) copy-start(f32[512,256]{1,0:T(8,128)} %copy-done.9) | copy-start | bytes 1572868
  149.8 1.3 copy-start.1
  151.0 1.3 copy-start.2
  152.3 1.3 copy-start.3
  174.5 13.6 %all-to-all-start.7 = ((bf16[8,144,128]{2,1,0:T(8,128)(2,1)}), bf16[8,144,128]{2,1,0:T(8,128)(2,1)S(1)}, u32[]{:S(2)}, u32[]{:S(2)}) async-start(bf16[8,144,128]{2,1,0:T(8,128)(2,1)} %shard_map.135.qkv0_ref), calls=%async_computation.7 | async-start | bytes 589824 | tf_op jit(solution)/shard_map/all_to_all | solution.py:348
  178.1 11.0 %collective-permute-start = (f32[8,2176]{1,0:T(8,128)S(1)}, f32[8,2176]{1,0:T(8,128)S(1)}, u32[]{:S(2)}, u32[]{:S(2)}) collective-permute-start(f32[8,2176]{1,0:T(8,128)S(1)} %shard_map.138.a_ref), channel_id=1, source_target_pairs={{0,64},{64,0},{128,192},{192,128},{1,65},{65,1},{129,193},{193,129... | collective-permute-start | bytes 208904 | tf_op jit(solution)/shard_map/ppermute | solution.py:425
  184.8 5.2 %collective-permute-start.1 = (f32[8,2176]{1,0:T(8,128)S(1)}, f32[8,2176]{1,0:T(8,128)S(1)}, u32[]{:S(2)}, u32[]{:S(2)}) collective-permute-start(f32[8,2176]{1,0:T(8,128)S(1)} %shard_map.138.a_ref), channel_id=1, source_target_pairs={{0,128},{64,192},{128,0},{192,64},{1,129},{65,193},{129,1},{193,65... | collective-permute-start | bytes 208904 | tf_op jit(solution)/shard_map/ppermute | solution.py:425
  187.5 5.7 %collective-permute-start.2 = (f32[8,2176]{1,0:T(8,128)S(1)}, f32[8,2176]{1,0:T(8,128)S(1)}, u32[]{:S(2)}, u32[]{:S(2)}) collective-permute-start(f32[8,2176]{1,0:T(8,128)S(1)} %shard_map.138.a_ref), channel_id=1, source_target_pairs={{0,192},{64,128},{128,64},{192,0},{1,193},{65,129},{129,65},{193,1... | collective-permute-start | bytes 208904 | tf_op jit(solution)/shard_map/ppermute | solution.py:425
Sparse Core Ops, SparseCore 0:
  9.8 40.7 all-gather.3
  52.9 48.9 all-gather.5
  103.6 46.0 all-gather.7

commit v2 on v1

v2 whole, which is shorter than its diff:
```python
import functools

import jax
import jax.numpy as jnp
from jax import lax
from jax.experimental import pallas as pl
from jax.experimental.pallas import tpu as pltpu
from jax.sharding import PartitionSpec as P

C = 512
HEADS = 8
HD = 32
WIN = 24
HH = 256
SHIFT = 12
GROUP = 8
TOK = 144
CELLS = WIN * WIN
ROWS_DEV = 3
PACK = 48
DEVS = 64
SENT = 2 * 3 * HH + 2 * HH + 128
HALF = 1152

norm_eps = 1e-05
mask_value = 100.0
f32 = jnp.float32
bf16 = jnp.bfloat16


def dot(a, b):
    return jnp.dot(a, b, preferred_element_type=f32)


def dot_t(a, b):
    return lax.dot_general(a, b, (((1,), (1,)), ((), ())), preferred_element_type=f32)


def dot_0(a, b):
    return lax.dot_general(a, b, (((0,), (0,)), ((), ())), preferred_element_type=f32)


def iota(shape, axis):
    return lax.broadcasted_iota(jnp.int32, shape, axis)


def head_sums(x):
    width = x.shape[1]
    ones = (iota((width, width), 0) // HD == iota((width, width), 1) // HD).astype(f32).astype(bf16)
    high = x.astype(bf16)
    low = (x - high.astype(f32)).astype(bf16)
    return dot(high, ones) + dot(low, ones)


def split_two(x):
    high = x.astype(bf16).astype(f32)
    return high, x - high


def lane_slice(x, at):
    return x[:, at : at + HD]


def send_projected(tokens, weight, scale_ref, block, out_ref):
    projected = dot(tokens, weight)
    query, key, value = projected[:, :HH], projected[:, HH : 2 * HH], projected[:, 2 * HH :]
    lane = iota((1, HH), 1)
    scale = jnp.zeros((1, HH), f32)
    for h in range(HEADS):
        scale = jnp.where(lane // HD == h, scale_ref[block, h], scale)
    q_factor = lax.rsqrt(1.0 + head_sums(query * query))
    k_factor = lax.rsqrt(1.0 + head_sums(key * key))
    q_hat = query * q_factor * jnp.exp(scale)
    k_hat = key * k_factor
    q_high, q_low = split_two(q_factor)
    k_high, k_low = split_two(k_factor)
    slot = iota(q_hat.shape, 1) % HD
    extra = jnp.where(
        slot == 0,
        q_high,
        jnp.where(slot == 1, q_low, jnp.where(slot == 2, k_high, jnp.where(slot == 3, k_low, 0.0))),
    )
    for h in range(HEADS):
        at = h * HD
        out_ref[h] = jnp.concatenate(
            [lane_slice(q_hat, at), lane_slice(k_hat, at), lane_slice(value, at), lane_slice(extra, at)], 1
        ).astype(bf16)


def unpack_heads(packed_ref):
    packed = [packed_ref[h].astype(f32) for h in range(HEADS)]
    rows = [
        jnp.concatenate([lane_slice(packed[h], r * HD) for h in range(HEADS)], 1)
        for r in range(ROWS_DEV)
    ]
    return jnp.concatenate(rows, 0).astype(bf16)


def pack_heads(array, out_ref):
    zeros = jnp.zeros((PACK, HD), f32)
    for h in range(HEADS):
        out_ref[h] = jnp.concatenate(
            [lane_slice(array[r * PACK : (r + 1) * PACK], h * HD) for r in range(ROWS_DEV)] + [zeros], 1
        ).astype(bf16)


def to_windows(array):
    split = array.reshape(GROUP, ROWS_DEV, 2, WIN, array.shape[-1])
    return [split[:, :, w].reshape(CELLS, array.shape[-1]) for w in range(2)]


def from_windows(pair):
    depth = pair[0].shape[-1]
    parts = [part.reshape(GROUP, ROWS_DEV, 1, WIN, depth) for part in pair]
    return jnp.concatenate(parts, 2).reshape(GROUP, TOK, depth)


def roll_tokens(array, by):
    by = by % TOK
    return jnp.concatenate([array[TOK - by :], array[: TOK - by]], 0)


def normalized(attended, weight):
    outputs = dot(attended, weight)
    centered = outputs - jnp.mean(outputs, -1, keepdims=True)
    inverse = lax.rsqrt(jnp.mean(centered * centered, -1, keepdims=True) + norm_eps)
    return centered * inverse, inverse


def finish_back(attended, weight, gain_row, grad_out):
    y_hat, inverse = normalized(attended, weight)
    grad_gain = jnp.sum(grad_out * y_hat, 0, keepdims=True)
    grad_bias = jnp.sum(grad_out, 0, keepdims=True)
    scaled = grad_out * gain_row
    grad_y = inverse * (
        scaled
        - jnp.mean(scaled, -1, keepdims=True)
        - y_hat * jnp.mean(scaled * y_hat, -1, keepdims=True)
    )
    grad_y = grad_y.astype(bf16)
    gains = jnp.concatenate([grad_gain, grad_bias, jnp.zeros((6, C), f32)], 0)
    return grad_y, dot_t(grad_y, weight), gains


def labels_of(axis, window, first_row, row_ref, col_ref):
    shape = (CELLS, 1) if axis == 0 else (1, CELLS)
    at = iota(shape, axis)
    source = at // (ROWS_DEV * WIN)
    rest = at - source * (ROWS_DEV * WIN)
    local_row = rest // WIN
    column = rest - local_row * WIN + window * WIN
    local_row = local_row + (column >= 36).astype(jnp.int32)
    local_row = jnp.where(local_row >= ROWS_DEV, local_row - ROWS_DEV, local_row)
    row = first_row + source * ROWS_DEV + local_row
    row_label = jnp.zeros(shape, jnp.int32)
    col_label = jnp.zeros(shape, jnp.int32)
    for label in (1, 2):
        row_cut = jnp.sum((row_ref[...] < label).astype(jnp.int32), 1, keepdims=True)
        col_cut = jnp.sum((col_ref[...] < label).astype(jnp.int32), 1, keepdims=True)
        row_label = row_label + (row >= row_cut).astype(jnp.int32)
        col_label = col_label + (column >= col_cut).astype(jnp.int32)
    return 3 * row_label + col_label


def masked(scores, window, mask_refs):
    if mask_refs is None:
        return scores
    first_row = mask_refs[0][0]
    one = labels_of(0, window, first_row, *mask_refs[1:])
    two = labels_of(1, window, first_row, *mask_refs[1:])
    return scores - jnp.where(one == two, 0.0, mask_value)


def attend_kernel(masks, x_ref, *refs):
    mask_refs = refs[:3] if masks else None
    out_ref = refs[-1]
    lane = iota((CELLS, 128), 1)
    per_window = []
    for w, cells in enumerate(to_windows(x_ref[...].astype(f32))):
        query = cells[:, :HD].astype(bf16)
        key = cells[:, HD : 2 * HD].astype(bf16)
        value = jnp.where(lane < HD, pltpu.roll(cells, 64, 1), jnp.where(lane == HD, 1.0, 0.0)).astype(bf16)
        scores = masked(dot_t(query, key), w, mask_refs)
        weights = jnp.exp(scores).astype(bf16)
        summed = dot(weights, value)
        attended = jnp.where(lane < HD, summed * (1.0 / summed[:, HD : HD + 1]), 0.0)
        per_window.append(attended.reshape(GROUP, ROWS_DEV, WIN, 128))
    total = 0.0
    for r in range(ROWS_DEV):
        rows = jnp.concatenate([part[:, r] for part in per_window], 1).reshape(GROUP * PACK, 128)
        total = total + (rows if r == 0 else pltpu.roll(rows, r * HD, 1))
    out_ref[...] = total.astype(bf16).reshape(GROUP, PACK, 128)


def attend_back_kernel(block, masks, head_ref, scale_ref, x_ref, grad_ref, *refs):
    mask_refs = refs[:3] if masks else None
    out_ref = refs[-1]
    lane = iota((CELLS, 128), 1)
    low = iota((HD, CELLS), 0)
    scale_row = jnp.exp(jnp.full((1, 128), scale_ref[block, head_ref[0]], f32))
    packed = grad_ref[...].astype(f32).reshape(GROUP * PACK, 128)
    rolled = [packed if r == 0 else pltpu.roll(packed, 128 - r * HD, 1) for r in range(ROWS_DEV)]
    rolled = [part.reshape(GROUP, 1, 2, WIN, 128) for part in rolled]
    grads = jnp.concatenate(rolled, 1)
    results = []
    for w, cells in enumerate(to_windows(x_ref[...].astype(f32))):
        turned = cells.T
        query_t = turned[:HD].astype(bf16)
        key_t = turned[HD : 2 * HD].astype(bf16)
        value_t = turned[2 * HD : 3 * HD]
        grad_t = grads[:, :, w].reshape(CELLS, 128).T[:HD]
        key = cells[:, HD : 2 * HD].astype(bf16)
        scores = masked(dot(key, query_t), w, mask_refs)
        weights = jnp.exp(scores).astype(bf16)
        summed = dot(jnp.concatenate([value_t, jnp.where(low == 0, 1.0, 0.0)], 0).astype(bf16), weights)
        inverse = 1.0 / summed[HD : HD + 1]
        grad_t = (grad_t * inverse).astype(bf16).astype(f32)
        row_high, row_low = split_two(jnp.sum(grad_t * summed[:HD], 0, keepdims=True) * inverse)
        rows = jnp.where(low == 0, -row_high, jnp.where(low == 1, -row_low, 0.0))
        grad_ext = jnp.concatenate([grad_t, rows], 0).astype(bf16)
        ones = jnp.where(lane < HD + 2, 1.0, 0.0)
        value_ext = jnp.where(lane < HD, pltpu.roll(cells, 64, 1), ones)[:, :64].astype(bf16)
        grad_scores = (weights.astype(f32) * dot(value_ext, grad_ext)).astype(bf16)
        query_at = jnp.where((lane >= HD) & (lane < 2 * HD), pltpu.roll(cells, HD, 1), 0.0).astype(bf16)
        zeros = jnp.zeros((HD, CELLS), f32)
        grad_at = jnp.concatenate([zeros, zeros, grad_t, zeros], 0).T.astype(bf16)
        grad_kv = dot(grad_scores, query_at) + dot(weights, grad_at)
        grad_q = dot(key_t, grad_scores)
        grad_q = jnp.concatenate([grad_q, zeros, zeros, zeros], 0).T
        total = jnp.where(lane < HD, grad_q * scale_row, grad_kv)
        unit = jnp.where(lane < HD, cells / scale_row, jnp.where(lane < 2 * HD, cells, 0.0))
        q_factor = cells[:, 96:97] + cells[:, 97:98]
        k_factor = cells[:, 98:99] + cells[:, 99:100]
        factor = jnp.where(lane < HD, q_factor, jnp.where(lane < 2 * HD, k_factor, 1.0))
        results.append(factor * (total - unit * head_sums(unit * total)))
    out_ref[...] = from_windows(results).astype(bf16)


def first_kernel(scale_ref, tokens_ref, w_ref, out_ref):
    send_projected(tokens_ref[...], w_ref[0], scale_ref, 0, out_ref)


def middle_kernel(scale_ref, packed_ref, tokens_ref, w_proj_ref, gain_ref, bias_ref, w_ref, rolled_ref, out_ref):
    attended = unpack_heads(packed_ref)
    y_hat, _ = normalized(attended, w_proj_ref[0])
    out = (tokens_ref[...].astype(f32) + y_hat * gain_ref[0:1] + bias_ref[0:1]).astype(bf16).astype(f32)
    rolled = roll_tokens(out, -SHIFT).astype(bf16)
    rolled_ref[...] = rolled
    send_projected(rolled, w_ref[1], scale_ref, 1, out_ref)


def turn_kernel(packed_ref, grad_ref, w_proj_ref, gain_ref, out_ref, grad_proj_ref, gains_ref):
    attended = unpack_heads(packed_ref)
    grad = roll_tokens(grad_ref[...].astype(f32), -SHIFT)
    grad_y, grad_att, gains = finish_back(attended, w_proj_ref[1], gain_ref[1:2], grad)
    pack_heads(grad_att, out_ref)
    grad_proj_ref[...] = dot_0(grad_y, attended).astype(bf16)
    gains_ref[...] = gains


def gather_qkv(qkv_ref):
    parts = [qkv_ref[h].astype(f32) for h in range(HEADS)]
    return jnp.concatenate(
        [lane_slice(parts[h], kind * HD) for kind in range(3) for h in range(HEADS)], 1
    ).astype(bf16)


def back_kernel(
    qkv_ref,
    w_ref,
    tokens_ref,
    grad_ref,
    packed_ref,
    w_proj_ref,
    gain_ref,
    out_ref,
    grad0_ref,
    grad_qkv_ref,
    grad_proj_ref,
    gains_ref,
):
    d_qkv = gather_qkv(qkv_ref)
    from_qkv = roll_tokens(dot_t(d_qkv, w_ref[1]), SHIFT)
    grad = (grad_ref[...].astype(f32) + from_qkv).astype(bf16)
    grad0_ref[...] = grad
    attended = unpack_heads(packed_ref)
    grad_y, grad_att, gains = finish_back(attended, w_proj_ref[0], gain_ref[0:1], grad.astype(f32))
    pack_heads(grad_att, out_ref)
    grad_qkv_ref[...] = dot_0(tokens_ref[...], d_qkv).astype(bf16)
    grad_proj_ref[...] = dot_0(grad_y, attended).astype(bf16)
    gains_ref[...] = gains


def last_kernel(
    qkv_ref,
    w_ref,
    tokens_ref,
    grad_ref,
    grad_qkv1_ref,
    proj0_ref,
    proj1_ref,
    gains0_ref,
    gains1_ref,
    out_ref,
    parts_ref,
):
    d_qkv = gather_qkv(qkv_ref)
    out_ref[...] = (grad_ref[...].astype(f32) + dot_t(d_qkv, w_ref[0])).astype(bf16)
    pieces = []
    for ref in (gains0_ref, gains1_ref):
        for row in (0, 1):
            pieces += split_two(ref[row : row + 1])
    pieces.append(jnp.zeros((128 - len(pieces), C), f32))
    gains = jnp.concatenate(pieces, 0).T
    at = 0
    for part in (dot_0(tokens_ref[...], d_qkv), grad_qkv1_ref[...], proj0_ref[...], proj1_ref[...], gains):
        width = part.shape[1]
        parts_ref[:, :, at : at + width] = part.astype(bf16).reshape(8, C // 8, width)
        at += width


def first_sum_kernel(parts_ref, out_ref):
    total = jnp.sum(parts_ref[...].astype(f32), 0).reshape(8, 8, SENT)
    right = jnp.concatenate([total[:, :, HALF:], jnp.zeros((8, 8, 2 * HALF - SENT), f32)], 2)
    out_ref[...] = jnp.concatenate([total[:, :, :HALF], right], 1).astype(bf16)


def second_sum_kernel(parts_ref, out_ref):
    out_ref[...] = jnp.sum(parts_ref[...].astype(f32), 0)


def final_kernel(a_ref, b_ref, c_ref, d_ref, qkv_ref, proj_ref, gain_ref, bias_ref):
    total = (a_ref[...] + b_ref[...]) + (c_ref[...] + d_ref[...])
    total = jnp.concatenate([total[:8], total[8:]], 1)
    qkv_ref[0] = total[:, :768]
    qkv_ref[1] = total[:, 768:1536]
    proj_ref[0] = total[:, 1536:1792]
    proj_ref[1] = total[:, 1792:2048]
    gains = total[:, 2048:2176].T
    gain_ref[...] = jnp.concatenate([gains[0:1] + gains[1:2], gains[4:5] + gains[5:6]], 0)
    bias_ref[...] = jnp.concatenate([gains[2:3] + gains[3:4], gains[6:7] + gains[7:8]], 0)


def call(kernel, outs, scalars, arrays, masks=()):
    smem = pl.BlockSpec(memory_space=pltpu.SMEM)
    vmem = pl.BlockSpec(memory_space=pltpu.VMEM)
    specs = [smem] * len(scalars) + [vmem] * len(arrays) + [smem, vmem, vmem][: len(masks)]
    return pl.pallas_call(
        kernel,
        out_shape=[jax.ShapeDtypeStruct(shape, dtype) for shape, dtype in outs],
        in_specs=specs,
        out_specs=[vmem] * len(outs),
        compiler_params=pltpu.CompilerParams(vmem_limit_bytes=24 * 2**20),
    )(*scalars, *arrays, *masks)


def body(image, out_grad, w_qkv, w_proj, norm_gain, norm_bias, logit_scale, row_band, col_band):
    position = lax.axis_index("rows")
    half = GROUP // 2
    rings = range(DEVS // GROUP)
    aligned = [[GROUP * g + i for i in range(GROUP)] for g in rings]
    moved = [[(GROUP * g + half + i) % DEVS for i in range(GROUP)] for g in rings]
    across = [[GROUP * g + i for g in rings] for i in range(GROUP)]
    moved_position = (position + DEVS - half) % DEVS
    head0 = (position % GROUP).reshape(1)
    head1 = (moved_position % GROUP).reshape(1)
    first_row = (moved_position // GROUP * WIN).reshape(1)
    masks = (first_row, row_band.reshape(1, -1), col_band.reshape(1, -1))

    def exchange(array, groups):
        return lax.all_to_all(array, "rows", 0, 0, axis_index_groups=groups, tiled=True)

    tokens0 = image.reshape(TOK, C)
    grad_out = out_grad.reshape(TOK, C)
    wide = ((GROUP, TOK, 128), bf16)
    narrow = ((GROUP, PACK, 128), bf16)
    cells = ((TOK, C), bf16)
    proj = ((C, HH), bf16)
    gains = ((8, C), f32)

    (x0,) = call(first_kernel, [wide], (logit_scale,), (tokens0, w_qkv))
    x0 = exchange(x0, aligned)
    (a0,) = call(functools.partial(attend_kernel, False), [narrow], (), (x0,))
    a0 = exchange(a0, aligned)
    tokens1, x1 = call(
        middle_kernel, [cells, wide], (logit_scale,), (a0, tokens0, w_proj, norm_gain, norm_bias, w_qkv)
    )
    x1 = exchange(x1, moved)
    (a1,) = call(functools.partial(attend_kernel, True), [narrow], (), (x1,), masks)
    a1 = exchange(a1, moved)
    d1, proj1, gains1 = call(turn_kernel, [narrow, proj, gains], (), (a1, grad_out, w_proj, norm_gain))
    d1 = exchange(d1, moved)
    (qkv1,) = call(
        functools.partial(attend_back_kernel, 1, True), [wide], (head1, logit_scale), (x1, d1), masks
    )
    qkv1 = exchange(qkv1, moved)
    d0, grad0, grad_qkv1, proj0, gains0 = call(
        back_kernel,
        [narrow, cells, ((C, 3 * HH), bf16), proj, gains],
        (),
        (qkv1, w_qkv, tokens1, grad_out, a0, w_proj, norm_gain),
    )
    d0 = exchange(d0, aligned)
    (qkv0,) = call(functools.partial(attend_back_kernel, 0, False), [wide], (head0, logit_scale), (x0, d0))
    qkv0 = exchange(qkv0, aligned)
    grad_image, parts = call(
        last_kernel,
        [cells, ((8, C // 8, SENT), bf16)],
        (),
        (qkv0, w_qkv, tokens0, grad0, grad_qkv1, proj0, proj1, gains0, gains1),
    )
    parts = exchange(parts, across)
    (parts,) = call(first_sum_kernel, [((8, 16, HALF), bf16)], (), (parts,))
    parts = exchange(parts, aligned)
    (share,) = call(second_sum_kernel, [((16, HALF), f32)], (), (parts,))
    others = [lax.ppermute(share, "dp", [(i, i ^ k) for i in range(4)]) for k in (1, 2, 3)]
    small = ((2, 8), f32)
    grad_qkv, grad_proj, grad_gain, grad_bias = call(
        final_kernel, [((2, 8, 3 * HH), f32), ((2, 8, HH), f32), small, small], (), (share, *others)
    )
    return (
        grad_image.reshape(image.shape),
        grad_qkv,
        grad_proj.transpose(0, 2, 1),
        grad_gain,
        grad_bias,
    )


def solution(mesh):
    placed = (P("dp", "rows", None, None), P("dp", "rows", None, None)) + (P(),) * 7
    return jax.shard_map(
        body,
        mesh=mesh,
        in_specs=placed,
        out_specs=(
            P("dp", "rows", None, None),
            P(None, "rows", None),
            P(None, None, "rows"),
            P(None, "rows"),
            P(None, "rows"),
        ),
        check_vma=False,
    )
```

time: 204 us -> 197 us (0.966)
  blocking collectives: 65.3 us -> 107 us
  waiting for transfers between devices: 44.3 us -> 18.9 us
  between operations: 13.9 us -> 0.73 us
  Pallas kernels: 25.4 us -> 20.1 us
    all_to_all x3 -> x7, blocking collectives: 46.3 us -> 107 us  [exchange(): lax.all_to_all(array, 'rows', 0, 0, axis_index_groups=groups, tiled=True)]
    all_to_all x1 -> x0, blocking collectives: 19.1 us -> none  [body(): parts = lax.all_to_all(parts, 'rows', 0, 0, tiled=True)]
    all_gather x3 -> x0, waiting for transfers between devices: 15.7 us -> none  [gather(): return lax.all_gather(array, 'rows', axis_index_groups=groups, tiled=True)]
    all_to_all x5 -> x3, waiting for transfers between devices: 23.8 us -> 14.7 us  [exchange(): lax.all_to_all(array, 'rows', 0, 0, axis_index_groups=groups, tiled=True)]
    pallas_call x2 -> x0, Pallas kernels: 7.55 us -> none  [masked_call(): pl.pallas_call(kernel, out_shape=[jax.ShapeDtypeStruct(shape, dtype) for...]
    all_to_all x5 -> x3, starting transfers between devices: 31.5 us -> 24.3 us  [exchange(): lax.all_to_all(array, 'rows', 0, 0, axis_index_groups=groups, tiled=True)]
    ppermute x3, starting transfers between devices: 9.94 us -> 15.2 us  [body(): lax.ppermute(share, 'dp', [(i, i ^ k) for i in range(4)])]
    pallas_call x10 -> x12, Pallas kernels: 17.8 us -> 20.1 us  [call(): pl.pallas_call(kernel, out_shape=[jax.ShapeDtypeStruct(shape, dtype) for...]
  transfers between devices with their start and end apart: 11 -> 6, of which waited for: 7 -> 5; matrix products, arithmetic and copies ran while one was open for 1% -> 0% of each run, Pallas kernels for 11% -> 0%
where the time goes in v2:
time: 197 us; the launch traced here: 196 us
  blocking collectives  107 us (54%)
  starting transfers between devices  39.5 us (20%)
  Pallas kernels  20.1 us (10%)
  waiting for transfers between devices  18.9 us (10%)
  local copies, waits for them, and re-layouts  10.2 us (5%)
    all_to_all x7, blocking collectives, exchange(): lax.all_to_all(array, 'rows', 0, 0, axis_index_groups=groups, tiled=True)  107 us
    all_to_all x3, starting transfers between devices, exchange(): lax.all_to_all(array, 'rows', 0, 0, axis_index_groups=groups, tiled=True)  24.3 us
    pallas_call x12, Pallas kernels, call(): pl.pallas_call(kernel, out_shape=[jax.ShapeDtypeStruct(shape, dtype) for...  20.1 us
    ppermute x3, starting transfers between devices, body(): lax.ppermute(share, 'dp', [(i, i ^ k) for i in range(4)])  15.2 us
    all_to_all x3, waiting for transfers between devices, exchange(): lax.all_to_all(array, 'rows', 0, 0, axis_index_groups=groups, tiled=True)  14.7 us
    unnamed x44, local copies, waits for them, and re-layouts  10.2 us
    ppermute x3, waiting for transfers between devices, body(): lax.ppermute(share, 'dp', [(i, i ^ k) for i in range(4)])  4.2 us
  transfers between devices with their start and end apart: 6, of which 5 were waited for; matrix products, arithmetic and copies ran while one was open for 0% of the time, Pallas kernels for 0%

profile of v2, /device:TPU:1, one launch (start us, length us, event | category | flops | bytes accessed | tf_op | source)
XLA Modules:
  0.0 195.9 jit_solution(4925240206236945793)
XLA Ops:
  0.6 0.0 copy-start
  0.6 1.4 copy-done
  2.0 0.0 copy-start.3
  2.0 0.9 copy-done.3
  3.0 0.0 copy-start.14
  3.0 0.7 copy-done.14
  3.6 0.0 copy-start.1
  3.6 0.0 copy-start.2
  3.6 0.0 copy-start.12
  3.6 0.0 copy-start.19
  3.6 1.2 shard_map.128
  4.8 0.0 copy-start.20
  4.8 0.0 copy-start.21
  4.8 19.7 %all_to_all.50.x_ref = bf16[8,144,128]{2,1,0:T(8,128)(2,1)S(1)} all-to-all(bf16[8,144,128]{2,1,0:T(8,128)(2,1)S(1)} %shard_map.128), channel_id=1, replica_groups={{0,1,2,3,4,5,6,7},{8,9,10,11,12,13,14,15},{16,17,18,19,20,21,22,23},{24..., dimensions={0} | all-to-all | bytes 589824 | tf_op jit(solution)/shard_map/all_to_all | solution.py:371
  24.5 0.0 copy-start.7
  24.5 1.3 shard_map.129
  25.8 10.6 %all_to_all.51.packed_ref = bf16[8,48,128]{2,1,0:T(8,128)(2,1)S(1)} all-to-all(bf16[8,48,128]{2,1,0:T(8,128)(2,1)S(1)} %shard_map.129), channel_id=1, replica_groups={{0,1,2,3,4,5,6,7},{8,9,10,11,12,13,14,15},{16,17,18,19,20,21,22,23},{24..., dimensions={0} | all-to-all | bytes 196608 | tf_op jit(solution)/shard_map/all_to_all | solution.py:371
  36.4 0.0 copy-done.1
  36.4 0.0 copy-done.2
  36.4 0.0 copy-done.12
  36.4 0.0 copy-done.19
  36.4 0.0 copy-start.15
  36.4 2.3 %shard_map.130 = (bf16[144,512]{1,0:T(8,128)(2,1)S(1)}, bf16[8,144,128]{2,1,0:T(8,128)(2,1)}) custom-call(f32[2,8]{1,0:T(2,128)S(1)} %copy-done.14, bf16[8,48,128]{2,1,0:T(8,128)(2,1)S(1)} %all_to_all.51.packed_ref, bf16[144,512]{1,0:T(8,128)(2,1)S(1)} %bitcast.10, bf16[2,256,512]{2,1,0:T(8,128)(2,1)S(1)} %copy-done.2, f32[2,512]{1,0:T(2,128)S(1)} %copy-done.12, ...), custom_call_target="tpu_custom_call" | custom-call | tf_op jit(solution)/shard_map/pallas_call | solution.py:348
  38.8 0.0 copy-start.8
  38.8 0.7 copy-done.8
  39.4 9.7 %all-to-all-start.2 = ((bf16[8,144,128]{2,1,0:T(8,128)(2,1)}), bf16[8,144,128]{2,1,0:T(8,128)(2,1)S(1)}, u32[]{:S(2)}, u32[]{:S(2)}) async-start(bf16[8,144,128]{2,1,0:T(8,128)(2,1)} %get-tuple-element.21), calls=%async_computation.2 | async-start | bytes 589824 | tf_op jit(solution)/shard_map/all_to_all | solution.py:371
  49.1 4.6 %all-to-all-done.2.x_ref = bf16[8,144,128]{2,1,0:T(8,128)(2,1)S(1)} async-done(((bf16[8,144,128]{2,1,0:T(8,128)(2,1)}), bf16[8,144,128]{2,1,0:T(8,128)(2,1)S(1)}, u32[]{:S(2)}, u32[]{:S(2)}) %all-to-all-start.2) | async-done | bytes 294944 | tf_op jit(solution)/shard_map/all_to_all | solution.py:371
  53.7 0.0 copy-done.20
  53.7 0.0 copy-done.21
  53.7 1.9 shard_map.131
  55.6 12.5 %all_to_all.52.packed_ref = bf16[8,48,128]{2,1,0:T(8,128)(2,1)S(1)} all-to-all(bf16[8,48,128]{2,1,0:T(8,128)(2,1)S(1)} %shard_map.131), channel_id=1, replica_groups={{4,5,6,7,8,9,10,11},{12,13,14,15,16,17,18,19},{20,21,22,23,24,25,26,27}..., dimensions={0} | all-to-all | bytes 196608 | tf_op jit(solution)/shard_map/all_to_all | solution.py:371
  68.1 0.0 copy-done.7
  68.1 1.4 shard_map.132
  69.5 0.6 copy-done.17
  70.1 10.9 %all-to-all-start.4 = ((bf16[8,48,128]{2,1,0:T(8,128)(2,1)}), bf16[8,48,128]{2,1,0:T(8,128)(2,1)S(1)}, u32[]{:S(2)}, u32[]{:S(2)}) async-start(bf16[8,48,128]{2,1,0:T(8,128)(2,1)} %get-tuple-element.22), calls=%async_computation.4 | async-start | bytes 196608 | tf_op jit(solution)/shard_map/all_to_all | solution.py:371
  81.0 2.5 %all-to-all-done.4.grad_ref = bf16[8,48,128]{2,1,0:T(8,128)(2,1)S(1)} async-done(((bf16[8,48,128]{2,1,0:T(8,128)(2,1)}), bf16[8,48,128]{2,1,0:T(8,128)(2,1)S(1)}, u32[]{:S(2)}, u32[]{:S(2)}) %all-to-all-start.4) | async-done | bytes 98336 | tf_op jit(solution)/shard_map/all_to_all | solution.py:371
  83.4 0.0 copy-done.15
  83.4 4.2 %shard_map.133 = bf16[8,144,128]{2,1,0:T(8,128)(2,1)S(1)} custom-call(s32[1]{0:T(128)} %bitcast.2.head_ref, f32[2,8]{1,0:T(2,128)S(1)} %copy-done.15, bf16[8,144,128]{2,1,0:T(8,128)(2,1)S(1)} %all-to-all-done.2.x_ref, bf16[8,48,128]{2,1,0:T(8,128)(2,1)S(1)} %all-to-all-done.4.grad_ref, s32[1]{0:T(128)} %bitcast.3.refs_0_, s32[1,192]{1,0:T(1,128)S(1)} %bitcast.15, ...), custom_call_target="tpu_custom_call" | custom-call | tf_op jit(solution)/shard_map/pallas_call | solution.py:348
  87.7 14.8 %all_to_all.53.qkv_ref = bf16[8,144,128]{2,1,0:T(8,128)(2,1)S(1)} all-to-all(bf16[8,144,128]{2,1,0:T(8,128)(2,1)S(1)} %shard_map.133), channel_id=1, replica_groups={{4,5,6,7,8,9,10,11},{12,13,14,15,16,17,18,19},{20,21,22,23,24,25,26,27}..., dimensions={0} | all-to-all | bytes 589824 | tf_op jit(solution)/shard_map/all_to_all | solution.py:371
  102.5 0.9 copy-done.9
  103.4 0.7 copy-done.13
  104.1 1.8 shard_map.134
  105.9 0.9 copy-done.5
  106.8 0.7 copy-done.10
  107.4 3.8 %all-to-all-start.6 = ((bf16[8,48,128]{2,1,0:T(8,128)(2,1)}), bf16[8,48,128]{2,1,0:T(8,128)(2,1)S(1)}, u32[]{:S(2)}, u32[]{:S(2)}) async-start(bf16[8,48,128]{2,1,0:T(8,128)(2,1)} %get-tuple-element.24), calls=%async_computation.6 | async-start | bytes 196608 | tf_op jit(solution)/shard_map/all_to_all | solution.py:371
  111.2 7.6 %all-to-all-done.6.grad_ref = bf16[8,48,128]{2,1,0:T(8,128)(2,1)S(1)} async-done(((bf16[8,48,128]{2,1,0:T(8,128)(2,1)}), bf16[8,48,128]{2,1,0:T(8,128)(2,1)S(1)}, u32[]{:S(2)}, u32[]{:S(2)}) %all-to-all-start.6) | async-done | bytes 98336 | tf_op jit(solution)/shard_map/all_to_all | solution.py:371
  118.8 0.7 copy-done.16
  119.4 3.7 %shard_map.135 = bf16[8,144,128]{2,1,0:T(8,128)(2,1)S(1)} custom-call(s32[1]{0:T(128)} %bitcast.head_ref, f32[2,8]{1,0:T(2,128)S(1)} %copy-done.16, bf16[8,144,128]{2,1,0:T(8,128)(2,1)S(1)} %all_to_all.50.x_ref, bf16[8,48,128]{2,1,0:T(8,128)(2,1)S(1)} %all-to-all-done.6.grad_ref), custom_call_target="tpu_custom_call" | custom-call | tf_op jit(solution)/shard_map/pallas_call | solution.py:348
  123.1 12.1 %all_to_all.54.qkv_ref = bf16[8,144,128]{2,1,0:T(8,128)(2,1)S(1)} all-to-all(bf16[8,144,128]{2,1,0:T(8,128)(2,1)S(1)} %shard_map.135), channel_id=1, replica_groups={{0,1,2,3,4,5,6,7},{8,9,10,11,12,13,14,15},{16,17,18,19,20,21,22,23},{24..., dimensions={0} | all-to-all | bytes 589824 | tf_op jit(solution)/shard_map/all_to_all | solution.py:371
  135.2 0.0 copy-done.4
  135.2 0.0 copy-done.18
  135.2 1.1 copy-done.6
  136.3 0.9 copy-done.11
  137.2 1.3 shard_map.136
  138.6 24.9 %all_to_all.55.parts_ref = bf16[8,64,2176]{2,1,0:T(8,128)(2,1)S(1)} all-to-all(bf16[8,64,2176]{2,1,0:T(8,128)(2,1)S(1)} %get-tuple-element.32), channel_id=1, replica_groups={{0,8,16,24,32,40,48,56},{1,9,17,25,33,41,49,57},{2,10,18,26,34,42,50,58..., dimensions={0} | all-to-all | bytes 4456448 | tf_op jit(solution)/shard_map/all_to_all | solution.py:371
  163.4 0.3 shard_map.137
  163.7 12.1 %all_to_all.56.parts_ref = bf16[8,16,1152]{2,1,0:T(8,128)(2,1)S(1)} all-to-all(bf16[8,16,1152]{2,1,0:T(8,128)(2,1)S(1)} %shard_map.137), channel_id=1, replica_groups={{0,1,2,3,4,5,6,7},{8,9,10,11,12,13,14,15},{16,17,18,19,20,21,22,23},{24..., dimensions={0} | all-to-all | bytes 589824 | tf_op jit(solution)/shard_map/all_to_all | solution.py:371
  175.8 14.7 %collective-permute-start.2 = (f32[16,1152]{1,0:T(8,128)S(1)}, f32[16,1152]{1,0:T(8,128)S(1)}, u32[]{:S(2)}, u32[]{:S(2)}) collective-permute-start(f32[16,1152]{1,0:T(8,128)S(1)} %shard_map.138.a_ref), channel_id=1, source_target_pairs={{0,192},{64,128},{128,64},{192,0},{1,193},{65,129},{129,65},{193,1... | collective-permute-start | bytes 221192 | tf_op jit(solution)/shard_map/ppermute | solution.py:416
  190.6 0.5 collective-permute-start.1
  191.1 0.0 collective-permute-start
  191.1 2.4 %collective-permute-done.2.d_ref = f32[16,1152]{1,0:T(8,128)S(1)} collective-permute-done((f32[16,1152]{1,0:T(8,128)S(1)}, f32[16,1152]{1,0:T(8,128)S(1)}, u32[]{:S(2)}, u32[]{:S(2)}) %collective-permute-start.2) | collective-permute-done | bytes 73760 | tf_op jit(solution)/shard_map/ppermute | solution.py:416
  193.5 1.8 collective-permute-done.1.c_ref
  195.3 0.0 collective-permute-done.b_ref
  195.3 0.6 shard_map.139
  (11 shorter events, 0.1 us)
Async XLA Ops:
  0.6 1.4 copy-start
  2.0 0.9 copy-start.3
  3.0 0.7 copy-start.14
  3.6 32.8 %copy-start.1 = (bf16[2,512,768]{2,1,0:T(8,128)(2,1)S(1)}, bf16[2,512,768]{2,1,0:T(8,128)(2,1)}, u32[]{:S(2)}) copy-start(bf16[2,512,768]{2,1,0:T(8,128)(2,1)} %w_ref.7) | copy-start | bytes 4718596
  3.6 32.8 %copy-start.2 = (bf16[2,256,512]{2,1,0:T(8,128)(2,1)S(1)}, bf16[2,256,512]{2,1,0:T(8,128)(2,1)}, u32[]{:S(2)}) copy-start(bf16[2,256,512]{2,1,0:T(8,128)(2,1)} %w_proj_ref.5) | copy-start | bytes 1572868
  3.6 32.8 %copy-start.12 = (f32[2,512]{1,0:T(2,128)S(1)}, f32[2,512]{1,0:T(2,128)}, u32[]{:S(2)}) copy-start(f32[2,512]{1,0:T(2,128)} %gain_ref.5) | copy-start | bytes 12292
  3.6 32.8 %copy-start.19 = (f32[2,512]{1,0:T(2,128)S(1)}, f32[2,512]{1,0:T(2,128)}, u32[]{:S(2)}) copy-start(f32[2,512]{1,0:T(2,128)} %bias_ref.1) | copy-start | bytes 12292
  4.8 48.9 %copy-start.20 = (s32[192]{0:T(256)S(1)}, s32[192]{0:T(256)}, u32[]{:S(2)}) copy-start(s32[192]{0:T(256)} %param.16) | copy-start | bytes 2308
  4.8 48.9 %copy-start.21 = (s32[48]{0:T(128)S(1)}, s32[48]{0:T(128)}, u32[]{:S(2)}) copy-start(s32[48]{0:T(128)} %param.17) | copy-start | bytes 580
  24.5 43.6 %copy-start.7 = (bf16[1,3,48,512]{3,2,1,0:T(8,128)(2,1)S(1)}, bf16[1,3,48,512]{3,2,1,0:T(8,128)(2,1)}, u32[]{:S(2)}) copy-start(bf16[1,3,48,512]{3,2,1,0:T(8,128)(2,1)} %param.10) | copy-start | bytes 442372
  36.4 47.0 %copy-start.15 = (f32[2,8]{1,0:T(2,128)S(1)}, f32[2,8]{1,0:T(2,128)}, u32[]{:S(2)}) copy-start(f32[2,8]{1,0:T(2,128)} %scale_ref.7) | copy-start | bytes 196
  38.8 0.7 copy-start.8
  39.4 14.3 %all-to-all-start.2 = ((bf16[8,144,128]{2,1,0:T(8,128)(2,1)}), bf16[8,144,128]{2,1,0:T(8,128)(2,1)S(1)}, u32[]{:S(2)}, u32[]{:S(2)}) async-start(bf16[8,144,128]{2,1,0:T(8,128)(2,1)} %get-tuple-element.21), calls=%async_computation.2 | async-start | bytes 589824 | tf_op jit(solution)/shard_map/all_to_all | solution.py:371
  69.5 0.6 copy-start.17
  70.1 13.3 %all-to-all-start.4 = ((bf16[8,48,128]{2,1,0:T(8,128)(2,1)}), bf16[8,48,128]{2,1,0:T(8,128)(2,1)S(1)}, u32[]{:S(2)}, u32[]{:S(2)}) async-start(bf16[8,48,128]{2,1,0:T(8,128)(2,1)} %get-tuple-element.22), calls=%async_computation.4 | async-start | bytes 196608 | tf_op jit(solution)/shard_map/all_to_all | solution.py:371
  102.5 32.7 %copy-start.4 = (bf16[1,3,48,512]{3,2,1,0:T(8,128)(2,1)S(1)}, bf16[1,3,48,512]{3,2,1,0:T(8,128)(2,1)}, u32[]{:S(2)}) copy-start(bf16[1,3,48,512]{3,2,1,0:T(8,128)(2,1)} %param.9) | copy-start | bytes 442372
  102.5 0.9 copy-start.9
  103.4 0.7 copy-start.13
  104.1 31.1 %copy-start.18 = (f32[8,512]{1,0:T(8,128)S(1)}, f32[8,512]{1,0:T(8,128)}, u32[]{:S(2)}) copy-start(f32[8,512]{1,0:T(8,128)} %copy-done.17) | copy-start | bytes 49156
  105.9 0.9 copy-start.5
  106.8 0.7 copy-start.10
  107.4 11.3 %all-to-all-start.6 = ((bf16[8,48,128]{2,1,0:T(8,128)(2,1)}), bf16[8,48,128]{2,1,0:T(8,128)(2,1)S(1)}, u32[]{:S(2)}, u32[]{:S(2)}) async-start(bf16[8,48,128]{2,1,0:T(8,128)(2,1)} %get-tuple-element.24), calls=%async_computation.6 | async-start | bytes 196608 | tf_op jit(solution)/shard_map/all_to_all | solution.py:371
  118.8 0.7 copy-start.16
  135.2 1.1 copy-start.6
  136.3 0.9 copy-start.11
  175.8 17.6 %collective-permute-start.2 = (f32[16,1152]{1,0:T(8,128)S(1)}, f32[16,1152]{1,0:T(8,128)S(1)}, u32[]{:S(2)}, u32[]{:S(2)}) collective-permute-start(f32[16,1152]{1,0:T(8,128)S(1)} %shard_map.138.a_ref), channel_id=1, source_target_pairs={{0,192},{64,128},{128,64},{192,0},{1,193},{65,129},{129,65},{193,1... | collective-permute-start | bytes 221192 | tf_op jit(solution)/shard_map/ppermute | solution.py:416
  190.6 4.7 %collective-permute-start.1 = (f32[16,1152]{1,0:T(8,128)S(1)}, f32[16,1152]{1,0:T(8,128)S(1)}, u32[]{:S(2)}, u32[]{:S(2)}) collective-permute-start(f32[16,1152]{1,0:T(8,128)S(1)} %shard_map.138.a_ref), channel_id=1, source_target_pairs={{0,128},{64,192},{128,0},{192,64},{1,129},{65,193},{129,1},{193,65... | collective-permute-start | bytes 221192 | tf_op jit(solution)/shard_map/ppermute | solution.py:416
  191.1 4.2 %collective-permute-start = (f32[16,1152]{1,0:T(8,128)S(1)}, f32[16,1152]{1,0:T(8,128)S(1)}, u32[]{:S(2)}, u32[]{:S(2)}) collective-permute-start(f32[16,1152]{1,0:T(8,128)S(1)} %shard_map.138.a_ref), channel_id=1, source_target_pairs={{0,64},{64,0},{128,192},{192,128},{1,65},{65,1},{129,193},{193,129... | collective-permute-start | bytes 221192 | tf_op jit(solution)/shard_map/ppermute | solution.py:416

commit v3 on v2

--- a/solution.py
+++ b/solution.py
@@ -19,8 +19,9 @@
 ROWS_DEV = 3
 PACK = 48
 DEVS = 64
-SENT = 2 * 3 * HH + 2 * HH + 128
-HALF = 1152
+VMEM_LIMIT = 24 * 2**20
+EARLY = 3 * HH + 2 * HH
+TILES = (3 * HH + EARLY // 2 + 128) // 128
 
 norm_eps = 1e-05
 mask_value = 100.0
@@ -237,22 +238,22 @@
 
 
 def first_kernel(scale_ref, tokens_ref, w_ref, out_ref):
-    send_projected(tokens_ref[...], w_ref[0], scale_ref, 0, out_ref)
-
-
-def middle_kernel(scale_ref, packed_ref, tokens_ref, w_proj_ref, gain_ref, bias_ref, w_ref, rolled_ref, out_ref):
+    send_projected(tokens_ref[...], w_ref[...], scale_ref, 0, out_ref)
+
+
+def middle_kernel(scale_ref, packed_ref, gain_ref, bias_ref, tokens_ref, w_proj_ref, w_ref, out_ref, rolled_ref):
     attended = unpack_heads(packed_ref)
-    y_hat, _ = normalized(attended, w_proj_ref[0])
+    y_hat, _ = normalized(attended, w_proj_ref[...])
     out = (tokens_ref[...].astype(f32) + y_hat * gain_ref[0:1] + bias_ref[0:1]).astype(bf16).astype(f32)
     rolled = roll_tokens(out, -SHIFT).astype(bf16)
     rolled_ref[...] = rolled
-    send_projected(rolled, w_ref[1], scale_ref, 1, out_ref)
-
-
-def turn_kernel(packed_ref, grad_ref, w_proj_ref, gain_ref, out_ref, grad_proj_ref, gains_ref):
+    send_projected(rolled, w_ref[...], scale_ref, 1, out_ref)
+
+
+def turn_kernel(packed_ref, gain_ref, grad_ref, w_proj_ref, out_ref, grad_proj_ref, gains_ref):
     attended = unpack_heads(packed_ref)
     grad = roll_tokens(grad_ref[...].astype(f32), -SHIFT)
-    grad_y, grad_att, gains = finish_back(attended, w_proj_ref[1], gain_ref[1:2], grad)
+    grad_y, grad_att, gains = finish_back(attended, w_proj_ref[...], gain_ref[1:2], grad)
     pack_heads(grad_att, out_ref)
     grad_proj_ref[...] = dot_0(grad_y, attended).astype(bf16)
     gains_ref[...] = gains
@@ -265,93 +266,158 @@
     ).astype(bf16)
 
 
+def give(array, side, kept_ref, given_ref):
+    half = array.shape[1] // 2
+    left, right = array[:, :half], array[:, half:]
+    kept_ref[...] = jnp.where(side == 0, left, right).astype(bf16)
+    given_ref[...] = jnp.where(side == 0, right, left).astype(bf16)
+
+
 def back_kernel(
+    core_ref,
     qkv_ref,
+    packed_ref,
+    gain_ref,
     w_ref,
+    w_proj_ref,
+    grad_ref,
+    proj1_ref,
     tokens_ref,
-    grad_ref,
-    packed_ref,
-    w_proj_ref,
-    gain_ref,
     out_ref,
+    gains_ref,
     grad0_ref,
-    grad_qkv_ref,
-    grad_proj_ref,
-    gains_ref,
+    kept_ref,
+    given_ref,
 ):
     d_qkv = gather_qkv(qkv_ref)
-    from_qkv = roll_tokens(dot_t(d_qkv, w_ref[1]), SHIFT)
+    from_qkv = roll_tokens(dot_t(d_qkv, w_ref[...]), SHIFT)
     grad = (grad_ref[...].astype(f32) + from_qkv).astype(bf16)
     grad0_ref[...] = grad
     attended = unpack_heads(packed_ref)
-    grad_y, grad_att, gains = finish_back(attended, w_proj_ref[0], gain_ref[0:1], grad.astype(f32))
+    grad_y, grad_att, gains = finish_back(attended, w_proj_ref[...], gain_ref[0:1], grad.astype(f32))
     pack_heads(grad_att, out_ref)
-    grad_qkv_ref[...] = dot_0(tokens_ref[...], d_qkv).astype(bf16)
-    grad_proj_ref[...] = dot_0(grad_y, attended).astype(bf16)
+    parts = [dot_0(tokens_ref[...], d_qkv), proj1_ref[...].astype(f32), dot_0(grad_y, attended)]
+    early = jnp.concatenate(parts, 1)
+    give(early, core_ref[0], kept_ref, given_ref)
     gains_ref[...] = gains
 
 
 def last_kernel(
-    qkv_ref,
-    w_ref,
-    tokens_ref,
-    grad_ref,
-    grad_qkv1_ref,
-    proj0_ref,
-    proj1_ref,
-    gains0_ref,
-    gains1_ref,
-    out_ref,
-    parts_ref,
+    qkv_ref, w_ref, tokens_ref, got_ref, gains0_ref, gains1_ref, grad_ref, kept_ref, parts_ref, out_ref
 ):
     d_qkv = gather_qkv(qkv_ref)
-    out_ref[...] = (grad_ref[...].astype(f32) + dot_t(d_qkv, w_ref[0])).astype(bf16)
+    out_ref[...] = (grad_ref[...].astype(f32) + dot_t(d_qkv, w_ref[...])).astype(bf16)
     pieces = []
     for ref in (gains0_ref, gains1_ref):
         for row in (0, 1):
             pieces += split_two(ref[row : row + 1])
     pieces.append(jnp.zeros((128 - len(pieces), C), f32))
     gains = jnp.concatenate(pieces, 0).T
-    at = 0
-    for part in (dot_0(tokens_ref[...], d_qkv), grad_qkv1_ref[...], proj0_ref[...], proj1_ref[...], gains):
-        width = part.shape[1]
-        parts_ref[:, :, at : at + width] = part.astype(bf16).reshape(8, C // 8, width)
-        at += width
+    early = kept_ref[...].astype(f32) + got_ref[...].astype(f32)
+    tile = 0
+    for part in (dot_0(tokens_ref[...], d_qkv), early, gains):
+        for at in range(0, part.shape[1], 128):
+            block = part[:, at : at + 128].astype(bf16).reshape(8, C // 8, 128)
+            parts_ref[:, tile * (C // 8) : (tile + 1) * (C // 8), :] = block
+            tile += 1
 
 
 def first_sum_kernel(parts_ref, out_ref):
-    total = jnp.sum(parts_ref[...].astype(f32), 0).reshape(8, 8, SENT)
-    right = jnp.concatenate([total[:, :, HALF:], jnp.zeros((8, 8, 2 * HALF - SENT), f32)], 2)
-    out_ref[...] = jnp.concatenate([total[:, :, :HALF], right], 1).astype(bf16)
+    total = jnp.sum(parts_ref[...].astype(f32), 0).reshape(TILES, 8, 8, 128)
+    for ring in range(8):
+        out_ref[ring] = total[:, ring].reshape(TILES * 8, 128).astype(bf16)
 
 
 def second_sum_kernel(parts_ref, out_ref):
     out_ref[...] = jnp.sum(parts_ref[...].astype(f32), 0)
 
 
-def final_kernel(a_ref, b_ref, c_ref, d_ref, qkv_ref, proj_ref, gain_ref, bias_ref):
-    total = (a_ref[...] + b_ref[...]) + (c_ref[...] + d_ref[...])
-    total = jnp.concatenate([total[:8], total[8:]], 1)
-    qkv_ref[0] = total[:, :768]
-    qkv_ref[1] = total[:, 768:1536]
-    proj_ref[0] = total[:, 1536:1792]
-    proj_ref[1] = total[:, 1792:2048]
-    gains = total[:, 2048:2176].T
+def final_kernel(core_ref, own_ref, core1_ref, chip_ref, chip1_ref, qkv_ref, proj_ref, gain_ref, bias_ref):
+    same = own_ref[...] + chip_ref[...]
+    other = core1_ref[...] + chip1_ref[...]
+    both = (same + other).reshape(TILES, 8, 128)
+    first = core_ref[0] == 0
+    left = jnp.where(first, same, other).reshape(TILES, 8, 128)
+    right = jnp.where(first, other, same).reshape(TILES, 8, 128)
+    tiles = [left[i] for i in range(6, 11)] + [right[i] for i in range(6, 11)]
+    qkv_ref[0] = jnp.concatenate([both[i] for i in range(6)], 1)
+    qkv_ref[1] = jnp.concatenate(tiles[:6], 1)
+    proj_ref[1] = jnp.concatenate(tiles[6:8], 1)
+    proj_ref[0] = jnp.concatenate(tiles[8:], 1)
+    gains = both[11].T
     gain_ref[...] = jnp.concatenate([gains[0:1] + gains[1:2], gains[4:5] + gains[5:6]], 0)
     bias_ref[...] = jnp.concatenate([gains[2:3] + gains[3:4], gains[6:7] + gains[7:8]], 0)
 
 
-def call(kernel, outs, scalars, arrays, masks=()):
+class Fetched:
+    def __init__(self, source, ref, sem):
+        self.ref, self.copy = ref, pltpu.make_async_copy(source, ref, sem)
+        self.copy.start()
+        self.waited = False
+
+    def __getitem__(self, at):
+        if not self.waited:
+            self.copy.wait()
+            self.waited = True
+        return self.ref[at]
+
+
+class Stored:
+    def __init__(self, ref, target, sem):
+        self.ref, self.copy = ref, pltpu.make_async_copy(ref, target, sem)
+
+    def __setitem__(self, at, value):
+        self.ref[at] = value
+        self.copy.start()
+
+
+def call(kernel, outs, scalars, arrays, masks=(), fetched=(), stored=()):
+    arrays = [item if isinstance(item, tuple) else (item, None) for item in arrays]
+    fetched = [item if isinstance(item, tuple) else (item, None) for item in fetched]
+    counts = [len(scalars), len(arrays), len(fetched), len(masks), len(outs), len(stored), len(fetched), len(stored)]
+
+    def wrapped(*refs):
+        parts, at = [], 0
+        for count in counts:
+            parts.append(refs[at : at + count])
+            at += count
+        scalar_refs, array_refs, sources, mask_refs, out_refs, targets, filled, sent = parts
+        sems = refs[-1]
+        near = [ref if block is None else ref.at[block] for ref, (_, block) in zip(array_refs, arrays)]
+        far = []
+        for i, (_, block) in enumerate(fetched):
+            source = sources[i] if block is None else sources[i].at[block]
+            far.append(Fetched(source, filled[i], sems.at[i]))
+        results = [Stored(sent[i], targets[i], sems.at[len(fetched) + i]) for i in range(len(stored))]
+        kernel(*scalar_refs, *near, *far, *mask_refs, *out_refs, *results)
+        for result in results:
+            result.copy.wait()
+
     smem = pl.BlockSpec(memory_space=pltpu.SMEM)
     vmem = pl.BlockSpec(memory_space=pltpu.VMEM)
-    specs = [smem] * len(scalars) + [vmem] * len(arrays) + [smem, vmem, vmem][: len(masks)]
+    hbm = pl.BlockSpec(memory_space=pltpu.HBM)
+    scratch = [
+        pltpu.VMEM(array.shape if block is None else array.shape[1:], array.dtype) for array, block in fetched
+    ]
+    scratch += [pltpu.VMEM(*out) for out in stored]
+    if scratch:
+        scratch.append(pltpu.SemaphoreType.DMA((len(scratch),)))
     return pl.pallas_call(
-        kernel,
-        out_shape=[jax.ShapeDtypeStruct(shape, dtype) for shape, dtype in outs],
-        in_specs=specs,
-        out_specs=[vmem] * len(outs),
-        compiler_params=pltpu.CompilerParams(vmem_limit_bytes=24 * 2**20),
-    )(*scalars, *arrays, *masks)
+        wrapped,
+        out_shape=[jax.ShapeDtypeStruct(*out) for out in outs] + [pltpu.HBM(*out) for out in stored],
+        in_specs=[smem] * len(scalars)
+        + [vmem] * len(arrays)
+        + [hbm] * len(fetched)
+        + [smem, vmem, vmem][: len(masks)],
+        out_specs=[vmem] * len(outs) + [hbm] * len(stored),
+        scratch_shapes=scratch,
+        compiler_params=pltpu.CompilerParams(vmem_limit_bytes=VMEM_LIMIT),
+    )(
+        *scalars,
+        *(array for array, _ in arrays),
+        *(pltpu.with_memory_space_constraint(array, pltpu.HBM) for array, _ in fetched),
+        *masks,
+    )
 
 
 def body(image, out_grad, w_qkv, w_proj, norm_gain, norm_bias, logit_scale, row_band, col_band):
@@ -359,12 +425,14 @@
     half = GROUP // 2
     rings = range(DEVS // GROUP)
     aligned = [[GROUP * g + i for i in range(GROUP)] for g in rings]
+    across = [[GROUP * g + i for g in rings] for i in range(GROUP)]
     moved = [[(GROUP * g + half + i) % DEVS for i in range(GROUP)] for g in rings]
-    across = [[GROUP * g + i for g in rings] for i in range(GROUP)]
     moved_position = (position + DEVS - half) % DEVS
     head0 = (position % GROUP).reshape(1)
     head1 = (moved_position % GROUP).reshape(1)
     first_row = (moved_position // GROUP * WIN).reshape(1)
+    core = (lax.axis_index("dp") % 2).reshape(1)
+    image, head0, head1, first_row, core = lax.optimization_barrier((image, head0, head1, first_row, core))
     masks = (first_row, row_band.reshape(1, -1), col_band.reshape(1, -1))
 
     def exchange(array, groups):
@@ -377,46 +445,62 @@
     cells = ((TOK, C), bf16)
     proj = ((C, HH), bf16)
     gains = ((8, C), f32)
-
-    (x0,) = call(first_kernel, [wide], (logit_scale,), (tokens0, w_qkv))
+    half_early = ((C, EARLY // 2), bf16)
+
+    def swap(array, apart):
+        return lax.ppermute(array, "dp", [(i, i ^ apart) for i in range(4)])
+
+    (x0,) = call(first_kernel, [wide], (logit_scale,), (), fetched=(tokens0, (w_qkv, 0)))
     x0 = exchange(x0, aligned)
     (a0,) = call(functools.partial(attend_kernel, False), [narrow], (), (x0,))
     a0 = exchange(a0, aligned)
-    tokens1, x1 = call(
-        middle_kernel, [cells, wide], (logit_scale,), (a0, tokens0, w_proj, norm_gain, norm_bias, w_qkv)
+    x1, tokens1 = call(
+        middle_kernel,
+        [wide],
+        (logit_scale,),
+        (a0, norm_gain, norm_bias, tokens0, (w_proj, 0), (w_qkv, 1)),
+        stored=[cells],
     )
     x1 = exchange(x1, moved)
     (a1,) = call(functools.partial(attend_kernel, True), [narrow], (), (x1,), masks)
     a1 = exchange(a1, moved)
-    d1, proj1, gains1 = call(turn_kernel, [narrow, proj, gains], (), (a1, grad_out, w_proj, norm_gain))
+    d1, proj1, gains1 = call(
+        turn_kernel, [narrow, proj, gains], (), (a1, norm_gain, grad_out, (w_proj, 1))
+    )
     d1 = exchange(d1, moved)
     (qkv1,) = call(
         functools.partial(attend_back_kernel, 1, True), [wide], (head1, logit_scale), (x1, d1), masks
     )
     qkv1 = exchange(qkv1, moved)
-    d0, grad0, grad_qkv1, proj0, gains0 = call(
+    d0, gains0, grad0, kept, given = call(
         back_kernel,
-        [narrow, cells, ((C, 3 * HH), bf16), proj, gains],
-        (),
-        (qkv1, w_qkv, tokens1, grad_out, a0, w_proj, norm_gain),
-    )
+        [narrow, gains],
+        (core,),
+        (qkv1, a0, norm_gain, (w_qkv, 1), (w_proj, 0), grad_out, proj1),
+        fetched=(tokens1,),
+        stored=[cells, half_early, half_early],
+    )
+    d0, got = lax.optimization_barrier((d0, swap(given, 1)))
     d0 = exchange(d0, aligned)
     (qkv0,) = call(functools.partial(attend_back_kernel, 0, False), [wide], (head0, logit_scale), (x0, d0))
     qkv0 = exchange(qkv0, aligned)
-    grad_image, parts = call(
+    parts, grad_image = call(
         last_kernel,
-        [cells, ((8, C // 8, SENT), bf16)],
+        [((8, TILES * C // 8, 128), bf16), cells],
         (),
-        (qkv0, w_qkv, tokens0, grad0, grad_qkv1, proj0, proj1, gains0, gains1),
+        (qkv0, (w_qkv, 0), tokens0, got, gains0, gains1),
+        fetched=(grad0, kept),
     )
     parts = exchange(parts, across)
-    (parts,) = call(first_sum_kernel, [((8, 16, HALF), bf16)], (), (parts,))
+    (parts,) = call(first_sum_kernel, [((8, TILES * 8, 128), bf16)], (), (parts,))
     parts = exchange(parts, aligned)
-    (share,) = call(second_sum_kernel, [((16, HALF), f32)], (), (parts,))
-    others = [lax.ppermute(share, "dp", [(i, i ^ k) for i in range(4)]) for k in (1, 2, 3)]
+    (share,) = call(second_sum_kernel, [((TILES * 8, 128), f32)], (), (parts,))
     small = ((2, 8), f32)
     grad_qkv, grad_proj, grad_gain, grad_bias = call(
-        final_kernel, [((2, 8, 3 * HH), f32), ((2, 8, HH), f32), small, small], (), (share, *others)
+        final_kernel,
+        [((2, 8, 3 * HH), f32), ((2, 8, HH), f32), small, small],
+        (core,),
+        (share, swap(share, 1), swap(share, 2), swap(share, 3)),
     )
     return (
         grad_image.reshape(image.shape),

time: 197 us -> 191 us (0.970)
  blocking collectives: 107 us -> 144 us
  starting transfers between devices: 39.5 us -> 15.8 us
  waiting for transfers between devices: 18.9 us -> 5.89 us
  local copies, waits for them, and re-layouts: 10.2 us -> 0.7 us
  Pallas kernels: 20.1 us -> 23.2 us
    all_to_all x7 -> x10, blocking collectives: 107 us -> 144 us  [exchange(): lax.all_to_all(array, 'rows', 0, 0, axis_index_groups=groups, tiled=True)]
    all_to_all x3 -> x0, starting transfers between devices: 24.3 us -> none  [exchange(): lax.all_to_all(array, 'rows', 0, 0, axis_index_groups=groups, tiled=True)]
    all_to_all x3 -> x0, waiting for transfers between devices: 14.7 us -> none  [exchange(): lax.all_to_all(array, 'rows', 0, 0, axis_index_groups=groups, tiled=True)]
    unnamed x44 -> x18, local copies, waits for them, and re-layouts: 10.2 us -> 0.7 us
    pallas_call x12, Pallas kernels: 20.1 us -> 23.2 us  [call(): pl.pallas_call(wrapped, out_shape=[jax.ShapeDtypeStruct(*out) for out in...]
    ppermute x3 -> x4, waiting for transfers between devices: 4.2 us -> 5.89 us  [swap(): return lax.ppermute(array, 'dp', [(i, i ^ apart) for i in range(4)])]
    ppermute x3 -> x4, starting transfers between devices: 15.2 us -> 15.8 us  [swap(): return lax.ppermute(array, 'dp', [(i, i ^ apart) for i in range(4)])]
  transfers between devices with their start and end apart: 6 -> 4, of which waited for: 5 -> 3; matrix products, arithmetic and copies ran while one was open for 0% -> 0% of each run, Pallas kernels for 0% -> 0%
where the time goes in v3:
time: 191 us
  blocking collectives  144 us (75%)
  Pallas kernels  23.2 us (12%)
  starting transfers between devices  15.8 us (8%)
  waiting for transfers between devices  5.89 us (3%)
    all_to_all x10, blocking collectives, exchange(): lax.all_to_all(array, 'rows', 0, 0, axis_index_groups=groups, tiled=True)  144 us
    pallas_call x12, Pallas kernels, call(): pl.pallas_call(wrapped, out_shape=[jax.ShapeDtypeStruct(*out) for out in...  23.2 us
    ppermute x4, starting transfers between devices, swap(): return lax.ppermute(array, 'dp', [(i, i ^ apart) for i in range(4)])  15.8 us
    ppermute x4, waiting for transfers between devices, swap(): return lax.ppermute(array, 'dp', [(i, i ^ apart) for i in range(4)])  5.89 us
  transfers between devices with their start and end apart: 4, of which 3 were waited for; matrix products, arithmetic and copies ran while one was open for 0% of the time, Pallas kernels for 0%

profile of v3, /device:TPU:1, one launch (start us, length us, event | category | flops | bytes accessed | tf_op | source)
XLA Modules:
  0.0 190.7 jit_solution(214777990159901616)
XLA Ops:
  0.7 0.0 copy-start.5
  0.7 0.7 copy-done.5
  1.4 0.0 copy-start
  1.4 0.0 copy-start.1
  1.4 0.0 copy-start.2
  1.4 0.0 copy-start.4
  1.4 0.0 copy-start.6
  1.4 2.5 %shard_map.128 = bf16[8,144,128]{2,1,0:T(8,128)(2,1)S(1)} custom-call(f32[2,8]{1,0:T(2,128)S(1)} %copy-done.5, bf16[144,512]{1,0:T(8,128)(2,1)} %bitcast.10, bf16[2,512,768]{2,1,0:T(8,128)(2,1)} %refs_1_.7), custom_call_target="tpu_custom_call" | custom-call | tf_op jit(solution)/shard_map/pallas_call | solution.py:405
  3.9 19.6 %all_to_all.50.refs_0_.refs_2_ = bf16[8,144,128]{2,1,0:T(8,128)(2,1)S(1)} all-to-all(bf16[8,144,128]{2,1,0:T(8,128)(2,1)S(1)} %shard_map.128), channel_id=1, replica_groups={{0,1,2,3,4,5,6,7},{8,9,10,11,12,13,14,15},{16,17,18,19,20,21,22,23},{24..., dimensions={0} | all-to-all | bytes 589824 | tf_op jit(solution)/shard_map/all_to_all | solution.py:439
  23.6 1.3 shard_map.129
  24.8 0.0 copy-start.7
  24.8 0.0 copy-start.8
  24.9 10.8 %all_to_all.51.refs_1_.refs_2_ = bf16[8,48,128]{2,1,0:T(8,128)(2,1)S(1)} all-to-all(bf16[8,48,128]{2,1,0:T(8,128)(2,1)S(1)} %shard_map.129), channel_id=1, replica_groups={{0,1,2,3,4,5,6,7},{8,9,10,11,12,13,14,15},{16,17,18,19,20,21,22,23},{24..., dimensions={0} | all-to-all | bytes 196608 | tf_op jit(solution)/shard_map/all_to_all | solution.py:439
  35.6 0.0 copy-done
  35.6 0.0 copy-done.1
  35.6 0.0 copy-done.2
  35.7 0.0 copy-done.4
  35.7 0.0 copy-done.6
  35.7 0.0 copy-start.3
  35.7 2.2 %shard_map.130 = (bf16[8,144,128]{2,1,0:T(8,128)(2,1)S(1)}, bf16[144,512]{1,0:T(8,128)(2,1)}) custom-call(f32[2,8]{1,0:T(2,128)S(1)} %copy-done.5, bf16[8,48,128]{2,1,0:T(8,128)(2,1)S(1)} %all_to_all.51.refs_1_.refs_2_, f32[2,512]{1,0:T(2,128)S(1)} %copy-done.4, f32[2,512]{1,0:T(2,128)S(1)} %copy-done.6, bf16[144,512]{1,0:T(8,128)(2,1)S(1)} %bitcast.11, ...), custom_call_target="tpu_custom_call" | custom-call | tf_op jit(solution)/shard_map/pallas_call | solution.py:405
  37.9 14.2 %all_to_all.52.refs_0_.refs_2_ = bf16[8,144,128]{2,1,0:T(8,128)(2,1)S(1)} all-to-all(bf16[8,144,128]{2,1,0:T(8,128)(2,1)S(1)} %get-tuple-element.32), channel_id=1, replica_groups={{4,5,6,7,8,9,10,11},{12,13,14,15,16,17,18,19},{20,21,22,23,24,25,26,27}..., dimensions={0} | all-to-all | bytes 589824 | tf_op jit(solution)/shard_map/all_to_all | solution.py:439
  52.1 0.0 copy-done.7
  52.1 0.0 copy-done.8
  52.1 1.9 shard_map.131
  54.0 12.2 %all_to_all.53.refs_0_ = bf16[8,48,128]{2,1,0:T(8,128)(2,1)S(1)} all-to-all(bf16[8,48,128]{2,1,0:T(8,128)(2,1)S(1)} %shard_map.131), channel_id=1, replica_groups={{4,5,6,7,8,9,10,11},{12,13,14,15,16,17,18,19},{20,21,22,23,24,25,26,27}..., dimensions={0} | all-to-all | bytes 196608 | tf_op jit(solution)/shard_map/all_to_all | solution.py:439
  66.2 0.0 copy-done.3
  66.2 0.8 shard_map.132
  67.0 12.4 %all_to_all.54.refs_3_ = bf16[8,48,128]{2,1,0:T(8,128)(2,1)S(1)} all-to-all(bf16[8,48,128]{2,1,0:T(8,128)(2,1)S(1)} %get-tuple-element.34), channel_id=1, replica_groups={{4,5,6,7,8,9,10,11},{12,13,14,15,16,17,18,19},{20,21,22,23,24,25,26,27}..., dimensions={0} | all-to-all | bytes 196608 | tf_op jit(solution)/shard_map/all_to_all | solution.py:439
  79.5 4.2 %shard_map.133 = bf16[8,144,128]{2,1,0:T(8,128)(2,1)S(1)} custom-call(s32[1]{0:T(128)} %bitcast.1.refs_0_, f32[2,8]{1,0:T(2,128)S(1)} %copy-done.5, bf16[8,144,128]{2,1,0:T(8,128)(2,1)S(1)} %all_to_all.52.refs_0_.refs_2_, bf16[8,48,128]{2,1,0:T(8,128)(2,1)S(1)} %all_to_all.54.refs_3_, s32[1]{0:T(128)} %bitcast.2.refs_1_.refs_4_, s32[1,192]{1,0:T(1,128)S(1)} %bitcast.16, ...), custom_call_target="tpu_custom_call" | custom-call | tf_op jit(solution)/shard_map/pallas_call | solution.py:405
  83.7 14.5 %all_to_all.55.refs_1_ = bf16[8,144,128]{2,1,0:T(8,128)(2,1)S(1)} all-to-all(bf16[8,144,128]{2,1,0:T(8,128)(2,1)S(1)} %shard_map.133), channel_id=1, replica_groups={{4,5,6,7,8,9,10,11},{12,13,14,15,16,17,18,19},{20,21,22,23,24,25,26,27}..., dimensions={0} | all-to-all | bytes 589824 | tf_op jit(solution)/shard_map/all_to_all | solution.py:439
  98.2 3.4 %shard_map.134 = (bf16[8,48,128]{2,1,0:T(8,128)(2,1)S(1)}, f32[8,512]{1,0:T(8,128)S(1)}, bf16[144,512]{1,0:T(8,128)(2,1)}, bf16[512,640]{1,0:T(8,128)(2,1)}, bf16[512,640]{1,0:T(8,128)(2,1)}) custom-call(s32[1]{0:T(128)} %bitcast.3.refs_0_, bf16[8,144,128]{2,1,0:T(8,128)(2,1)S(1)} %all_to_all.55.refs_1_, bf16[8,48,128]{2,1,0:T(8,128)(2,1)S(1)} %all_to_all.51.refs_1_.refs_2_, ...), custom_call_target="tpu_custom_call" | custom-call | tf_op jit(solution)/shard_map/pallas_call | solution.py:405
  101.6 7.9 %collective-permute-start = (bf16[512,640]{1,0:T(8,128)(2,1)}, bf16[512,640]{1,0:T(8,128)(2,1)S(1)}, u32[]{:S(2)}, u32[]{:S(2)}) collective-permute-start(bf16[512,640]{1,0:T(8,128)(2,1)} %get-tuple-element.38), channel_id=1, source_target_pairs={{0,64},{64,0},{128,192},{192,128},{1,65},{65,1},{129,193},{193,129... | collective-permute-start | bytes 1966088 | tf_op jit(solution)/shard_map/ppermute | solution.py:451
  109.6 1.9 %collective-permute-done.refs_3_ = bf16[512,640]{1,0:T(8,128)(2,1)S(1)} collective-permute-done((bf16[512,640]{1,0:T(8,128)(2,1)}, bf16[512,640]{1,0:T(8,128)(2,1)S(1)}, u32[]{:S(2)}, u32[]{:S(2)}) %collective-permute-start) | collective-permute-done | bytes 655392 | tf_op jit(solution)/shard_map/ppermute | solution.py:451
  111.5 10.5 %all_to_all.56.refs_3_ = bf16[8,48,128]{2,1,0:T(8,128)(2,1)S(1)} all-to-all(bf16[8,48,128]{2,1,0:T(8,128)(2,1)S(1)} %get-tuple-element.39), channel_id=1, replica_groups={{0,1,2,3,4,5,6,7},{8,9,10,11,12,13,14,15},{16,17,18,19,20,21,22,23},{24..., dimensions={0} | all-to-all | bytes 196608 | tf_op jit(solution)/shard_map/all_to_all | solution.py:439
  122.0 3.7 %shard_map.135 = bf16[8,144,128]{2,1,0:T(8,128)(2,1)S(1)} custom-call(s32[1]{0:T(128)} %bitcast.refs_0_, f32[2,8]{1,0:T(2,128)S(1)} %copy-done.5, bf16[8,144,128]{2,1,0:T(8,128)(2,1)S(1)} %all_to_all.50.refs_0_.refs_2_, bf16[8,48,128]{2,1,0:T(8,128)(2,1)S(1)} %all_to_all.56.refs_3_), custom_call_target="tpu_custom_call" | custom-call | tf_op jit(solution)/shard_map/pallas_call | solution.py:405
  125.7 12.1 %all_to_all.57.refs_0_ = bf16[8,144,128]{2,1,0:T(8,128)(2,1)S(1)} all-to-all(bf16[8,144,128]{2,1,0:T(8,128)(2,1)S(1)} %shard_map.135), channel_id=1, replica_groups={{0,1,2,3,4,5,6,7},{8,9,10,11,12,13,14,15},{16,17,18,19,20,21,22,23},{24..., dimensions={0} | all-to-all | bytes 589824 | tf_op jit(solution)/shard_map/all_to_all | solution.py:439
  137.8 2.3 %shard_map.136 = (bf16[8,768,128]{2,1,0:T(8,128)(2,1)S(1)}, bf16[144,512]{1,0:T(8,128)(2,1)}) custom-call(bf16[8,144,128]{2,1,0:T(8,128)(2,1)S(1)} %all_to_all.57.refs_0_, bf16[2,512,768]{2,1,0:T(8,128)(2,1)S(1)} %copy-done, bf16[144,512]{1,0:T(8,128)(2,1)S(1)} %bitcast.12, bf16[512,640]{1,0:T(8,128)(2,1)S(1)} %collective-permute-done.refs_3_, ...), custom_call_target="tpu_custom_call" | custom-call | tf_op jit(solution)/shard_map/pallas_call | solution.py:405
  140.1 23.8 %all_to_all.58.refs_0_ = bf16[8,768,128]{2,1,0:T(8,128)(2,1)S(1)} all-to-all(bf16[8,768,128]{2,1,0:T(8,128)(2,1)S(1)} %get-tuple-element.46), channel_id=1, replica_groups={{0,8,16,24,32,40,48,56},{1,9,17,25,33,41,49,57},{2,10,18,26,34,42,50,58..., dimensions={0} | all-to-all | bytes 3145728 | tf_op jit(solution)/shard_map/all_to_all | solution.py:439
  163.9 0.3 shard_map.137
  164.2 14.0 %all_to_all.59.refs_0_ = bf16[8,96,128]{2,1,0:T(8,128)(2,1)S(1)} all-to-all(bf16[8,96,128]{2,1,0:T(8,128)(2,1)S(1)} %shard_map.137), channel_id=1, replica_groups={{0,1,2,3,4,5,6,7},{8,9,10,11,12,13,14,15},{16,17,18,19,20,21,22,23},{24..., dimensions={0} | all-to-all | bytes 393216 | tf_op jit(solution)/shard_map/all_to_all | solution.py:439
  178.2 7.4 %collective-permute-start.3 = (f32[96,128]{1,0:T(8,128)S(1)}, f32[96,128]{1,0:T(8,128)S(1)}, u32[]{:S(2)}, u32[]{:S(2)}) collective-permute-start(f32[96,128]{1,0:T(8,128)S(1)} %shard_map.138.refs_1_), channel_id=1, source_target_pairs={{0,192},{64,128},{128,64},{192,0},{1,193},{65,129},{129,65},{193,1... | collective-permute-start | bytes 147464 | tf_op jit(solution)/shard_map/ppermute | solution.py:451
  185.6 0.2 collective-permute-start.2
  185.8 0.3 collective-permute-start.1
  186.1 1.9 %collective-permute-done.3.refs_4_ = f32[96,128]{1,0:T(8,128)S(1)} collective-permute-done((f32[96,128]{1,0:T(8,128)S(1)}, f32[96,128]{1,0:T(8,128)S(1)}, u32[]{:S(2)}, u32[]{:S(2)}) %collective-permute-start.3) | collective-permute-done | bytes 49184 | tf_op jit(solution)/shard_map/ppermute | solution.py:451
  188.0 2.0 %collective-permute-done.2.refs_3_ = f32[96,128]{1,0:T(8,128)S(1)} collective-permute-done((f32[96,128]{1,0:T(8,128)S(1)}, f32[96,128]{1,0:T(8,128)S(1)}, u32[]{:S(2)}, u32[]{:S(2)}) %collective-permute-start.2) | collective-permute-done | bytes 49184 | tf_op jit(solution)/shard_map/ppermute | solution.py:451
  190.0 0.0 collective-permute-done.1.refs_2_
  190.0 0.6 shard_map.139
  (1 shorter events, 0.0 us)
Async XLA Ops:
  0.7 0.7 copy-start.5
  1.4 34.3 %copy-start = (bf16[2,512,768]{2,1,0:T(8,128)(2,1)S(1)}, bf16[2,512,768]{2,1,0:T(8,128)(2,1)}, u32[]{:S(2)}) copy-start(bf16[2,512,768]{2,1,0:T(8,128)(2,1)} %refs_1_.7) | copy-start | bytes 4718596
  1.4 34.3 %copy-start.1 = (bf16[2,256,512]{2,1,0:T(8,128)(2,1)S(1)}, bf16[2,256,512]{2,1,0:T(8,128)(2,1)}, u32[]{:S(2)}) copy-start(bf16[2,256,512]{2,1,0:T(8,128)(2,1)} %refs_5_.3) | copy-start | bytes 1572868
  1.4 34.3 %copy-start.2 = (bf16[1,3,48,512]{3,2,1,0:T(8,128)(2,1)S(1)}, bf16[1,3,48,512]{3,2,1,0:T(8,128)(2,1)}, u32[]{:S(2)}) copy-start(bf16[1,3,48,512]{3,2,1,0:T(8,128)(2,1)} %param.9) | copy-start | bytes 442372
  1.4 34.3 %copy-start.4 = (f32[2,512]{1,0:T(2,128)S(1)}, f32[2,512]{1,0:T(2,128)}, u32[]{:S(2)}) copy-start(f32[2,512]{1,0:T(2,128)} %refs_3_.5) | copy-start | bytes 12292
  1.4 34.3 %copy-start.6 = (f32[2,512]{1,0:T(2,128)S(1)}, f32[2,512]{1,0:T(2,128)}, u32[]{:S(2)}) copy-start(f32[2,512]{1,0:T(2,128)} %refs_3_.3) | copy-start | bytes 12292
  24.8 27.2 %copy-start.7 = (s32[192]{0:T(256)S(1)}, s32[192]{0:T(256)}, u32[]{:S(2)}) copy-start(s32[192]{0:T(256)} %param.16) | copy-start | bytes 2308
  24.8 27.2 %copy-start.8 = (s32[48]{0:T(128)S(1)}, s32[48]{0:T(128)}, u32[]{:S(2)}) copy-start(s32[48]{0:T(128)} %param.17) | copy-start | bytes 580
  35.7 30.5 %copy-start.3 = (bf16[1,3,48,512]{3,2,1,0:T(8,128)(2,1)S(1)}, bf16[1,3,48,512]{3,2,1,0:T(8,128)(2,1)}, u32[]{:S(2)}) copy-start(bf16[1,3,48,512]{3,2,1,0:T(8,128)(2,1)} %param.10) | copy-start | bytes 442372
  101.6 9.9 %collective-permute-start = (bf16[512,640]{1,0:T(8,128)(2,1)}, bf16[512,640]{1,0:T(8,128)(2,1)S(1)}, u32[]{:S(2)}, u32[]{:S(2)}) collective-permute-start(bf16[512,640]{1,0:T(8,128)(2,1)} %get-tuple-element.38), channel_id=1, source_target_pairs={{0,64},{64,0},{128,192},{192,128},{1,65},{65,1},{129,193},{193,129... | collective-permute-start | bytes 1966088 | tf_op jit(solution)/shard_map/ppermute | solution.py:451
  178.2 9.8 %collective-permute-start.3 = (f32[96,128]{1,0:T(8,128)S(1)}, f32[96,128]{1,0:T(8,128)S(1)}, u32[]{:S(2)}, u32[]{:S(2)}) collective-permute-start(f32[96,128]{1,0:T(8,128)S(1)} %shard_map.138.refs_1_), channel_id=1, source_target_pairs={{0,192},{64,128},{128,64},{192,0},{1,193},{65,129},{129,65},{193,1... | collective-permute-start | bytes 147464 | tf_op jit(solution)/shard_map/ppermute | solution.py:451
  185.6 4.4 %collective-permute-start.2 = (f32[96,128]{1,0:T(8,128)S(1)}, f32[96,128]{1,0:T(8,128)S(1)}, u32[]{:S(2)}, u32[]{:S(2)}) collective-permute-start(f32[96,128]{1,0:T(8,128)S(1)} %shard_map.138.refs_1_), channel_id=1, source_target_pairs={{0,128},{64,192},{128,0},{192,64},{1,129},{65,193},{129,1},{193,65... | collective-permute-start | bytes 147464 | tf_op jit(solution)/shard_map/ppermute | solution.py:451
  185.8 4.2 %collective-permute-start.1 = (f32[96,128]{1,0:T(8,128)S(1)}, f32[96,128]{1,0:T(8,128)S(1)}, u32[]{:S(2)}, u32[]{:S(2)}) collective-permute-start(f32[96,128]{1,0:T(8,128)S(1)} %shard_map.138.refs_1_), channel_id=1, source_target_pairs={{0,64},{64,0},{128,192},{192,128},{1,65},{65,1},{129,193},{193,129... | collective-permute-start | bytes 147464 | tf_op jit(solution)/shard_map/ppermute | solution.py:451

commit v4 on v3

--- a/solution.py
+++ b/solution.py
@@ -21,6 +21,7 @@
 DEVS = 64
 VMEM_LIMIT = 24 * 2**20
 EARLY = 3 * HH + 2 * HH
+SHORT = 112
 TILES = (3 * HH + EARLY // 2 + 128) // 128
 
 norm_eps = 1e-05
@@ -67,8 +68,9 @@
     query, key, value = projected[:, :HH], projected[:, HH : 2 * HH], projected[:, 2 * HH :]
     lane = iota((1, HH), 1)
     scale = jnp.zeros((1, HH), f32)
+    scales = scale_ref[...][block : block + 1]
     for h in range(HEADS):
-        scale = jnp.where(lane // HD == h, scale_ref[block, h], scale)
+        scale = jnp.where(lane // HD == h, scales[:, h : h + 1], scale)
     q_factor = lax.rsqrt(1.0 + head_sums(query * query))
     k_factor = lax.rsqrt(1.0 + head_sums(key * key))
     q_hat = query * q_factor * jnp.exp(scale)
@@ -114,6 +116,14 @@
     depth = pair[0].shape[-1]
     parts = [part.reshape(GROUP, ROWS_DEV, 1, WIN, depth) for part in pair]
     return jnp.concatenate(parts, 2).reshape(GROUP, TOK, depth)
+
+
+def pack_cells(cells):
+    tail = cells[:, SHORT:].reshape(GROUP * 32, 128)
+    moved = [pltpu.roll(tail, 96 - 32 * kind, 1).reshape(GROUP, 32, 128) for kind in range(3)]
+    moved = jnp.concatenate(moved + [jnp.zeros((GROUP, SHORT - 96, 128), f32)], 1)
+    lane = iota(moved.shape, 2)
+    return jnp.where(lane < 96, cells[:, :SHORT], moved)
 
 
 def roll_tokens(array, by):
@@ -234,14 +244,14 @@
         k_factor = cells[:, 98:99] + cells[:, 99:100]
         factor = jnp.where(lane < HD, q_factor, jnp.where(lane < 2 * HD, k_factor, 1.0))
         results.append(factor * (total - unit * head_sums(unit * total)))
-    out_ref[...] = from_windows(results).astype(bf16)
-
-
-def first_kernel(scale_ref, tokens_ref, w_ref, out_ref):
+    out_ref[...] = pack_cells(from_windows(results)).astype(bf16)
+
+
+def first_kernel(tokens_ref, w_ref, scale_ref, out_ref):
     send_projected(tokens_ref[...], w_ref[...], scale_ref, 0, out_ref)
 
 
-def middle_kernel(scale_ref, packed_ref, gain_ref, bias_ref, tokens_ref, w_proj_ref, w_ref, out_ref, rolled_ref):
+def middle_kernel(packed_ref, scale_ref, gain_ref, bias_ref, tokens_ref, w_proj_ref, w_ref, out_ref, rolled_ref):
     attended = unpack_heads(packed_ref)
     y_hat, _ = normalized(attended, w_proj_ref[...])
     out = (tokens_ref[...].astype(f32) + y_hat * gain_ref[0:1] + bias_ref[0:1]).astype(bf16).astype(f32)
@@ -261,9 +271,9 @@
 
 def gather_qkv(qkv_ref):
     parts = [qkv_ref[h].astype(f32) for h in range(HEADS)]
-    return jnp.concatenate(
-        [lane_slice(parts[h], kind * HD) for kind in range(3) for h in range(HEADS)], 1
-    ).astype(bf16)
+    top = [lane_slice(parts[h][:SHORT], kind * HD) for kind in range(3) for h in range(HEADS)]
+    tail = [lane_slice(parts[h][kind * 32 : kind * 32 + 32], 96) for kind in range(3) for h in range(HEADS)]
+    return jnp.concatenate([jnp.concatenate(top, 1), jnp.concatenate(tail, 1)], 0).astype(bf16)
 
 
 def give(array, side, kept_ref, given_ref):
@@ -302,11 +312,12 @@
     gains_ref[...] = gains
 
 
-def last_kernel(
-    qkv_ref, w_ref, tokens_ref, got_ref, gains0_ref, gains1_ref, grad_ref, kept_ref, parts_ref, out_ref
-):
+def image_kernel(qkv_ref, w_ref, grad_ref, out_ref):
+    out_ref[...] = (grad_ref[...].astype(f32) + dot_t(gather_qkv(qkv_ref), w_ref[...])).astype(bf16)
+
+
+def last_kernel(qkv_ref, tokens_ref, got_ref, gains0_ref, gains1_ref, kept_ref, parts_ref):
     d_qkv = gather_qkv(qkv_ref)
-    out_ref[...] = (grad_ref[...].astype(f32) + dot_t(d_qkv, w_ref[...])).astype(bf16)
     pieces = []
     for ref in (gains0_ref, gains1_ref):
         for row in (0, 1):
@@ -332,13 +343,16 @@
     out_ref[...] = jnp.sum(parts_ref[...].astype(f32), 0)
 
 
-def final_kernel(core_ref, own_ref, core1_ref, chip_ref, chip1_ref, qkv_ref, proj_ref, gain_ref, bias_ref):
-    same = own_ref[...] + chip_ref[...]
-    other = core1_ref[...] + chip1_ref[...]
-    both = (same + other).reshape(TILES, 8, 128)
+def add_kernel(one_ref, two_ref, out_ref):
+    out_ref[...] = one_ref[...] + two_ref[...]
+
+
+def final_kernel(core_ref, own_ref, other_ref, qkv_ref, proj_ref, gain_ref, bias_ref):
+    own = own_ref[...].reshape(TILES, 8, 128)
+    other = other_ref[...].reshape(TILES, 8, 128)
+    both = own + other
     first = core_ref[0] == 0
-    left = jnp.where(first, same, other).reshape(TILES, 8, 128)
-    right = jnp.where(first, other, same).reshape(TILES, 8, 128)
+    left, right = jnp.where(first, own, other), jnp.where(first, other, own)
     tiles = [left[i] for i in range(6, 11)] + [right[i] for i in range(6, 11)]
     qkv_ref[0] = jnp.concatenate([both[i] for i in range(6)], 1)
     qkv_ref[1] = jnp.concatenate(tiles[:6], 1)
@@ -349,26 +363,46 @@
     bias_ref[...] = jnp.concatenate([gains[2:3] + gains[3:4], gains[6:7] + gains[7:8]], 0)
 
 
+def pieces_of(shape):
+    return 4 if shape[0] % 64 == 0 and shape[0] * shape[1] >= 2**18 else 1
+
+
+def copies_of(source, target, sems, first):
+    count = pieces_of(target.shape)
+    rows = target.shape[0] // count
+    if count == 1:
+        return [pltpu.make_async_copy(source, target, sems.at[first])]
+    return [
+        pltpu.make_async_copy(
+            source.at[pl.ds(i * rows, rows)], target.at[pl.ds(i * rows, rows)], sems.at[first + i]
+        )
+        for i in range(count)
+    ]
+
+
 class Fetched:
-    def __init__(self, source, ref, sem):
-        self.ref, self.copy = ref, pltpu.make_async_copy(source, ref, sem)
-        self.copy.start()
+    def __init__(self, source, ref, sems, first):
+        self.ref, self.copies = ref, copies_of(source, ref, sems, first)
+        for copy in self.copies:
+            copy.start()
         self.waited = False
 
     def __getitem__(self, at):
         if not self.waited:
-            self.copy.wait()
+            for copy in self.copies:
+                copy.wait()
             self.waited = True
         return self.ref[at]
 
 
 class Stored:
-    def __init__(self, ref, target, sem):
-        self.ref, self.copy = ref, pltpu.make_async_copy(ref, target, sem)
+    def __init__(self, ref, target, sems, first):
+        self.ref, self.copies = ref, copies_of(ref, target, sems, first)
 
     def __setitem__(self, at, value):
         self.ref[at] = value
-        self.copy.start()
+        for copy in self.copies:
+            copy.start()
 
 
 def call(kernel, outs, scalars, arrays, masks=(), fetched=(), stored=()):
@@ -384,14 +418,18 @@
         scalar_refs, array_refs, sources, mask_refs, out_refs, targets, filled, sent = parts
         sems = refs[-1]
         near = [ref if block is None else ref.at[block] for ref, (_, block) in zip(array_refs, arrays)]
-        far = []
+        far, results, first = [], [], 0
         for i, (_, block) in enumerate(fetched):
             source = sources[i] if block is None else sources[i].at[block]
-            far.append(Fetched(source, filled[i], sems.at[i]))
-        results = [Stored(sent[i], targets[i], sems.at[len(fetched) + i]) for i in range(len(stored))]
+            far.append(Fetched(source, filled[i], sems, first))
+            first += pieces_of(filled[i].shape)
+        for i in range(len(stored)):
+            results.append(Stored(sent[i], targets[i], sems, first))
+            first += pieces_of(sent[i].shape)
         kernel(*scalar_refs, *near, *far, *mask_refs, *out_refs, *results)
         for result in results:
-            result.copy.wait()
+            for copy in result.copies:
+                copy.wait()
 
     smem = pl.BlockSpec(memory_space=pltpu.SMEM)
     vmem = pl.BlockSpec(memory_space=pltpu.VMEM)
@@ -401,7 +439,7 @@
     ]
     scratch += [pltpu.VMEM(*out) for out in stored]
     if scratch:
-        scratch.append(pltpu.SemaphoreType.DMA((len(scratch),)))
+        scratch.append(pltpu.SemaphoreType.DMA((sum(pieces_of(buffer.shape) for buffer in scratch),)))
     return pl.pallas_call(
         wrapped,
         out_shape=[jax.ShapeDtypeStruct(*out) for out in outs] + [pltpu.HBM(*out) for out in stored],
@@ -441,6 +479,7 @@
     tokens0 = image.reshape(TOK, C)
     grad_out = out_grad.reshape(TOK, C)
     wide = ((GROUP, TOK, 128), bf16)
+    short = ((GROUP, SHORT, 128), bf16)
     narrow = ((GROUP, PACK, 128), bf16)
     cells = ((TOK, C), bf16)
     proj = ((C, HH), bf16)
@@ -450,15 +489,15 @@
     def swap(array, apart):
         return lax.ppermute(array, "dp", [(i, i ^ apart) for i in range(4)])
 
-    (x0,) = call(first_kernel, [wide], (logit_scale,), (), fetched=(tokens0, (w_qkv, 0)))
+    (x0,) = call(first_kernel, [wide], (), (), fetched=(tokens0, (w_qkv, 0), logit_scale))
     x0 = exchange(x0, aligned)
     (a0,) = call(functools.partial(attend_kernel, False), [narrow], (), (x0,))
     a0 = exchange(a0, aligned)
     x1, tokens1 = call(
         middle_kernel,
         [wide],
-        (logit_scale,),
-        (a0, norm_gain, norm_bias, tokens0, (w_proj, 0), (w_qkv, 1)),
+        (),
+        (a0, logit_scale, norm_gain, norm_bias, tokens0, (w_proj, 0), (w_qkv, 1)),
         stored=[cells],
     )
     x1 = exchange(x1, moved)
@@ -469,7 +508,7 @@
     )
     d1 = exchange(d1, moved)
     (qkv1,) = call(
-        functools.partial(attend_back_kernel, 1, True), [wide], (head1, logit_scale), (x1, d1), masks
+        functools.partial(attend_back_kernel, 1, True), [short], (head1, logit_scale), (x1, d1), masks
     )
     qkv1 = exchange(qkv1, moved)
     d0, gains0, grad0, kept, given = call(
@@ -482,25 +521,29 @@
     )
     d0, got = lax.optimization_barrier((d0, swap(given, 1)))
     d0 = exchange(d0, aligned)
-    (qkv0,) = call(functools.partial(attend_back_kernel, 0, False), [wide], (head0, logit_scale), (x0, d0))
+    (qkv0,) = call(functools.partial(attend_back_kernel, 0, False), [short], (head0, logit_scale), (x0, d0))
     qkv0 = exchange(qkv0, aligned)
-    parts, grad_image = call(
+    (parts,) = call(
         last_kernel,
-        [((8, TILES * C // 8, 128), bf16), cells],
+        [((8, TILES * C // 8, 128), bf16)],
         (),
-        (qkv0, (w_qkv, 0), tokens0, got, gains0, gains1),
-        fetched=(grad0, kept),
+        (qkv0, tokens0, got, gains0, gains1),
+        fetched=(kept,),
     )
     parts = exchange(parts, across)
     (parts,) = call(first_sum_kernel, [((8, TILES * 8, 128), bf16)], (), (parts,))
     parts = exchange(parts, aligned)
     (share,) = call(second_sum_kernel, [((TILES * 8, 128), f32)], (), (parts,))
+    (share,) = call(add_kernel, [((TILES * 8, 128), f32)], (), (share, swap(share, 2)))
+    other = swap(share, 1)
+    qkv0, _ = lax.optimization_barrier((qkv0, share))
+    (grad_image,) = call(image_kernel, [cells], (), (qkv0, (w_qkv, 0), grad0))
     small = ((2, 8), f32)
     grad_qkv, grad_proj, grad_gain, grad_bias = call(
         final_kernel,
         [((2, 8, 3 * HH), f32), ((2, 8, HH), f32), small, small],
         (core,),
-        (share, swap(share, 1), swap(share, 2), swap(share, 3)),
+        (share, other),
     )
     return (
         grad_image.reshape(image.shape),

time: 191 us -> 186 us (0.974)
  blocking collectives: 144 us -> 140 us
  waiting for transfers between devices: 5.89 us -> 3.93 us
    all_to_all x10, blocking collectives: 144 us -> 140 us  [exchange(): lax.all_to_all(array, 'rows', 0, 0, axis_index_groups=groups, tiled=True)]
    ppermute x4 -> x3, waiting for transfers between devices: 5.89 us -> 3.93 us  [swap(): return lax.ppermute(array, 'dp', [(i, i ^ apart) for i in range(4)])]
    ppermute x4 -> x3, starting transfers between devices: 15.8 us -> 17.6 us  [swap(): return lax.ppermute(array, 'dp', [(i, i ^ apart) for i in range(4)])]
    pallas_call x12 -> x14, Pallas kernels: 23.2 us -> 23.3 us  [call(): pl.pallas_call(wrapped, out_shape=[jax.ShapeDtypeStruct(*out) for out in...]
  transfers between devices with their start and end apart: 4 -> 3, of which waited for: 3 -> 2; matrix products, arithmetic and copies ran while one was open for 0% -> 0% of each run, Pallas kernels for 0% -> 1%
where the time goes in v4:
time: 186 us
  blocking collectives  140 us (75%)
  Pallas kernels  23.3 us (13%)
  starting transfers between devices  17.6 us (9%)
  waiting for transfers between devices  3.93 us (2%)
    all_to_all x10, blocking collectives, exchange(): lax.all_to_all(array, 'rows', 0, 0, axis_index_groups=groups, tiled=True)  140 us
    pallas_call x14, Pallas kernels, call(): pl.pallas_call(wrapped, out_shape=[jax.ShapeDtypeStruct(*out) for out in...  23.3 us
    ppermute x3, starting transfers between devices, swap(): return lax.ppermute(array, 'dp', [(i, i ^ apart) for i in range(4)])  17.6 us
    ppermute x3, waiting for transfers between devices, swap(): return lax.ppermute(array, 'dp', [(i, i ^ apart) for i in range(4)])  3.93 us
  transfers between devices with their start and end apart: 3, of which 2 were waited for; matrix products, arithmetic and copies ran while one was open for 0% of the time, Pallas kernels for 1%

profile of v4, /device:TPU:1, one launch (start us, length us, event | category | flops | bytes accessed | tf_op | source)
XLA Modules:
  0.0 186.0 jit_solution(3611159595596749835)
XLA Ops:
  0.7 0.0 copy-start
  0.7 0.0 copy-start.1
  0.7 0.0 copy-start.2
  0.7 0.0 copy-start.5
  0.7 0.0 copy-start.6
  0.7 0.0 copy-start.7
  0.7 2.2 %shard_map.128 = bf16[8,144,128]{2,1,0:T(8,128)(2,1)S(1)} custom-call(bf16[144,512]{1,0:T(8,128)(2,1)} %bitcast.10, bf16[2,512,768]{2,1,0:T(8,128)(2,1)} %refs_1_.11, f32[2,8]{1,0:T(2,128)} %refs_1_.10), custom_call_target="tpu_custom_call" | custom-call | tf_op jit(solution)/shard_map/pallas_call | solution.py:443
  3.0 19.7 %all_to_all.50.refs_0_.refs_2_ = bf16[8,144,128]{2,1,0:T(8,128)(2,1)S(1)} all-to-all(bf16[8,144,128]{2,1,0:T(8,128)(2,1)S(1)} %shard_map.128), channel_id=1, replica_groups={{0,1,2,3,4,5,6,7},{8,9,10,11,12,13,14,15},{16,17,18,19,20,21,22,23},{24..., dimensions={0} | all-to-all | bytes 589824 | tf_op jit(solution)/shard_map/all_to_all | solution.py:477
  22.6 1.3 shard_map.129
  23.9 0.0 copy-start.8
  23.9 0.0 copy-start.9
  23.9 10.8 %all_to_all.51.refs_0_.refs_2_ = bf16[8,48,128]{2,1,0:T(8,128)(2,1)S(1)} all-to-all(bf16[8,48,128]{2,1,0:T(8,128)(2,1)S(1)} %shard_map.129), channel_id=1, replica_groups={{0,1,2,3,4,5,6,7},{8,9,10,11,12,13,14,15},{16,17,18,19,20,21,22,23},{24..., dimensions={0} | all-to-all | bytes 196608 | tf_op jit(solution)/shard_map/all_to_all | solution.py:477
  34.7 0.0 copy-done
  34.7 0.0 copy-done.1
  34.7 0.0 copy-done.2
  34.7 0.0 copy-done.5
  34.7 0.0 copy-done.6
  34.7 0.0 copy-done.7
  34.7 0.0 copy-start.3
  34.7 1.7 shard_map.130
  36.4 14.2 %all_to_all.52.refs_0_.refs_2_ = bf16[8,144,128]{2,1,0:T(8,128)(2,1)S(1)} all-to-all(bf16[8,144,128]{2,1,0:T(8,128)(2,1)S(1)} %get-tuple-element.31), channel_id=1, replica_groups={{4,5,6,7,8,9,10,11},{12,13,14,15,16,17,18,19},{20,21,22,23,24,25,26,27}..., dimensions={0} | all-to-all | bytes 589824 | tf_op jit(solution)/shard_map/all_to_all | solution.py:477
  50.6 0.0 copy-done.8
  50.6 0.0 copy-done.9
  50.6 1.9 %shard_map.131 = bf16[8,48,128]{2,1,0:T(8,128)(2,1)S(1)} custom-call(bf16[8,144,128]{2,1,0:T(8,128)(2,1)S(1)} %all_to_all.52.refs_0_.refs_2_, s32[1]{0:T(128)} %bitcast.2.refs_1_.refs_4_, s32[1,192]{1,0:T(1,128)S(1)} %bitcast.15, s32[1,48]{1,0:T(1,128)S(1)} %bitcast.17), custom_call_target="tpu_custom_call" | custom-call | tf_op jit(solution)/shard_map/pallas_call | solution.py:443
  52.5 12.2 %all_to_all.53.refs_0_ = bf16[8,48,128]{2,1,0:T(8,128)(2,1)S(1)} all-to-all(bf16[8,48,128]{2,1,0:T(8,128)(2,1)S(1)} %shard_map.131), channel_id=1, replica_groups={{4,5,6,7,8,9,10,11},{12,13,14,15,16,17,18,19},{20,21,22,23,24,25,26,27}..., dimensions={0} | all-to-all | bytes 196608 | tf_op jit(solution)/shard_map/all_to_all | solution.py:477
  64.7 0.0 copy-done.3
  64.7 0.8 shard_map.132
  65.5 12.4 %all_to_all.54.refs_3_ = bf16[8,48,128]{2,1,0:T(8,128)(2,1)S(1)} all-to-all(bf16[8,48,128]{2,1,0:T(8,128)(2,1)S(1)} %get-tuple-element.33), channel_id=1, replica_groups={{4,5,6,7,8,9,10,11},{12,13,14,15,16,17,18,19},{20,21,22,23,24,25,26,27}..., dimensions={0} | all-to-all | bytes 196608 | tf_op jit(solution)/shard_map/all_to_all | solution.py:477
  78.0 4.3 %shard_map.133 = bf16[8,112,128]{2,1,0:T(8,128)(2,1)S(1)} custom-call(s32[1]{0:T(128)} %bitcast.1.refs_0_, f32[2,8]{1,0:T(2,128)S(1)} %copy-done.6, bf16[8,144,128]{2,1,0:T(8,128)(2,1)S(1)} %all_to_all.52.refs_0_.refs_2_, bf16[8,48,128]{2,1,0:T(8,128)(2,1)S(1)} %all_to_all.54.refs_3_, s32[1]{0:T(128)} %bitcast.2.refs_1_.refs_4_, s32[1,192]{1,0:T(1,128)S(1)} %bitcast.16, ...), custom_call_target="tpu_custom_call" | custom-call | tf_op jit(solution)/shard_map/pallas_call | solution.py:443
  82.2 13.9 %all_to_all.55.refs_1_ = bf16[8,112,128]{2,1,0:T(8,128)(2,1)S(1)} all-to-all(bf16[8,112,128]{2,1,0:T(8,128)(2,1)S(1)} %shard_map.133), channel_id=1, replica_groups={{4,5,6,7,8,9,10,11},{12,13,14,15,16,17,18,19},{20,21,22,23,24,25,26,27}..., dimensions={0} | all-to-all | bytes 458752 | tf_op jit(solution)/shard_map/all_to_all | solution.py:477
  96.1 3.4 %shard_map.134 = (bf16[8,48,128]{2,1,0:T(8,128)(2,1)S(1)}, f32[8,512]{1,0:T(8,128)S(1)}, bf16[144,512]{1,0:T(8,128)(2,1)}, bf16[512,640]{1,0:T(8,128)(2,1)}, bf16[512,640]{1,0:T(8,128)(2,1)}) custom-call(s32[1]{0:T(128)} %bitcast.3.refs_0_, bf16[8,112,128]{2,1,0:T(8,128)(2,1)S(1)} %all_to_all.55.refs_1_, bf16[8,48,128]{2,1,0:T(8,128)(2,1)S(1)} %all_to_all.51.refs_0_.refs_2_, ...), custom_call_target="tpu_custom_call" | custom-call | tf_op jit(solution)/shard_map/pallas_call | solution.py:443
  99.5 7.9 %collective-permute-start = (bf16[512,640]{1,0:T(8,128)(2,1)}, bf16[512,640]{1,0:T(8,128)(2,1)S(1)}, u32[]{:S(2)}, u32[]{:S(2)}) collective-permute-start(bf16[512,640]{1,0:T(8,128)(2,1)} %get-tuple-element.37), channel_id=1, source_target_pairs={{0,64},{64,0},{128,192},{192,128},{1,65},{65,1},{129,193},{193,129... | collective-permute-start | bytes 1966088 | tf_op jit(solution)/shard_map/ppermute | solution.py:490
  107.5 1.9 %collective-permute-done.refs_2_ = bf16[512,640]{1,0:T(8,128)(2,1)S(1)} collective-permute-done((bf16[512,640]{1,0:T(8,128)(2,1)}, bf16[512,640]{1,0:T(8,128)(2,1)S(1)}, u32[]{:S(2)}, u32[]{:S(2)}) %collective-permute-start) | collective-permute-done | bytes 655392 | tf_op jit(solution)/shard_map/ppermute | solution.py:490
  109.4 10.3 %all_to_all.56.refs_3_ = bf16[8,48,128]{2,1,0:T(8,128)(2,1)S(1)} all-to-all(bf16[8,48,128]{2,1,0:T(8,128)(2,1)S(1)} %get-tuple-element.38), channel_id=1, replica_groups={{0,1,2,3,4,5,6,7},{8,9,10,11,12,13,14,15},{16,17,18,19,20,21,22,23},{24..., dimensions={0} | all-to-all | bytes 196608 | tf_op jit(solution)/shard_map/all_to_all | solution.py:477
  119.7 3.7 %shard_map.135 = bf16[8,112,128]{2,1,0:T(8,128)(2,1)S(1)} custom-call(s32[1]{0:T(128)} %bitcast.refs_0_, f32[2,8]{1,0:T(2,128)S(1)} %copy-done.6, bf16[8,144,128]{2,1,0:T(8,128)(2,1)S(1)} %all_to_all.50.refs_0_.refs_2_, bf16[8,48,128]{2,1,0:T(8,128)(2,1)S(1)} %all_to_all.56.refs_3_), custom_call_target="tpu_custom_call" | custom-call | tf_op jit(solution)/shard_map/pallas_call | solution.py:443
  123.4 11.3 %all_to_all.57.refs_0_ = bf16[8,112,128]{2,1,0:T(8,128)(2,1)S(1)} all-to-all(bf16[8,112,128]{2,1,0:T(8,128)(2,1)S(1)} %shard_map.135), channel_id=1, replica_groups={{0,1,2,3,4,5,6,7},{8,9,10,11,12,13,14,15},{16,17,18,19,20,21,22,23},{24..., dimensions={0} | all-to-all | bytes 458752 | tf_op jit(solution)/shard_map/all_to_all | solution.py:477
  134.7 2.0 %shard_map.136 = bf16[8,768,128]{2,1,0:T(8,128)(2,1)S(1)} custom-call(bf16[8,112,128]{2,1,0:T(8,128)(2,1)S(1)} %all_to_all.57.refs_0_, bf16[144,512]{1,0:T(8,128)(2,1)S(1)} %bitcast.12, bf16[512,640]{1,0:T(8,128)(2,1)S(1)} %collective-permute-done.refs_2_, f32[8,512]{1,0:T(8,128)S(1)} %get-tuple-element.40.refs_3_, f32[8,512]{1,0:T(8,128)S(1)} %get-tuple-element.41.refs_4_, ...), custom_call_target="tpu_custom_call" | custom-call | tf_op jit(solution)/shard_map/pallas_call | solution.py:443
  136.8 24.4 %all_to_all.58.refs_0_ = bf16[8,768,128]{2,1,0:T(8,128)(2,1)S(1)} all-to-all(bf16[8,768,128]{2,1,0:T(8,128)(2,1)S(1)} %shard_map.136), channel_id=1, replica_groups={{0,8,16,24,32,40,48,56},{1,9,17,25,33,41,49,57},{2,10,18,26,34,42,50,58..., dimensions={0} | all-to-all | bytes 3145728 | tf_op jit(solution)/shard_map/all_to_all | solution.py:477
  161.2 0.0 copy-start.4
  161.2 0.3 shard_map.137
  161.5 11.0 %all_to_all.59.refs_0_ = bf16[8,96,128]{2,1,0:T(8,128)(2,1)S(1)} all-to-all(bf16[8,96,128]{2,1,0:T(8,128)(2,1)S(1)} %shard_map.137), channel_id=1, replica_groups={{0,1,2,3,4,5,6,7},{8,9,10,11,12,13,14,15},{16,17,18,19,20,21,22,23},{24..., dimensions={0} | all-to-all | bytes 393216 | tf_op jit(solution)/shard_map/all_to_all | solution.py:477
  172.5 2.8 %collective-permute-start.1 = (f32[96,128]{1,0:T(8,128)S(1)}, f32[96,128]{1,0:T(8,128)S(1)}, u32[]{:S(2)}, u32[]{:S(2)}) collective-permute-start(f32[96,128]{1,0:T(8,128)S(1)} %shard_map.138.refs_0_), channel_id=1, source_target_pairs={{0,128},{64,192},{128,0},{192,64},{1,129},{65,193},{129,1},{193,65... | collective-permute-start | bytes 147464 | tf_op jit(solution)/shard_map/ppermute | solution.py:490
  175.4 2.0 %collective-permute-done.1.refs_1_ = f32[96,128]{1,0:T(8,128)S(1)} collective-permute-done((f32[96,128]{1,0:T(8,128)S(1)}, f32[96,128]{1,0:T(8,128)S(1)}, u32[]{:S(2)}, u32[]{:S(2)}) %collective-permute-start.1) | collective-permute-done | bytes 49184 | tf_op jit(solution)/shard_map/ppermute | solution.py:490
  177.4 6.8 %collective-permute-start.2 = (f32[96,128]{1,0:T(8,128)S(1)}, f32[96,128]{1,0:T(8,128)S(1)}, u32[]{:S(2)}, u32[]{:S(2)}) collective-permute-start(f32[96,128]{1,0:T(8,128)S(1)} %shard_map.139.refs_1_), channel_id=1, source_target_pairs={{0,64},{64,0},{128,192},{192,128},{1,65},{65,1},{129,193},{193,129... | collective-permute-start | bytes 147464 | tf_op jit(solution)/shard_map/ppermute | solution.py:490
  184.2 0.0 copy-done.4
  184.2 1.1 shard_map.140
  185.3 0.0 collective-permute-done.2.refs_2_
  185.3 0.6 shard_map.141
  (2 shorter events, 0.0 us)
Async XLA Ops:
  0.7 34.0 %copy-start = (bf16[2,512,768]{2,1,0:T(8,128)(2,1)S(1)}, bf16[2,512,768]{2,1,0:T(8,128)(2,1)}, u32[]{:S(2)}) copy-start(bf16[2,512,768]{2,1,0:T(8,128)(2,1)} %refs_1_.11) | copy-start | bytes 4718596
  0.7 34.0 %copy-start.1 = (bf16[2,256,512]{2,1,0:T(8,128)(2,1)S(1)}, bf16[2,256,512]{2,1,0:T(8,128)(2,1)}, u32[]{:S(2)}) copy-start(bf16[2,256,512]{2,1,0:T(8,128)(2,1)} %refs_5_.3) | copy-start | bytes 1572868
  0.7 34.0 %copy-start.2 = (bf16[1,3,48,512]{3,2,1,0:T(8,128)(2,1)S(1)}, bf16[1,3,48,512]{3,2,1,0:T(8,128)(2,1)}, u32[]{:S(2)}) copy-start(bf16[1,3,48,512]{3,2,1,0:T(8,128)(2,1)} %param.9) | copy-start | bytes 442372
  0.7 34.0 %copy-start.5 = (f32[2,512]{1,0:T(2,128)S(1)}, f32[2,512]{1,0:T(2,128)}, u32[]{:S(2)}) copy-start(f32[2,512]{1,0:T(2,128)} %refs_3_.5) | copy-start | bytes 12292
  0.7 34.0 %copy-start.6 = (f32[2,8]{1,0:T(2,128)S(1)}, f32[2,8]{1,0:T(2,128)}, u32[]{:S(2)}) copy-start(f32[2,8]{1,0:T(2,128)} %refs_1_.10) | copy-start | bytes 196
  0.7 34.0 %copy-start.7 = (f32[2,512]{1,0:T(2,128)S(1)}, f32[2,512]{1,0:T(2,128)}, u32[]{:S(2)}) copy-start(f32[2,512]{1,0:T(2,128)} %refs_3_.3) | copy-start | bytes 12292
  23.9 26.7 %copy-start.8 = (s32[192]{0:T(256)S(1)}, s32[192]{0:T(256)}, u32[]{:S(2)}) copy-start(s32[192]{0:T(256)} %param.16) | copy-start | bytes 2308
  23.9 26.7 %copy-start.9 = (s32[48]{0:T(128)S(1)}, s32[48]{0:T(128)}, u32[]{:S(2)}) copy-start(s32[48]{0:T(128)} %param.17) | copy-start | bytes 580
  34.7 30.0 %copy-start.3 = (bf16[1,3,48,512]{3,2,1,0:T(8,128)(2,1)S(1)}, bf16[1,3,48,512]{3,2,1,0:T(8,128)(2,1)}, u32[]{:S(2)}) copy-start(bf16[1,3,48,512]{3,2,1,0:T(8,128)(2,1)} %param.10) | copy-start | bytes 442372
  99.5 9.9 %collective-permute-start = (bf16[512,640]{1,0:T(8,128)(2,1)}, bf16[512,640]{1,0:T(8,128)(2,1)S(1)}, u32[]{:S(2)}, u32[]{:S(2)}) collective-permute-start(bf16[512,640]{1,0:T(8,128)(2,1)} %get-tuple-element.37), channel_id=1, source_target_pairs={{0,64},{64,0},{128,192},{192,128},{1,65},{65,1},{129,193},{193,129... | collective-permute-start | bytes 1966088 | tf_op jit(solution)/shard_map/ppermute | solution.py:490
  161.2 23.0 %copy-start.4 = (bf16[144,512]{1,0:T(8,128)(2,1)S(1)}, bf16[144,512]{1,0:T(8,128)(2,1)}, u32[]{:S(2)}) copy-start(bf16[144,512]{1,0:T(8,128)(2,1)} %get-tuple-element.44.refs_2_) | copy-start | bytes 442372
  172.5 4.8 %collective-permute-start.1 = (f32[96,128]{1,0:T(8,128)S(1)}, f32[96,128]{1,0:T(8,128)S(1)}, u32[]{:S(2)}, u32[]{:S(2)}) collective-permute-start(f32[96,128]{1,0:T(8,128)S(1)} %shard_map.138.refs_0_), channel_id=1, source_target_pairs={{0,128},{64,192},{128,0},{192,64},{1,129},{65,193},{129,1},{193,65... | collective-permute-start | bytes 147464 | tf_op jit(solution)/shard_map/ppermute | solution.py:490
  177.4 7.9 %collective-permute-start.2 = (f32[96,128]{1,0:T(8,128)S(1)}, f32[96,128]{1,0:T(8,128)S(1)}, u32[]{:S(2)}, u32[]{:S(2)}) collective-permute-start(f32[96,128]{1,0:T(8,128)S(1)} %shard_map.139.refs_1_), channel_id=1, source_target_pairs={{0,64},{64,0},{128,192},{192,128},{1,65},{65,1},{129,193},{193,129... | collective-permute-start | bytes 147464 | tf_op jit(solution)/shard_map/ppermute | solution.py:490

commit v5 on v4

--- a/solution.py
+++ b/solution.py
@@ -22,7 +22,10 @@
 VMEM_LIMIT = 24 * 2**20
 EARLY = 3 * HH + 2 * HH
 SHORT = 112
-TILES = (3 * HH + EARLY // 2 + 128) // 128
+LATE = 3 * HH
+TILES = (LATE // 2 + EARLY // 2) // 128
+SENT = TILES * C // 8 + 16
+SHARE = TILES * 8 + 16
 
 norm_eps = 1e-05
 mask_value = 100.0
@@ -63,7 +66,7 @@
     return x[:, at : at + HD]
 
 
-def send_projected(tokens, weight, scale_ref, block, out_ref):
+def send_projected(tokens, weight, scale_ref, block, out_ref, factors_ref):
     projected = dot(tokens, weight)
     query, key, value = projected[:, :HH], projected[:, HH : 2 * HH], projected[:, 2 * HH :]
     lane = iota((1, HH), 1)
@@ -73,21 +76,32 @@
         scale = jnp.where(lane // HD == h, scales[:, h : h + 1], scale)
     q_factor = lax.rsqrt(1.0 + head_sums(query * query))
     k_factor = lax.rsqrt(1.0 + head_sums(key * key))
+    slot = iota((PACK, HH), 1) % HD
+    factors = jnp.zeros((PACK, HH), f32)
+    for r in range(ROWS_DEV):
+        rows = slice(r * PACK, (r + 1) * PACK)
+        values = [*split_two(q_factor[rows]), *split_two(k_factor[rows])]
+        for i, part in enumerate(values):
+            factors = jnp.where(slot == 4 * r + i, part, factors)
+    factors_ref[...] = factors.astype(bf16)
     q_hat = query * q_factor * jnp.exp(scale)
     k_hat = key * k_factor
-    q_high, q_low = split_two(q_factor)
-    k_high, k_low = split_two(k_factor)
-    slot = iota(q_hat.shape, 1) % HD
-    extra = jnp.where(
-        slot == 0,
-        q_high,
-        jnp.where(slot == 1, q_low, jnp.where(slot == 2, k_high, jnp.where(slot == 3, k_low, 0.0))),
-    )
+    zeros = jnp.zeros((SHORT - 3 * (TOK - SHORT), HD), f32)
     for h in range(HEADS):
-        at = h * HD
-        out_ref[h] = jnp.concatenate(
-            [lane_slice(q_hat, at), lane_slice(k_hat, at), lane_slice(value, at), lane_slice(extra, at)], 1
-        ).astype(bf16)
+        parts = [lane_slice(part, h * HD) for part in (q_hat, k_hat, value)]
+        tail = jnp.concatenate([part[SHORT:] for part in parts] + [zeros], 0)
+        out_ref[h] = jnp.concatenate([part[:SHORT] for part in parts] + [tail], 1).astype(bf16)
+
+
+def unpack_cells(x_ref):
+    x = x_ref[...].astype(f32)
+    lane = iota((GROUP * 32, 128), 1)
+    rolled = [
+        pltpu.roll(x[:, kind * 32 : kind * 32 + 32].reshape(GROUP * 32, 128), 32 + 32 * kind, 1)
+        for kind in range(3)
+    ]
+    tail = jnp.where(lane < HD, rolled[0], jnp.where(lane < 2 * HD, rolled[1], rolled[2]))
+    return jnp.concatenate([x, tail.reshape(GROUP, 32, 128)], 1)
 
 
 def unpack_heads(packed_ref):
@@ -99,12 +113,11 @@
     return jnp.concatenate(rows, 0).astype(bf16)
 
 
-def pack_heads(array, out_ref):
-    zeros = jnp.zeros((PACK, HD), f32)
+def pack_heads(array, factors, out_ref):
+    factors = factors.astype(f32)
     for h in range(HEADS):
-        out_ref[h] = jnp.concatenate(
-            [lane_slice(array[r * PACK : (r + 1) * PACK], h * HD) for r in range(ROWS_DEV)] + [zeros], 1
-        ).astype(bf16)
+        parts = [lane_slice(array[r * PACK : (r + 1) * PACK], h * HD) for r in range(ROWS_DEV)]
+        out_ref[h] = jnp.concatenate(parts + [lane_slice(factors, h * HD)], 1).astype(bf16)
 
 
 def to_windows(array):
@@ -187,7 +200,7 @@
     out_ref = refs[-1]
     lane = iota((CELLS, 128), 1)
     per_window = []
-    for w, cells in enumerate(to_windows(x_ref[...].astype(f32))):
+    for w, cells in enumerate(to_windows(unpack_cells(x_ref))):
         query = cells[:, :HD].astype(bf16)
         key = cells[:, HD : 2 * HD].astype(bf16)
         value = jnp.where(lane < HD, pltpu.roll(cells, 64, 1), jnp.where(lane == HD, 1.0, 0.0)).astype(bf16)
@@ -209,17 +222,23 @@
     lane = iota((CELLS, 128), 1)
     low = iota((HD, CELLS), 0)
     scale_row = jnp.exp(jnp.full((1, 128), scale_ref[block, head_ref[0]], f32))
+    unscale_row = 1.0 / scale_row
     packed = grad_ref[...].astype(f32).reshape(GROUP * PACK, 128)
-    rolled = [packed if r == 0 else pltpu.roll(packed, 128 - r * HD, 1) for r in range(ROWS_DEV)]
+    low_lane = iota(packed.shape, 1) < HD
+    rolled = [packed] + [
+        jnp.where(low_lane, pltpu.roll(packed, 128 - r * HD, 1), pltpu.roll(packed, 128 - r * 4, 1))
+        for r in range(1, ROWS_DEV)
+    ]
     rolled = [part.reshape(GROUP, 1, 2, WIN, 128) for part in rolled]
     grads = jnp.concatenate(rolled, 1)
     results = []
-    for w, cells in enumerate(to_windows(x_ref[...].astype(f32))):
+    for w, cells in enumerate(to_windows(unpack_cells(x_ref))):
         turned = cells.T
         query_t = turned[:HD].astype(bf16)
         key_t = turned[HD : 2 * HD].astype(bf16)
         value_t = turned[2 * HD : 3 * HD]
-        grad_t = grads[:, :, w].reshape(CELLS, 128).T[:HD]
+        grad = grads[:, :, w].reshape(CELLS, 128)
+        grad_t = grad.T[:HD]
         key = cells[:, HD : 2 * HD].astype(bf16)
         scores = masked(dot(key, query_t), w, mask_refs)
         weights = jnp.exp(scores).astype(bf16)
@@ -239,33 +258,35 @@
         grad_q = dot(key_t, grad_scores)
         grad_q = jnp.concatenate([grad_q, zeros, zeros, zeros], 0).T
         total = jnp.where(lane < HD, grad_q * scale_row, grad_kv)
-        unit = jnp.where(lane < HD, cells / scale_row, jnp.where(lane < 2 * HD, cells, 0.0))
-        q_factor = cells[:, 96:97] + cells[:, 97:98]
-        k_factor = cells[:, 98:99] + cells[:, 99:100]
+        unit = jnp.where(lane < HD, cells * unscale_row, jnp.where(lane < 2 * HD, cells, 0.0))
+        q_factor = grad[:, 96:97] + grad[:, 97:98]
+        k_factor = grad[:, 98:99] + grad[:, 99:100]
         factor = jnp.where(lane < HD, q_factor, jnp.where(lane < 2 * HD, k_factor, 1.0))
         results.append(factor * (total - unit * head_sums(unit * total)))
     out_ref[...] = pack_cells(from_windows(results)).astype(bf16)
 
 
-def first_kernel(tokens_ref, w_ref, scale_ref, out_ref):
-    send_projected(tokens_ref[...], w_ref[...], scale_ref, 0, out_ref)
-
-
-def middle_kernel(packed_ref, scale_ref, gain_ref, bias_ref, tokens_ref, w_proj_ref, w_ref, out_ref, rolled_ref):
+def first_kernel(tokens_ref, w_ref, scale_ref, out_ref, factors_ref):
+    send_projected(tokens_ref[...], w_ref[...], scale_ref, 0, out_ref, factors_ref)
+
+
+def middle_kernel(packed_ref, scale_ref, gain_ref, bias_ref, tokens_ref, w_proj_ref, w_ref, out_ref, rolled_ref, factors_ref):
     attended = unpack_heads(packed_ref)
     y_hat, _ = normalized(attended, w_proj_ref[...])
     out = (tokens_ref[...].astype(f32) + y_hat * gain_ref[0:1] + bias_ref[0:1]).astype(bf16).astype(f32)
     rolled = roll_tokens(out, -SHIFT).astype(bf16)
     rolled_ref[...] = rolled
-    send_projected(rolled, w_ref[...], scale_ref, 1, out_ref)
-
-
-def turn_kernel(packed_ref, gain_ref, grad_ref, w_proj_ref, out_ref, grad_proj_ref, gains_ref):
+    send_projected(rolled, w_ref[...], scale_ref, 1, out_ref, factors_ref)
+
+
+def turn_kernel(core_ref, packed_ref, gain_ref, grad_ref, w_proj_ref, factors_ref, out_ref, kept_ref, given_ref, gains_ref):
     attended = unpack_heads(packed_ref)
     grad = roll_tokens(grad_ref[...].astype(f32), -SHIFT)
     grad_y, grad_att, gains = finish_back(attended, w_proj_ref[...], gain_ref[1:2], grad)
-    pack_heads(grad_att, out_ref)
-    grad_proj_ref[...] = dot_0(grad_y, attended).astype(bf16)
+    pack_heads(grad_att, factors_ref[...], out_ref)
+    kept, given = halves(attended, core_ref[0])
+    kept_ref[...] = dot_0(grad_y, kept).astype(bf16)
+    given_ref[...] = dot_0(grad_y, given).astype(bf16)
     gains_ref[...] = gains
 
 
@@ -276,11 +297,10 @@
     return jnp.concatenate([jnp.concatenate(top, 1), jnp.concatenate(tail, 1)], 0).astype(bf16)
 
 
-def give(array, side, kept_ref, given_ref):
+def halves(array, core):
     half = array.shape[1] // 2
-    left, right = array[:, :half], array[:, half:]
-    kept_ref[...] = jnp.where(side == 0, left, right).astype(bf16)
-    given_ref[...] = jnp.where(side == 0, right, left).astype(bf16)
+    left, right = array[:, :half].astype(f32), array[:, half:].astype(f32)
+    return jnp.where(core == 0, left, right).astype(bf16), jnp.where(core == 0, right, left).astype(bf16)
 
 
 def back_kernel(
@@ -291,8 +311,10 @@
     w_ref,
     w_proj_ref,
     grad_ref,
-    proj1_ref,
+    proj1_kept_ref,
+    proj1_given_ref,
     tokens_ref,
+    factors_ref,
     out_ref,
     gains_ref,
     grad0_ref,
@@ -305,10 +327,16 @@
     grad0_ref[...] = grad
     attended = unpack_heads(packed_ref)
     grad_y, grad_att, gains = finish_back(attended, w_proj_ref[...], gain_ref[0:1], grad.astype(f32))
-    pack_heads(grad_att, out_ref)
-    parts = [dot_0(tokens_ref[...], d_qkv), proj1_ref[...].astype(f32), dot_0(grad_y, attended)]
-    early = jnp.concatenate(parts, 1)
-    give(early, core_ref[0], kept_ref, given_ref)
+    sides = zip(halves(d_qkv, core_ref[0]), (proj1_kept_ref, proj1_given_ref), halves(attended, core_ref[0]))
+    kept, given = [
+        jnp.concatenate(
+            [dot_0(tokens_ref[...], part).astype(bf16), proj1_ref[...], dot_0(grad_y, att).astype(bf16)], 1
+        )
+        for part, proj1_ref, att in sides
+    ]
+    kept_ref[...] = kept
+    given_ref[...] = given
+    pack_heads(grad_att, factors_ref[...], out_ref)
     gains_ref[...] = gains
 
 
@@ -316,27 +344,40 @@
     out_ref[...] = (grad_ref[...].astype(f32) + dot_t(gather_qkv(qkv_ref), w_ref[...])).astype(bf16)
 
 
-def last_kernel(qkv_ref, tokens_ref, got_ref, gains0_ref, gains1_ref, kept_ref, parts_ref):
-    d_qkv = gather_qkv(qkv_ref)
+def last_kernel(core_ref, qkv_ref, tokens_ref, kept_ref, given_ref):
+    kept, given = halves(gather_qkv(qkv_ref), core_ref[0])
+    given_ref[...] = dot_0(tokens_ref[...], given).astype(bf16)
+    kept_ref[...] = dot_0(tokens_ref[...], kept).astype(bf16)
+
+
+def parts_kernel(late_ref, got_late_ref, got_ref, gains0_ref, gains1_ref, kept_ref, parts_ref):
     pieces = []
     for ref in (gains0_ref, gains1_ref):
         for row in (0, 1):
             pieces += split_two(ref[row : row + 1])
-    pieces.append(jnp.zeros((128 - len(pieces), C), f32))
-    gains = jnp.concatenate(pieces, 0).T
+    gains = jnp.concatenate(pieces + [jnp.zeros((16 - len(pieces), C), f32)], 0)
+    depth = C // 8
+    for ring in range(8):
+        block = gains[:, ring // 2 * 128 : ring // 2 * 128 + 128]
+        block = pltpu.roll(block, depth, 1) if ring % 2 else block
+        parts_ref[ring, TILES * depth :] = block.astype(bf16)
+    late = late_ref[...].astype(f32) + got_late_ref[...].astype(f32)
     early = kept_ref[...].astype(f32) + got_ref[...].astype(f32)
     tile = 0
-    for part in (dot_0(tokens_ref[...], d_qkv), early, gains):
+    for part in (late, early):
         for at in range(0, part.shape[1], 128):
-            block = part[:, at : at + 128].astype(bf16).reshape(8, C // 8, 128)
-            parts_ref[:, tile * (C // 8) : (tile + 1) * (C // 8), :] = block
+            block = part[:, at : at + 128].astype(bf16).reshape(8, depth, 128)
+            parts_ref[:, tile * depth : (tile + 1) * depth, :] = block
             tile += 1
 
 
 def first_sum_kernel(parts_ref, out_ref):
-    total = jnp.sum(parts_ref[...].astype(f32), 0).reshape(TILES, 8, 8, 128)
-    for ring in range(8):
-        out_ref[ring] = total[:, ring].reshape(TILES * 8, 128).astype(bf16)
+    total = jnp.sum(parts_ref[...].astype(f32), 0)
+    gains = total[TILES * C // 8 :]
+    total = total[: TILES * C // 8].reshape(TILES, 8, 8, 128)
+    for place in range(8):
+        rolled = pltpu.roll(gains, 128 - 8 * place, 1) if place else gains
+        out_ref[place] = jnp.concatenate([total[:, place].reshape(TILES * 8, 128), rolled], 0).astype(bf16)
 
 
 def second_sum_kernel(parts_ref, out_ref):
@@ -348,17 +389,15 @@
 
 
 def final_kernel(core_ref, own_ref, other_ref, qkv_ref, proj_ref, gain_ref, bias_ref):
-    own = own_ref[...].reshape(TILES, 8, 128)
-    other = other_ref[...].reshape(TILES, 8, 128)
-    both = own + other
+    own = own_ref[: TILES * 8].reshape(TILES, 8, 128)
+    other = other_ref[: TILES * 8].reshape(TILES, 8, 128)
     first = core_ref[0] == 0
     left, right = jnp.where(first, own, other), jnp.where(first, other, own)
-    tiles = [left[i] for i in range(6, 11)] + [right[i] for i in range(6, 11)]
-    qkv_ref[0] = jnp.concatenate([both[i] for i in range(6)], 1)
-    qkv_ref[1] = jnp.concatenate(tiles[:6], 1)
-    proj_ref[1] = jnp.concatenate(tiles[6:8], 1)
-    proj_ref[0] = jnp.concatenate(tiles[8:], 1)
-    gains = both[11].T
+    for block, tiles in ((0, (0, 1, 2)), (1, (3, 4, 5))):
+        qkv_ref[block] = jnp.concatenate([side[i] for side in (left, right) for i in tiles], 1)
+    proj_ref[1] = jnp.concatenate([left[6], right[6]], 1)
+    proj_ref[0] = jnp.concatenate([left[7], right[7]], 1)
+    gains = (own_ref[TILES * 8 :] + other_ref[TILES * 8 :])[:, :8]
     gain_ref[...] = jnp.concatenate([gains[0:1] + gains[1:2], gains[4:5] + gains[5:6]], 0)
     bias_ref[...] = jnp.concatenate([gains[2:3] + gains[3:4], gains[6:7] + gains[7:8]], 0)
 
@@ -478,33 +517,39 @@
 
     tokens0 = image.reshape(TOK, C)
     grad_out = out_grad.reshape(TOK, C)
-    wide = ((GROUP, TOK, 128), bf16)
     short = ((GROUP, SHORT, 128), bf16)
+    factors = ((PACK, HH), bf16)
     narrow = ((GROUP, PACK, 128), bf16)
     cells = ((TOK, C), bf16)
-    proj = ((C, HH), bf16)
+    proj = ((C, HH // 2), bf16)
     gains = ((8, C), f32)
     half_early = ((C, EARLY // 2), bf16)
+    half_late = ((C, LATE // 2), bf16)
 
     def swap(array, apart):
         return lax.ppermute(array, "dp", [(i, i ^ apart) for i in range(4)])
 
-    (x0,) = call(first_kernel, [wide], (), (), fetched=(tokens0, (w_qkv, 0), logit_scale))
+    x0, factors0 = call(
+        first_kernel, [short], (), (), fetched=(tokens0, (w_qkv, 0), logit_scale), stored=[factors]
+    )
     x0 = exchange(x0, aligned)
     (a0,) = call(functools.partial(attend_kernel, False), [narrow], (), (x0,))
     a0 = exchange(a0, aligned)
-    x1, tokens1 = call(
+    x1, tokens1, factors1 = call(
         middle_kernel,
-        [wide],
+        [short],
         (),
         (a0, logit_scale, norm_gain, norm_bias, tokens0, (w_proj, 0), (w_qkv, 1)),
-        stored=[cells],
+        stored=[cells, factors],
     )
     x1 = exchange(x1, moved)
     (a1,) = call(functools.partial(attend_kernel, True), [narrow], (), (x1,), masks)
     a1 = exchange(a1, moved)
-    d1, proj1, gains1 = call(
-        turn_kernel, [narrow, proj, gains], (), (a1, norm_gain, grad_out, (w_proj, 1))
+    d1, proj1_kept, proj1_given, gains1 = call(
+        turn_kernel,
+        [narrow, proj, proj, gains],
+        (core,),
+        (a1, norm_gain, grad_out, (w_proj, 1), factors1),
     )
     d1 = exchange(d1, moved)
     (qkv1,) = call(
@@ -515,26 +560,27 @@
         back_kernel,
         [narrow, gains],
         (core,),
-        (qkv1, a0, norm_gain, (w_qkv, 1), (w_proj, 0), grad_out, proj1),
-        fetched=(tokens1,),
+        (qkv1, a0, norm_gain, (w_qkv, 1), (w_proj, 0), grad_out, proj1_kept, proj1_given, tokens1, factors0),
         stored=[cells, half_early, half_early],
     )
-    d0, got = lax.optimization_barrier((d0, swap(given, 1)))
     d0 = exchange(d0, aligned)
     (qkv0,) = call(functools.partial(attend_back_kernel, 0, False), [short], (head0, logit_scale), (x0, d0))
     qkv0 = exchange(qkv0, aligned)
+    qkv0, given = lax.optimization_barrier((qkv0, given))
+    got = swap(given, 1)
+    late, given_late = call(last_kernel, [half_late, half_late], (core,), (qkv0, tokens0))
+    got_late = swap(given_late, 1)
     (parts,) = call(
-        last_kernel,
-        [((8, TILES * C // 8, 128), bf16)],
+        parts_kernel,
+        [((8, SENT, 128), bf16)],
         (),
-        (qkv0, tokens0, got, gains0, gains1),
-        fetched=(kept,),
+        (late, got_late, got, gains0, gains1, kept),
     )
     parts = exchange(parts, across)
-    (parts,) = call(first_sum_kernel, [((8, TILES * 8, 128), bf16)], (), (parts,))
+    (parts,) = call(first_sum_kernel, [((8, SHARE, 128), bf16)], (), (parts,))
     parts = exchange(parts, aligned)
-    (share,) = call(second_sum_kernel, [((TILES * 8, 128), f32)], (), (parts,))
-    (share,) = call(add_kernel, [((TILES * 8, 128), f32)], (), (share, swap(share, 2)))
+    (share,) = call(second_sum_kernel, [((SHARE, 128), f32)], (), (parts,))
+    (share,) = call(add_kernel, [((SHARE, 128), f32)], (), (share, swap(share, 2)))
     other = swap(share, 1)
     qkv0, _ = lax.optimization_barrier((qkv0, share))
     (grad_image,) = call(image_kernel, [cells], (), (qkv0, (w_qkv, 0), grad0))

time: 186 us -> 181 us (0.973)
  blocking collectives: 140 us -> 136 us
    all_to_all x10, blocking collectives: 140 us -> 136 us  [exchange(): lax.all_to_all(array, 'rows', 0, 0, axis_index_groups=groups, tiled=True)]
    pallas_call x14 -> x15, Pallas kernels: 23.3 us -> 22.1 us  [call(): pl.pallas_call(wrapped, out_shape=[jax.ShapeDtypeStruct(*out) for out in...]
    ppermute x3 -> x4, waiting for transfers between devices: 3.93 us -> 3.45 us  [swap(): return lax.ppermute(array, 'dp', [(i, i ^ apart) for i in range(4)])]
    ppermute x3 -> x4, starting transfers between devices: 17.6 us -> 17.4 us  [swap(): return lax.ppermute(array, 'dp', [(i, i ^ apart) for i in range(4)])]
  transfers between devices with their start and end apart: 3 -> 4, of which waited for: 2 -> 2; matrix products, arithmetic and copies ran while one was open for 0% -> 0% of each run, Pallas kernels for 1% -> 1%
where the time goes in v5:
time: 181 us
  blocking collectives  136 us (75%)
  Pallas kernels  22.1 us (12%)
  starting transfers between devices  17.4 us (10%)
  waiting for transfers between devices  3.45 us (2%)
    all_to_all x10, blocking collectives, exchange(): lax.all_to_all(array, 'rows', 0, 0, axis_index_groups=groups, tiled=True)  136 us
    pallas_call x15, Pallas kernels, call(): pl.pallas_call(wrapped, out_shape=[jax.ShapeDtypeStruct(*out) for out in...  22.1 us
    ppermute x4, starting transfers between devices, swap(): return lax.ppermute(array, 'dp', [(i, i ^ apart) for i in range(4)])  17.4 us
  transfers between devices with their start and end apart: 4, of which 2 were waited for; matrix products, arithmetic and copies ran while one was open for 0% of the time, Pallas kernels for 1%

profile of v5, /device:TPU:1, one launch (start us, length us, event | category | flops | bytes accessed | tf_op | source)
XLA Modules:
  0.0 180.7 jit_solution(10955779976913375235)
XLA Ops:
  0.7 0.0 copy-start
  0.7 0.0 copy-start.1
  0.7 0.0 copy-start.2
  0.7 0.0 copy-start.7
  0.7 0.0 copy-start.10
  0.7 0.0 copy-start.11
  0.7 2.7 %shard_map.128 = (bf16[8,112,128]{2,1,0:T(8,128)(2,1)S(1)}, bf16[48,256]{1,0:T(8,128)(2,1)}) custom-call(bf16[144,512]{1,0:T(8,128)(2,1)} %bitcast.10, bf16[2,512,768]{2,1,0:T(8,128)(2,1)} %refs_1_.9, f32[2,8]{1,0:T(2,128)} %refs_1_.8), custom_call_target="tpu_custom_call" | custom-call | tf_op jit(solution)/shard_map/pallas_call | solution.py:482
  3.4 18.6 %all_to_all.50.refs_0_.refs_2_ = bf16[8,112,128]{2,1,0:T(8,128)(2,1)S(1)} all-to-all(bf16[8,112,128]{2,1,0:T(8,128)(2,1)S(1)} %get-tuple-element.35), channel_id=1, replica_groups={{0,1,2,3,4,5,6,7},{8,9,10,11,12,13,14,15},{16,17,18,19,20,21,22,23},{24..., dimensions={0} | all-to-all | bytes 458752 | tf_op jit(solution)/shard_map/all_to_all | solution.py:516
  22.0 1.3 shard_map.129
  23.3 10.2 %all_to_all.51.refs_0_.refs_2_ = bf16[8,48,128]{2,1,0:T(8,128)(2,1)S(1)} all-to-all(bf16[8,48,128]{2,1,0:T(8,128)(2,1)S(1)} %shard_map.129), channel_id=1, replica_groups={{0,1,2,3,4,5,6,7},{8,9,10,11,12,13,14,15},{16,17,18,19,20,21,22,23},{24..., dimensions={0} | all-to-all | bytes 196608 | tf_op jit(solution)/shard_map/all_to_all | solution.py:516
  33.5 0.0 copy-done
  33.5 0.0 copy-done.1
  33.5 0.0 copy-done.2
  33.5 0.0 copy-done.7
  33.5 0.0 copy-done.10
  33.5 0.0 copy-done.11
  33.5 0.0 copy-start.12
  33.6 0.0 copy-start.13
  33.6 1.5 shard_map.130
  35.1 0.0 copy-start.4
  35.1 13.5 %all_to_all.52.refs_0_.refs_2_ = bf16[8,112,128]{2,1,0:T(8,128)(2,1)S(1)} all-to-all(bf16[8,112,128]{2,1,0:T(8,128)(2,1)S(1)} %get-tuple-element.38), channel_id=1, replica_groups={{4,5,6,7,8,9,10,11},{12,13,14,15,16,17,18,19},{20,21,22,23,24,25,26,27}..., dimensions={0} | all-to-all | bytes 458752 | tf_op jit(solution)/shard_map/all_to_all | solution.py:516
  48.6 0.0 copy-done.12
  48.6 0.0 copy-done.13
  48.6 2.0 %shard_map.131 = bf16[8,48,128]{2,1,0:T(8,128)(2,1)S(1)} custom-call(bf16[8,112,128]{2,1,0:T(8,128)(2,1)S(1)} %all_to_all.52.refs_0_.refs_2_, s32[1]{0:T(128)} %bitcast.2.refs_1_.refs_4_, s32[1,192]{1,0:T(1,128)S(1)} %bitcast.15, s32[1,48]{1,0:T(1,128)S(1)} %bitcast.17), custom_call_target="tpu_custom_call" | custom-call | tf_op jit(solution)/shard_map/pallas_call | solution.py:482
  50.6 0.0 copy-start.6
  50.6 0.0 copy-start.8
  50.6 12.1 %all_to_all.53.refs_1_ = bf16[8,48,128]{2,1,0:T(8,128)(2,1)S(1)} all-to-all(bf16[8,48,128]{2,1,0:T(8,128)(2,1)S(1)} %shard_map.131), channel_id=1, replica_groups={{4,5,6,7,8,9,10,11},{12,13,14,15,16,17,18,19},{20,21,22,23,24,25,26,27}..., dimensions={0} | all-to-all | bytes 196608 | tf_op jit(solution)/shard_map/all_to_all | solution.py:516
  62.6 0.0 copy-done.4
  62.7 0.0 copy-start.9
  62.7 0.7 copy-done.9
  63.4 0.9 shard_map.132
  64.3 12.4 %all_to_all.54.refs_3_ = bf16[8,48,128]{2,1,0:T(8,128)(2,1)S(1)} all-to-all(bf16[8,48,128]{2,1,0:T(8,128)(2,1)S(1)} %get-tuple-element.41), channel_id=1, replica_groups={{4,5,6,7,8,9,10,11},{12,13,14,15,16,17,18,19},{20,21,22,23,24,25,26,27}..., dimensions={0} | all-to-all | bytes 196608 | tf_op jit(solution)/shard_map/all_to_all | solution.py:516
  76.7 4.4 %shard_map.133 = bf16[8,112,128]{2,1,0:T(8,128)(2,1)S(1)} custom-call(s32[1]{0:T(128)} %bitcast.1.refs_0_, f32[2,8]{1,0:T(2,128)S(1)} %copy-done.10, bf16[8,112,128]{2,1,0:T(8,128)(2,1)S(1)} %all_to_all.52.refs_0_.refs_2_, bf16[8,48,128]{2,1,0:T(8,128)(2,1)S(1)} %all_to_all.54.refs_3_, s32[1]{0:T(128)} %bitcast.2.refs_1_.refs_4_, s32[1,192]{1,0:T(1,128)S(1)} %bitcast.16, ...), custom_call_target="tpu_custom_call" | custom-call | tf_op jit(solution)/shard_map/pallas_call | solution.py:482
  81.1 13.9 %all_to_all.55.refs_1_ = bf16[8,112,128]{2,1,0:T(8,128)(2,1)S(1)} all-to-all(bf16[8,112,128]{2,1,0:T(8,128)(2,1)S(1)} %shard_map.133), channel_id=1, replica_groups={{4,5,6,7,8,9,10,11},{12,13,14,15,16,17,18,19},{20,21,22,23,24,25,26,27}..., dimensions={0} | all-to-all | bytes 458752 | tf_op jit(solution)/shard_map/all_to_all | solution.py:516
  95.0 0.0 copy-done.6
  95.0 0.0 copy-done.8
  95.0 2.4 %shard_map.134 = (bf16[8,48,128]{2,1,0:T(8,128)(2,1)S(1)}, f32[8,512]{1,0:T(8,128)S(1)}, bf16[144,512]{1,0:T(8,128)(2,1)}, bf16[512,640]{1,0:T(8,128)(2,1)}, bf16[512,640]{1,0:T(8,128)(2,1)}) custom-call(s32[1]{0:T(128)} %bitcast.3.refs_0_, bf16[8,112,128]{2,1,0:T(8,128)(2,1)S(1)} %all_to_all.55.refs_1_, bf16[8,48,128]{2,1,0:T(8,128)(2,1)S(1)} %all_to_all.51.refs_0_.refs_2_, ...), custom_call_target="tpu_custom_call" | custom-call | tf_op jit(solution)/shard_map/pallas_call | solution.py:482
  97.4 0.0 copy-start.3
  97.4 10.8 %all_to_all.56.refs_3_ = bf16[8,48,128]{2,1,0:T(8,128)(2,1)S(1)} all-to-all(bf16[8,48,128]{2,1,0:T(8,128)(2,1)S(1)} %get-tuple-element.46), channel_id=1, replica_groups={{0,1,2,3,4,5,6,7},{8,9,10,11,12,13,14,15},{16,17,18,19,20,21,22,23},{24..., dimensions={0} | all-to-all | bytes 196608 | tf_op jit(solution)/shard_map/all_to_all | solution.py:516
  108.2 3.9 %shard_map.135 = bf16[8,112,128]{2,1,0:T(8,128)(2,1)S(1)} custom-call(s32[1]{0:T(128)} %bitcast.refs_0_, f32[2,8]{1,0:T(2,128)S(1)} %copy-done.10, bf16[8,112,128]{2,1,0:T(8,128)(2,1)S(1)} %all_to_all.50.refs_0_.refs_2_, bf16[8,48,128]{2,1,0:T(8,128)(2,1)S(1)} %all_to_all.56.refs_3_), custom_call_target="tpu_custom_call" | custom-call | tf_op jit(solution)/shard_map/pallas_call | solution.py:482
  112.1 11.4 %all_to_all.57.refs_1_.refs_0_ = bf16[8,112,128]{2,1,0:T(8,128)(2,1)S(1)} all-to-all(bf16[8,112,128]{2,1,0:T(8,128)(2,1)S(1)} %shard_map.135), channel_id=1, replica_groups={{0,1,2,3,4,5,6,7},{8,9,10,11,12,13,14,15},{16,17,18,19,20,21,22,23},{24..., dimensions={0} | all-to-all | bytes 458752 | tf_op jit(solution)/shard_map/all_to_all | solution.py:516
  123.4 10.8 %collective-permute-start.1 = (bf16[512,640]{1,0:T(8,128)(2,1)}, bf16[512,640]{1,0:T(8,128)(2,1)S(1)}, u32[]{:S(2)}, u32[]{:S(2)}) collective-permute-start(bf16[512,640]{1,0:T(8,128)(2,1)} %get-tuple-element.51), channel_id=1, source_target_pairs={{0,64},{64,0},{128,192},{192,128},{1,65},{65,1},{129,193},{193,129... | collective-permute-start | bytes 1966088 | tf_op jit(solution)/shard_map/ppermute | solution.py:530
  134.3 0.7 shard_map.136
  134.9 0.1 collective-permute-start
  135.0 1.7 collective-permute-done.refs_1_
  136.8 0.0 collective-permute-done.1.refs_2_
  136.8 0.0 copy-done.3
  136.8 0.4 shard_map.137
  137.2 22.8 %all_to_all.58.refs_0_ = bf16[8,528,128]{2,1,0:T(8,128)(2,1)S(1)} all-to-all(bf16[8,528,128]{2,1,0:T(8,128)(2,1)S(1)} %shard_map.137), channel_id=1, replica_groups={{0,8,16,24,32,40,48,56},{1,9,17,25,33,41,49,57},{2,10,18,26,34,42,50,58..., dimensions={0} | all-to-all | bytes 2162688 | tf_op jit(solution)/shard_map/all_to_all | solution.py:516
  159.9 0.0 copy-start.5
  159.9 0.2 shard_map.138
  160.2 10.6 %all_to_all.59.refs_0_ = bf16[8,80,128]{2,1,0:T(8,128)(2,1)S(1)} all-to-all(bf16[8,80,128]{2,1,0:T(8,128)(2,1)S(1)} %shard_map.138), channel_id=1, replica_groups={{0,1,2,3,4,5,6,7},{8,9,10,11,12,13,14,15},{16,17,18,19,20,21,22,23},{24..., dimensions={0} | all-to-all | bytes 327680 | tf_op jit(solution)/shard_map/all_to_all | solution.py:516
  170.8 2.7 %collective-permute-start.2 = (f32[80,128]{1,0:T(8,128)S(1)}, f32[80,128]{1,0:T(8,128)S(1)}, u32[]{:S(2)}, u32[]{:S(2)}) collective-permute-start(f32[80,128]{1,0:T(8,128)S(1)} %shard_map.139.refs_0_), channel_id=1, source_target_pairs={{0,128},{64,192},{128,0},{192,64},{1,129},{65,193},{129,1},{193,65... | collective-permute-start | bytes 122888 | tf_op jit(solution)/shard_map/ppermute | solution.py:530
  173.5 1.7 collective-permute-done.2.refs_1_
  175.2 3.8 %collective-permute-start.3 = (f32[80,128]{1,0:T(8,128)S(1)}, f32[80,128]{1,0:T(8,128)S(1)}, u32[]{:S(2)}, u32[]{:S(2)}) collective-permute-start(f32[80,128]{1,0:T(8,128)S(1)} %shard_map.140.refs_1_), channel_id=1, source_target_pairs={{0,64},{64,0},{128,192},{192,128},{1,65},{65,1},{129,193},{193,129... | collective-permute-start | bytes 122888 | tf_op jit(solution)/shard_map/ppermute | solution.py:530
  179.0 0.0 copy-done.5
  179.0 1.1 shard_map.141
  180.1 0.0 collective-permute-done.3.refs_2_
  180.1 0.6 shard_map.142
  (2 shorter events, 0.0 us)
Async XLA Ops:
  0.7 32.8 %copy-start = (bf16[2,512,768]{2,1,0:T(8,128)(2,1)S(1)}, bf16[2,512,768]{2,1,0:T(8,128)(2,1)}, u32[]{:S(2)}) copy-start(bf16[2,512,768]{2,1,0:T(8,128)(2,1)} %refs_1_.9) | copy-start | bytes 4718596
  0.7 32.8 %copy-start.1 = (bf16[2,256,512]{2,1,0:T(8,128)(2,1)S(1)}, bf16[2,256,512]{2,1,0:T(8,128)(2,1)}, u32[]{:S(2)}) copy-start(bf16[2,256,512]{2,1,0:T(8,128)(2,1)} %refs_5_.3) | copy-start | bytes 1572868
  0.7 32.8 %copy-start.2 = (bf16[1,3,48,512]{3,2,1,0:T(8,128)(2,1)S(1)}, bf16[1,3,48,512]{3,2,1,0:T(8,128)(2,1)}, u32[]{:S(2)}) copy-start(bf16[1,3,48,512]{3,2,1,0:T(8,128)(2,1)} %param.9) | copy-start | bytes 442372
  0.7 32.8 %copy-start.7 = (f32[2,512]{1,0:T(2,128)S(1)}, f32[2,512]{1,0:T(2,128)}, u32[]{:S(2)}) copy-start(f32[2,512]{1,0:T(2,128)} %refs_3_.3) | copy-start | bytes 12292
  0.7 32.8 %copy-start.10 = (f32[2,8]{1,0:T(2,128)S(1)}, f32[2,8]{1,0:T(2,128)}, u32[]{:S(2)}) copy-start(f32[2,8]{1,0:T(2,128)} %refs_1_.8) | copy-start | bytes 196
  0.7 32.8 %copy-start.11 = (f32[2,512]{1,0:T(2,128)S(1)}, f32[2,512]{1,0:T(2,128)}, u32[]{:S(2)}) copy-start(f32[2,512]{1,0:T(2,128)} %refs_3_.2) | copy-start | bytes 12292
  33.5 15.0 %copy-start.12 = (s32[192]{0:T(256)S(1)}, s32[192]{0:T(256)}, u32[]{:S(2)}) copy-start(s32[192]{0:T(256)} %param.16) | copy-start | bytes 2308
  33.6 15.0 %copy-start.13 = (s32[48]{0:T(128)S(1)}, s32[48]{0:T(128)}, u32[]{:S(2)}) copy-start(s32[48]{0:T(128)} %param.17) | copy-start | bytes 580
  35.1 27.6 %copy-start.4 = (bf16[1,3,48,512]{3,2,1,0:T(8,128)(2,1)S(1)}, bf16[1,3,48,512]{3,2,1,0:T(8,128)(2,1)}, u32[]{:S(2)}) copy-start(bf16[1,3,48,512]{3,2,1,0:T(8,128)(2,1)} %param.10) | copy-start | bytes 442372
  50.6 44.4 %copy-start.6 = (bf16[144,512]{1,0:T(8,128)(2,1)S(1)}, bf16[144,512]{1,0:T(8,128)(2,1)}, u32[]{:S(2)}) copy-start(bf16[144,512]{1,0:T(8,128)(2,1)} %get-tuple-element.44.refs_9_) | copy-start | bytes 442372
  50.6 44.4 %copy-start.8 = (bf16[48,256]{1,0:T(8,128)(2,1)S(1)}, bf16[48,256]{1,0:T(8,128)(2,1)}, u32[]{:S(2)}) copy-start(bf16[48,256]{1,0:T(8,128)(2,1)} %get-tuple-element.45.refs_10_) | copy-start | bytes 73732
  62.7 0.7 copy-start.9
  97.4 39.4 %copy-start.3 = (bf16[512,640]{1,0:T(8,128)(2,1)S(1)}, bf16[512,640]{1,0:T(8,128)(2,1)}, u32[]{:S(2)}) copy-start(bf16[512,640]{1,0:T(8,128)(2,1)} %get-tuple-element.54.refs_5_) | copy-start | bytes 1966084
  123.4 13.3 %collective-permute-start.1 = (bf16[512,640]{1,0:T(8,128)(2,1)}, bf16[512,640]{1,0:T(8,128)(2,1)S(1)}, u32[]{:S(2)}, u32[]{:S(2)}) collective-permute-start(bf16[512,640]{1,0:T(8,128)(2,1)} %get-tuple-element.51), channel_id=1, source_target_pairs={{0,64},{64,0},{128,192},{192,128},{1,65},{65,1},{129,193},{193,129... | collective-permute-start | bytes 1966088 | tf_op jit(solution)/shard_map/ppermute | solution.py:530
  134.9 1.8 %collective-permute-start = (bf16[512,384]{1,0:T(8,128)(2,1)S(1)}, bf16[512,384]{1,0:T(8,128)(2,1)S(1)}, u32[]{:S(2)}, u32[]{:S(2)}) collective-permute-start(bf16[512,384]{1,0:T(8,128)(2,1)S(1)} %get-tuple-element.50), channel_id=1, source_target_pairs={{0,64},{64,0},{128,192},{192,128},{1,65},{65,1},{129,193},{193,129... | collective-permute-start | bytes 1179656 | tf_op jit(solution)/shard_map/ppermute | solution.py:530
  159.9 19.1 %copy-start.5 = (bf16[144,512]{1,0:T(8,128)(2,1)S(1)}, bf16[144,512]{1,0:T(8,128)(2,1)}, u32[]{:S(2)}) copy-start(bf16[144,512]{1,0:T(8,128)(2,1)} %get-tuple-element.56.refs_2_) | copy-start | bytes 442372
  170.8 4.4 %collective-permute-start.2 = (f32[80,128]{1,0:T(8,128)S(1)}, f32[80,128]{1,0:T(8,128)S(1)}, u32[]{:S(2)}, u32[]{:S(2)}) collective-permute-start(f32[80,128]{1,0:T(8,128)S(1)} %shard_map.139.refs_0_), channel_id=1, source_target_pairs={{0,128},{64,192},{128,0},{192,64},{1,129},{65,193},{129,1},{193,65... | collective-permute-start | bytes 122888 | tf_op jit(solution)/shard_map/ppermute | solution.py:530
  175.2 4.9 %collective-permute-start.3 = (f32[80,128]{1,0:T(8,128)S(1)}, f32[80,128]{1,0:T(8,128)S(1)}, u32[]{:S(2)}, u32[]{:S(2)}) collective-permute-start(f32[80,128]{1,0:T(8,128)S(1)} %shard_map.140.refs_1_), channel_id=1, source_target_pairs={{0,64},{64,0},{128,192},{192,128},{1,65},{65,1},{129,193},{193,129... | collective-permute-start | bytes 122888 | tf_op jit(solution)/shard_map/ppermute | solution.py:530

commit v6 on v5

--- a/solution.py
+++ b/solution.py
@@ -28,7 +28,6 @@
 SHARE = TILES * 8 + 16
 
 norm_eps = 1e-05
-mask_value = 100.0
 f32 = jnp.float32
 bf16 = jnp.bfloat16
 
@@ -66,7 +65,7 @@
     return x[:, at : at + HD]
 
 
-def send_projected(tokens, weight, scale_ref, block, out_ref, factors_ref):
+def send_projected(tokens, weight, scale_ref, block, out_ref):
     projected = dot(tokens, weight)
     query, key, value = projected[:, :HH], projected[:, HH : 2 * HH], projected[:, 2 * HH :]
     lane = iota((1, HH), 1)
@@ -76,20 +75,16 @@
         scale = jnp.where(lane // HD == h, scales[:, h : h + 1], scale)
     q_factor = lax.rsqrt(1.0 + head_sums(query * query))
     k_factor = lax.rsqrt(1.0 + head_sums(key * key))
-    slot = iota((PACK, HH), 1) % HD
-    factors = jnp.zeros((PACK, HH), f32)
-    for r in range(ROWS_DEV):
-        rows = slice(r * PACK, (r + 1) * PACK)
-        values = [*split_two(q_factor[rows]), *split_two(k_factor[rows])]
-        for i, part in enumerate(values):
-            factors = jnp.where(slot == 4 * r + i, part, factors)
-    factors_ref[...] = factors.astype(bf16)
     q_hat = query * q_factor * jnp.exp(scale)
     k_hat = key * k_factor
-    zeros = jnp.zeros((SHORT - 3 * (TOK - SHORT), HD), f32)
+    slot = iota((16, HH), 1) % HD
+    factors = jnp.zeros((16, HH), f32)
+    for i in range(TOK // 16):
+        rows = slice(16 * i, 16 * i + 16)
+        factors = jnp.where(slot == 2 * i, q_factor[rows], jnp.where(slot == 2 * i + 1, k_factor[rows], factors))
     for h in range(HEADS):
         parts = [lane_slice(part, h * HD) for part in (q_hat, k_hat, value)]
-        tail = jnp.concatenate([part[SHORT:] for part in parts] + [zeros], 0)
+        tail = jnp.concatenate([part[SHORT:] for part in parts] + [lane_slice(factors, h * HD)], 0)
         out_ref[h] = jnp.concatenate([part[:SHORT] for part in parts] + [tail], 1).astype(bf16)
 
 
@@ -104,6 +99,12 @@
     return jnp.concatenate([x, tail.reshape(GROUP, 32, 128)], 1)
 
 
+def unpack_factors(x_ref):
+    rows = x_ref[...].astype(f32)[:, SHORT - 16 :].reshape(GROUP * 16, 128)
+    rolled = [pltpu.roll(rows, 128 - 2 * i, 1) if i else rows for i in range(TOK // 16)]
+    return jnp.concatenate([part.reshape(GROUP, 16, 128) for part in rolled], 1)
+
+
 def unpack_heads(packed_ref):
     packed = [packed_ref[h].astype(f32) for h in range(HEADS)]
     rows = [
@@ -113,11 +114,11 @@
     return jnp.concatenate(rows, 0).astype(bf16)
 
 
-def pack_heads(array, factors, out_ref):
-    factors = factors.astype(f32)
+def pack_heads(array, out_ref):
+    zeros = jnp.zeros((PACK, HD), f32)
     for h in range(HEADS):
         parts = [lane_slice(array[r * PACK : (r + 1) * PACK], h * HD) for r in range(ROWS_DEV)]
-        out_ref[h] = jnp.concatenate(parts + [lane_slice(factors, h * HD)], 1).astype(bf16)
+        out_ref[h] = jnp.concatenate(parts + [zeros], 1).astype(bf16)
 
 
 def to_windows(array):
@@ -166,49 +167,68 @@
     return grad_y, dot_t(grad_y, weight), gains
 
 
-def labels_of(axis, window, first_row, row_ref, col_ref):
-    shape = (CELLS, 1) if axis == 0 else (1, CELLS)
-    at = iota(shape, axis)
-    source = at // (ROWS_DEV * WIN)
-    rest = at - source * (ROWS_DEV * WIN)
-    local_row = rest // WIN
-    column = rest - local_row * WIN + window * WIN
-    local_row = local_row + (column >= 36).astype(jnp.int32)
-    local_row = jnp.where(local_row >= ROWS_DEV, local_row - ROWS_DEV, local_row)
-    row = first_row + source * ROWS_DEV + local_row
-    row_label = jnp.zeros(shape, jnp.int32)
-    col_label = jnp.zeros(shape, jnp.int32)
+def tags_of(window, first_row_ref, row_ref, col_ref):
+    lane = iota((WIN, 128), 1)
+    place = iota((WIN, 1), 0)
+    column = place + window * WIN
+    col_label = jnp.zeros((WIN, 1), jnp.int32)
     for label in (1, 2):
-        row_cut = jnp.sum((row_ref[...] < label).astype(jnp.int32), 1, keepdims=True)
-        col_cut = jnp.sum((col_ref[...] < label).astype(jnp.int32), 1, keepdims=True)
-        row_label = row_label + (row >= row_cut).astype(jnp.int32)
-        col_label = col_label + (column >= col_cut).astype(jnp.int32)
-    return 3 * row_label + col_label
-
-
-def masked(scores, window, mask_refs):
+        cut = jnp.sum((col_ref[...] < label).astype(jnp.int32), 1, keepdims=True)
+        col_label = col_label + (column >= cut).astype(jnp.int32)
+    blocks = []
+    for source in range(GROUP):
+        rows = [row_ref[first_row_ref[0] + source * ROWS_DEV + r] for r in range(ROWS_DEV)]
+        for r in range(ROWS_DEV):
+            row_label = rows[r]
+            if window == 1:
+                row_label = jnp.where(column >= 36, rows[(r + 1) % ROWS_DEV], rows[r])
+            blocks.append(jnp.where(lane == col_label + 3 * row_label + 96, 10.0, 0.0))
+    return jnp.concatenate(blocks, 0)
+
+
+def tagged(cells, window, mask_refs):
     if mask_refs is None:
-        return scores
-    first_row = mask_refs[0][0]
-    one = labels_of(0, window, first_row, *mask_refs[1:])
-    two = labels_of(1, window, first_row, *mask_refs[1:])
-    return scores - jnp.where(one == two, 0.0, mask_value)
+        return cells
+    return jnp.where(iota(cells.shape, 1) < 96, cells, tags_of(window, *mask_refs))
+
+
+def with_tags(cells, at, key):
+    lane = iota(cells.shape, 1)
+    own = cells if at == 0 else pltpu.roll(cells, 128 - at, 1)
+    tags = pltpu.roll(cells, 64, 1)
+    if key:
+        tags = jnp.where(lane < HD + 9, tags - 10.0, tags)
+    return jnp.where(lane < HD, own, tags)[:, :64].astype(bf16)
+
+
+def together(steps):
+    steps = list(steps)
+    while steps:
+        steps = [step for step in steps if next(step, 0) is None]
 
 
 def attend_kernel(masks, x_ref, *refs):
     mask_refs = refs[:3] if masks else None
     out_ref = refs[-1]
     lane = iota((CELLS, 128), 1)
-    per_window = []
-    for w, cells in enumerate(to_windows(unpack_cells(x_ref))):
-        query = cells[:, :HD].astype(bf16)
-        key = cells[:, HD : 2 * HD].astype(bf16)
+    per_window = [None, None]
+
+    def attend(w, cells):
+        cells = tagged(cells, w, mask_refs)
+        query = with_tags(cells, 0, False) if masks else cells[:, :HD].astype(bf16)
+        key = with_tags(cells, HD, True) if masks else cells[:, HD : 2 * HD].astype(bf16)
         value = jnp.where(lane < HD, pltpu.roll(cells, 64, 1), jnp.where(lane == HD, 1.0, 0.0)).astype(bf16)
-        scores = masked(dot_t(query, key), w, mask_refs)
+        yield
+        scores = dot_t(query, key)
+        yield
         weights = jnp.exp(scores).astype(bf16)
+        yield
         summed = dot(weights, value)
+        yield
         attended = jnp.where(lane < HD, summed * (1.0 / summed[:, HD : HD + 1]), 0.0)
-        per_window.append(attended.reshape(GROUP, ROWS_DEV, WIN, 128))
+        per_window[w] = attended.reshape(GROUP, ROWS_DEV, WIN, 128)
+
+    together(attend(w, cells) for w, cells in enumerate(to_windows(unpack_cells(x_ref))))
     total = 0.0
     for r in range(ROWS_DEV):
         rows = jnp.concatenate([part[:, r] for part in per_window], 1).reshape(GROUP * PACK, 128)
@@ -221,69 +241,79 @@
     out_ref = refs[-1]
     lane = iota((CELLS, 128), 1)
     low = iota((HD, CELLS), 0)
+    zeros = jnp.zeros((HD, CELLS), f32)
     scale_row = jnp.exp(jnp.full((1, 128), scale_ref[block, head_ref[0]], f32))
     unscale_row = 1.0 / scale_row
     packed = grad_ref[...].astype(f32).reshape(GROUP * PACK, 128)
-    low_lane = iota(packed.shape, 1) < HD
-    rolled = [packed] + [
-        jnp.where(low_lane, pltpu.roll(packed, 128 - r * HD, 1), pltpu.roll(packed, 128 - r * 4, 1))
-        for r in range(1, ROWS_DEV)
-    ]
+    rolled = [packed if r == 0 else pltpu.roll(packed, 128 - r * HD, 1) for r in range(ROWS_DEV)]
     rolled = [part.reshape(GROUP, 1, 2, WIN, 128) for part in rolled]
     grads = jnp.concatenate(rolled, 1)
-    results = []
-    for w, cells in enumerate(to_windows(unpack_cells(x_ref))):
+    factors = to_windows(unpack_factors(x_ref))
+    results = [None, None]
+
+    def attend_back(w, cells):
+        cells = tagged(cells, w, mask_refs)
         turned = cells.T
-        query_t = turned[:HD].astype(bf16)
+        query_t = (jnp.concatenate([turned[:HD], turned[96:]], 0) if masks else turned[:HD]).astype(bf16)
         key_t = turned[HD : 2 * HD].astype(bf16)
         value_t = turned[2 * HD : 3 * HD]
-        grad = grads[:, :, w].reshape(CELLS, 128)
-        grad_t = grad.T[:HD]
-        key = cells[:, HD : 2 * HD].astype(bf16)
-        scores = masked(dot(key, query_t), w, mask_refs)
+        grad_t = grads[:, :, w].reshape(CELLS, 128).T[:HD]
+        key = with_tags(cells, HD, True) if masks else cells[:, HD : 2 * HD].astype(bf16)
+        yield
+        scores = dot(key, query_t)
+        yield
         weights = jnp.exp(scores).astype(bf16)
+        yield
         summed = dot(jnp.concatenate([value_t, jnp.where(low == 0, 1.0, 0.0)], 0).astype(bf16), weights)
+        yield
         inverse = 1.0 / summed[HD : HD + 1]
         grad_t = (grad_t * inverse).astype(bf16).astype(f32)
         row_high, row_low = split_two(jnp.sum(grad_t * summed[:HD], 0, keepdims=True) * inverse)
         rows = jnp.where(low == 0, -row_high, jnp.where(low == 1, -row_low, 0.0))
         grad_ext = jnp.concatenate([grad_t, rows], 0).astype(bf16)
+        yield
         ones = jnp.where(lane < HD + 2, 1.0, 0.0)
         value_ext = jnp.where(lane < HD, pltpu.roll(cells, 64, 1), ones)[:, :64].astype(bf16)
+        yield
         grad_scores = (weights.astype(f32) * dot(value_ext, grad_ext)).astype(bf16)
+        yield
         query_at = jnp.where((lane >= HD) & (lane < 2 * HD), pltpu.roll(cells, HD, 1), 0.0).astype(bf16)
-        zeros = jnp.zeros((HD, CELLS), f32)
         grad_at = jnp.concatenate([zeros, zeros, grad_t, zeros], 0).T.astype(bf16)
+        yield
         grad_kv = dot(grad_scores, query_at) + dot(weights, grad_at)
+        yield
         grad_q = dot(key_t, grad_scores)
+        yield
         grad_q = jnp.concatenate([grad_q, zeros, zeros, zeros], 0).T
+        yield
         total = jnp.where(lane < HD, grad_q * scale_row, grad_kv)
         unit = jnp.where(lane < HD, cells * unscale_row, jnp.where(lane < 2 * HD, cells, 0.0))
-        q_factor = grad[:, 96:97] + grad[:, 97:98]
-        k_factor = grad[:, 98:99] + grad[:, 99:100]
+        q_factor, k_factor = factors[w][:, 96:97], factors[w][:, 97:98]
         factor = jnp.where(lane < HD, q_factor, jnp.where(lane < 2 * HD, k_factor, 1.0))
-        results.append(factor * (total - unit * head_sums(unit * total)))
+        results[w] = factor * (total - unit * head_sums(unit * total))
+
+    together(attend_back(w, cells) for w, cells in enumerate(to_windows(unpack_cells(x_ref))))
     out_ref[...] = pack_cells(from_windows(results)).astype(bf16)
 
 
-def first_kernel(tokens_ref, w_ref, scale_ref, out_ref, factors_ref):
-    send_projected(tokens_ref[...], w_ref[...], scale_ref, 0, out_ref, factors_ref)
-
-
-def middle_kernel(packed_ref, scale_ref, gain_ref, bias_ref, tokens_ref, w_proj_ref, w_ref, out_ref, rolled_ref, factors_ref):
+def first_kernel(tokens_ref, w_ref, scale_ref, out_ref):
+    send_projected(tokens_ref[...], w_ref[...], scale_ref, 0, out_ref)
+
+
+def middle_kernel(packed_ref, scale_ref, gain_ref, bias_ref, tokens_ref, w_proj_ref, w_ref, out_ref, rolled_ref):
     attended = unpack_heads(packed_ref)
     y_hat, _ = normalized(attended, w_proj_ref[...])
     out = (tokens_ref[...].astype(f32) + y_hat * gain_ref[0:1] + bias_ref[0:1]).astype(bf16).astype(f32)
     rolled = roll_tokens(out, -SHIFT).astype(bf16)
     rolled_ref[...] = rolled
-    send_projected(rolled, w_ref[...], scale_ref, 1, out_ref, factors_ref)
-
-
-def turn_kernel(core_ref, packed_ref, gain_ref, grad_ref, w_proj_ref, factors_ref, out_ref, kept_ref, given_ref, gains_ref):
+    send_projected(rolled, w_ref[...], scale_ref, 1, out_ref)
+
+
+def turn_kernel(core_ref, packed_ref, gain_ref, grad_ref, w_proj_ref, out_ref, kept_ref, given_ref, gains_ref):
     attended = unpack_heads(packed_ref)
     grad = roll_tokens(grad_ref[...].astype(f32), -SHIFT)
     grad_y, grad_att, gains = finish_back(attended, w_proj_ref[...], gain_ref[1:2], grad)
-    pack_heads(grad_att, factors_ref[...], out_ref)
+    pack_heads(grad_att, out_ref)
     kept, given = halves(attended, core_ref[0])
     kept_ref[...] = dot_0(grad_y, kept).astype(bf16)
     given_ref[...] = dot_0(grad_y, given).astype(bf16)
@@ -314,7 +344,6 @@
     proj1_kept_ref,
     proj1_given_ref,
     tokens_ref,
-    factors_ref,
     out_ref,
     gains_ref,
     grad0_ref,
@@ -336,7 +365,7 @@
     ]
     kept_ref[...] = kept
     given_ref[...] = given
-    pack_heads(grad_att, factors_ref[...], out_ref)
+    pack_heads(grad_att, out_ref)
     gains_ref[...] = gains
 
 
@@ -485,7 +514,7 @@
         in_specs=[smem] * len(scalars)
         + [vmem] * len(arrays)
         + [hbm] * len(fetched)
-        + [smem, vmem, vmem][: len(masks)],
+        + [smem, smem, vmem][: len(masks)],
         out_specs=[vmem] * len(outs) + [hbm] * len(stored),
         scratch_shapes=scratch,
         compiler_params=pltpu.CompilerParams(vmem_limit_bytes=VMEM_LIMIT),
@@ -510,7 +539,7 @@
     first_row = (moved_position // GROUP * WIN).reshape(1)
     core = (lax.axis_index("dp") % 2).reshape(1)
     image, head0, head1, first_row, core = lax.optimization_barrier((image, head0, head1, first_row, core))
-    masks = (first_row, row_band.reshape(1, -1), col_band.reshape(1, -1))
+    masks = (first_row, row_band, col_band.reshape(1, -1))
 
     def exchange(array, groups):
         return lax.all_to_all(array, "rows", 0, 0, axis_index_groups=groups, tiled=True)
@@ -518,7 +547,6 @@
     tokens0 = image.reshape(TOK, C)
     grad_out = out_grad.reshape(TOK, C)
     short = ((GROUP, SHORT, 128), bf16)
-    factors = ((PACK, HH), bf16)
     narrow = ((GROUP, PACK, 128), bf16)
     cells = ((TOK, C), bf16)
     proj = ((C, HH // 2), bf16)
@@ -529,18 +557,16 @@
     def swap(array, apart):
         return lax.ppermute(array, "dp", [(i, i ^ apart) for i in range(4)])
 
-    x0, factors0 = call(
-        first_kernel, [short], (), (), fetched=(tokens0, (w_qkv, 0), logit_scale), stored=[factors]
-    )
+    (x0,) = call(first_kernel, [short], (), (), fetched=(tokens0, (w_qkv, 0), logit_scale))
     x0 = exchange(x0, aligned)
     (a0,) = call(functools.partial(attend_kernel, False), [narrow], (), (x0,))
     a0 = exchange(a0, aligned)
-    x1, tokens1, factors1 = call(
+    x1, tokens1 = call(
         middle_kernel,
         [short],
         (),
         (a0, logit_scale, norm_gain, norm_bias, tokens0, (w_proj, 0), (w_qkv, 1)),
-        stored=[cells, factors],
+        stored=[cells],
     )
     x1 = exchange(x1, moved)
     (a1,) = call(functools.partial(attend_kernel, True), [narrow], (), (x1,), masks)
@@ -549,7 +575,7 @@
         turn_kernel,
         [narrow, proj, proj, gains],
         (core,),
-        (a1, norm_gain, grad_out, (w_proj, 1), factors1),
+        (a1, norm_gain, grad_out, (w_proj, 1)),
     )
     d1 = exchange(d1, moved)
     (qkv1,) = call(
@@ -560,7 +586,7 @@
         back_kernel,
         [narrow, gains],
         (core,),
-        (qkv1, a0, norm_gain, (w_qkv, 1), (w_proj, 0), grad_out, proj1_kept, proj1_given, tokens1, factors0),
+        (qkv1, a0, norm_gain, (w_qkv, 1), (w_proj, 0), grad_out, proj1_kept, proj1_given, tokens1),
         stored=[cells, half_early, half_early],
     )
     d0 = exchange(d0, aligned)

time: 181 us -> 178 us (0.983)
  Pallas kernels: 22.1 us -> 19.9 us
    pallas_call x15, Pallas kernels: 22.1 us -> 19.9 us  [call(): pl.pallas_call(wrapped, out_shape=[jax.ShapeDtypeStruct(*out) for out in...]
where the time goes in v6:
time: 178 us
  blocking collectives  136 us (76%)
  Pallas kernels  19.9 us (11%)
  starting transfers between devices  17.5 us (10%)
  waiting for transfers between devices  3.44 us (2%)
    all_to_all x10, blocking collectives, exchange(): lax.all_to_all(array, 'rows', 0, 0, axis_index_groups=groups, tiled=True)  136 us
    pallas_call x15, Pallas kernels, call(): pl.pallas_call(wrapped, out_shape=[jax.ShapeDtypeStruct(*out) for out in...  19.9 us
    ppermute x4, starting transfers between devices, swap(): return lax.ppermute(array, 'dp', [(i, i ^ apart) for i in range(4)])  17.5 us
  transfers between devices with their start and end apart: 4, of which 2 were waited for; matrix products, arithmetic and copies ran while one was open for 0% of the time, Pallas kernels for 1%

profile of v6, /device:TPU:1, one launch (start us, length us, event | category | flops | bytes accessed | tf_op | source)
XLA Modules:
  0.0 177.8 jit_solution(6262663206470815101)
XLA Ops:
  0.7 0.0 copy-start
  0.7 0.0 copy-start.1
  0.7 0.0 copy-start.2
  0.7 0.0 copy-start.7
  0.7 0.0 copy-start.8
  0.7 0.0 copy-start.9
  0.7 2.2 %shard_map.128 = bf16[8,112,128]{2,1,0:T(8,128)(2,1)S(1)} custom-call(bf16[144,512]{1,0:T(8,128)(2,1)} %bitcast.9, bf16[2,512,768]{2,1,0:T(8,128)(2,1)} %refs_1_.9, f32[2,8]{1,0:T(2,128)} %refs_1_.8), custom_call_target="tpu_custom_call" | custom-call | tf_op jit(solution)/shard_map/pallas_call | solution.py:511
  2.9 18.6 %all_to_all.50.refs_0_.refs_2_ = bf16[8,112,128]{2,1,0:T(8,128)(2,1)S(1)} all-to-all(bf16[8,112,128]{2,1,0:T(8,128)(2,1)S(1)} %shard_map.128), channel_id=1, replica_groups={{0,1,2,3,4,5,6,7},{8,9,10,11,12,13,14,15},{16,17,18,19,20,21,22,23},{24..., dimensions={0} | all-to-all | bytes 458752 | tf_op jit(solution)/shard_map/all_to_all | solution.py:545
  21.5 1.3 shard_map.129
  22.8 10.2 %all_to_all.51.refs_0_.refs_2_ = bf16[8,48,128]{2,1,0:T(8,128)(2,1)S(1)} all-to-all(bf16[8,48,128]{2,1,0:T(8,128)(2,1)S(1)} %shard_map.129), channel_id=1, replica_groups={{0,1,2,3,4,5,6,7},{8,9,10,11,12,13,14,15},{16,17,18,19,20,21,22,23},{24..., dimensions={0} | all-to-all | bytes 196608 | tf_op jit(solution)/shard_map/all_to_all | solution.py:545
  32.9 0.0 copy-done
  32.9 0.0 copy-done.1
  32.9 0.0 copy-done.2
  32.9 0.0 copy-done.7
  33.0 0.0 copy-done.8
  33.0 0.0 copy-done.9
  33.0 0.0 copy-start.10
  33.0 0.0 copy-start.11
  33.0 1.2 shard_map.130
  34.2 0.0 copy-start.4
  34.2 13.5 %all_to_all.52.refs_0_.refs_2_ = bf16[8,112,128]{2,1,0:T(8,128)(2,1)S(1)} all-to-all(bf16[8,112,128]{2,1,0:T(8,128)(2,1)S(1)} %get-tuple-element.34), channel_id=1, replica_groups={{4,5,6,7,8,9,10,11},{12,13,14,15,16,17,18,19},{20,21,22,23,24,25,26,27}..., dimensions={0} | all-to-all | bytes 458752 | tf_op jit(solution)/shard_map/all_to_all | solution.py:545
  47.7 0.0 copy-done.10
  47.7 0.0 copy-done.11
  47.7 1.9 %shard_map.131 = bf16[8,48,128]{2,1,0:T(8,128)(2,1)S(1)} custom-call(bf16[8,112,128]{2,1,0:T(8,128)(2,1)S(1)} %all_to_all.52.refs_0_.refs_2_, s32[1]{0:T(128)} %bitcast.2.refs_1_.refs_4_, s32[192]{0:T(256)S(1)} %copy-done.10, s32[1,48]{1,0:T(1,128)S(1)} %bitcast.14), custom_call_target="tpu_custom_call" | custom-call | tf_op jit(solution)/shard_map/pallas_call | solution.py:511
  49.6 0.0 copy-start.6
  49.6 12.1 %all_to_all.53.refs_1_ = bf16[8,48,128]{2,1,0:T(8,128)(2,1)S(1)} all-to-all(bf16[8,48,128]{2,1,0:T(8,128)(2,1)S(1)} %shard_map.131), channel_id=1, replica_groups={{4,5,6,7,8,9,10,11},{12,13,14,15,16,17,18,19},{20,21,22,23,24,25,26,27}..., dimensions={0} | all-to-all | bytes 196608 | tf_op jit(solution)/shard_map/all_to_all | solution.py:545
  61.7 0.0 copy-done.4
  61.7 0.9 shard_map.132
  62.6 12.4 %all_to_all.54.refs_3_ = bf16[8,48,128]{2,1,0:T(8,128)(2,1)S(1)} all-to-all(bf16[8,48,128]{2,1,0:T(8,128)(2,1)S(1)} %get-tuple-element.36), channel_id=1, replica_groups={{4,5,6,7,8,9,10,11},{12,13,14,15,16,17,18,19},{20,21,22,23,24,25,26,27}..., dimensions={0} | all-to-all | bytes 196608 | tf_op jit(solution)/shard_map/all_to_all | solution.py:545
  75.0 3.6 %shard_map.133 = bf16[8,112,128]{2,1,0:T(8,128)(2,1)S(1)} custom-call(s32[1]{0:T(128)} %bitcast.1.refs_0_, f32[2,8]{1,0:T(2,128)S(1)} %copy-done.8, bf16[8,112,128]{2,1,0:T(8,128)(2,1)S(1)} %all_to_all.52.refs_0_.refs_2_, bf16[8,48,128]{2,1,0:T(8,128)(2,1)S(1)} %all_to_all.54.refs_3_, s32[1]{0:T(128)} %bitcast.2.refs_1_.refs_4_, s32[192]{0:T(256)S(1)} %copy-done.10, ...), custom_call_target="tpu_custom_call" | custom-call | tf_op jit(solution)/shard_map/pallas_call | solution.py:511
  78.6 13.9 %all_to_all.55.refs_1_ = bf16[8,112,128]{2,1,0:T(8,128)(2,1)S(1)} all-to-all(bf16[8,112,128]{2,1,0:T(8,128)(2,1)S(1)} %shard_map.133), channel_id=1, replica_groups={{4,5,6,7,8,9,10,11},{12,13,14,15,16,17,18,19},{20,21,22,23,24,25,26,27}..., dimensions={0} | all-to-all | bytes 458752 | tf_op jit(solution)/shard_map/all_to_all | solution.py:545
  92.5 0.0 copy-done.6
  92.5 2.4 %shard_map.134 = (bf16[8,48,128]{2,1,0:T(8,128)(2,1)S(1)}, f32[8,512]{1,0:T(8,128)S(1)}, bf16[144,512]{1,0:T(8,128)(2,1)}, bf16[512,640]{1,0:T(8,128)(2,1)}, bf16[512,640]{1,0:T(8,128)(2,1)}) custom-call(s32[1]{0:T(128)} %bitcast.3.refs_0_, bf16[8,112,128]{2,1,0:T(8,128)(2,1)S(1)} %all_to_all.55.refs_1_, bf16[8,48,128]{2,1,0:T(8,128)(2,1)S(1)} %all_to_all.51.refs_0_.refs_2_, ...), custom_call_target="tpu_custom_call" | custom-call | tf_op jit(solution)/shard_map/pallas_call | solution.py:511
  94.9 0.0 copy-start.3
  94.9 10.8 %all_to_all.56.refs_3_ = bf16[8,48,128]{2,1,0:T(8,128)(2,1)S(1)} all-to-all(bf16[8,48,128]{2,1,0:T(8,128)(2,1)S(1)} %get-tuple-element.40), channel_id=1, replica_groups={{0,1,2,3,4,5,6,7},{8,9,10,11,12,13,14,15},{16,17,18,19,20,21,22,23},{24..., dimensions={0} | all-to-all | bytes 196608 | tf_op jit(solution)/shard_map/all_to_all | solution.py:545
  105.7 3.4 %shard_map.135 = bf16[8,112,128]{2,1,0:T(8,128)(2,1)S(1)} custom-call(s32[1]{0:T(128)} %bitcast.refs_0_, f32[2,8]{1,0:T(2,128)S(1)} %copy-done.8, bf16[8,112,128]{2,1,0:T(8,128)(2,1)S(1)} %all_to_all.50.refs_0_.refs_2_, bf16[8,48,128]{2,1,0:T(8,128)(2,1)S(1)} %all_to_all.56.refs_3_), custom_call_target="tpu_custom_call" | custom-call | tf_op jit(solution)/shard_map/pallas_call | solution.py:511
  109.1 11.4 %all_to_all.57.refs_1_.refs_0_ = bf16[8,112,128]{2,1,0:T(8,128)(2,1)S(1)} all-to-all(bf16[8,112,128]{2,1,0:T(8,128)(2,1)S(1)} %shard_map.135), channel_id=1, replica_groups={{0,1,2,3,4,5,6,7},{8,9,10,11,12,13,14,15},{16,17,18,19,20,21,22,23},{24..., dimensions={0} | all-to-all | bytes 458752 | tf_op jit(solution)/shard_map/all_to_all | solution.py:545
  120.5 10.9 %collective-permute-start.1 = (bf16[512,640]{1,0:T(8,128)(2,1)}, bf16[512,640]{1,0:T(8,128)(2,1)S(1)}, u32[]{:S(2)}, u32[]{:S(2)}) collective-permute-start(bf16[512,640]{1,0:T(8,128)(2,1)} %get-tuple-element.45), channel_id=1, source_target_pairs={{0,64},{64,0},{128,192},{192,128},{1,65},{65,1},{129,193},{193,129... | collective-permute-start | bytes 1966088 | tf_op jit(solution)/shard_map/ppermute | solution.py:558
  131.3 0.7 shard_map.136
  132.0 0.1 collective-permute-start
  132.1 1.7 collective-permute-done.refs_1_
  133.8 0.0 collective-permute-done.1.refs_2_
  133.8 0.0 copy-done.3
  133.8 0.4 shard_map.137
  134.2 22.7 %all_to_all.58.refs_0_ = bf16[8,528,128]{2,1,0:T(8,128)(2,1)S(1)} all-to-all(bf16[8,528,128]{2,1,0:T(8,128)(2,1)S(1)} %shard_map.137), channel_id=1, replica_groups={{0,8,16,24,32,40,48,56},{1,9,17,25,33,41,49,57},{2,10,18,26,34,42,50,58..., dimensions={0} | all-to-all | bytes 2162688 | tf_op jit(solution)/shard_map/all_to_all | solution.py:545
  157.0 0.0 copy-start.5
  157.0 0.2 shard_map.138
  157.2 10.6 %all_to_all.59.refs_0_ = bf16[8,80,128]{2,1,0:T(8,128)(2,1)S(1)} all-to-all(bf16[8,80,128]{2,1,0:T(8,128)(2,1)S(1)} %shard_map.138), channel_id=1, replica_groups={{0,1,2,3,4,5,6,7},{8,9,10,11,12,13,14,15},{16,17,18,19,20,21,22,23},{24..., dimensions={0} | all-to-all | bytes 327680 | tf_op jit(solution)/shard_map/all_to_all | solution.py:545
  167.8 2.7 %collective-permute-start.2 = (f32[80,128]{1,0:T(8,128)S(1)}, f32[80,128]{1,0:T(8,128)S(1)}, u32[]{:S(2)}, u32[]{:S(2)}) collective-permute-start(f32[80,128]{1,0:T(8,128)S(1)} %shard_map.139.refs_0_), channel_id=1, source_target_pairs={{0,128},{64,192},{128,0},{192,64},{1,129},{65,193},{129,1},{193,65... | collective-permute-start | bytes 122888 | tf_op jit(solution)/shard_map/ppermute | solution.py:558
  170.5 1.7 collective-permute-done.2.refs_1_
  172.3 3.8 %collective-permute-start.3 = (f32[80,128]{1,0:T(8,128)S(1)}, f32[80,128]{1,0:T(8,128)S(1)}, u32[]{:S(2)}, u32[]{:S(2)}) collective-permute-start(f32[80,128]{1,0:T(8,128)S(1)} %shard_map.140.refs_1_), channel_id=1, source_target_pairs={{0,64},{64,0},{128,192},{192,128},{1,65},{65,1},{129,193},{193,129... | collective-permute-start | bytes 122888 | tf_op jit(solution)/shard_map/ppermute | solution.py:558
  176.1 0.0 copy-done.5
  176.1 1.1 shard_map.141
  177.1 0.0 collective-permute-done.3.refs_2_
  177.1 0.6 shard_map.142
  (2 shorter events, 0.0 us)
Async XLA Ops:
  0.7 32.2 %copy-start = (bf16[2,512,768]{2,1,0:T(8,128)(2,1)S(1)}, bf16[2,512,768]{2,1,0:T(8,128)(2,1)}, u32[]{:S(2)}) copy-start(bf16[2,512,768]{2,1,0:T(8,128)(2,1)} %refs_1_.9) | copy-start | bytes 4718596
  0.7 32.2 %copy-start.1 = (bf16[2,256,512]{2,1,0:T(8,128)(2,1)S(1)}, bf16[2,256,512]{2,1,0:T(8,128)(2,1)}, u32[]{:S(2)}) copy-start(bf16[2,256,512]{2,1,0:T(8,128)(2,1)} %refs_5_.5) | copy-start | bytes 1572868
  0.7 32.2 %copy-start.2 = (bf16[1,3,48,512]{3,2,1,0:T(8,128)(2,1)S(1)}, bf16[1,3,48,512]{3,2,1,0:T(8,128)(2,1)}, u32[]{:S(2)}) copy-start(bf16[1,3,48,512]{3,2,1,0:T(8,128)(2,1)} %param.9) | copy-start | bytes 442372
  0.7 32.2 %copy-start.7 = (f32[2,512]{1,0:T(2,128)S(1)}, f32[2,512]{1,0:T(2,128)}, u32[]{:S(2)}) copy-start(f32[2,512]{1,0:T(2,128)} %refs_3_.3) | copy-start | bytes 12292
  0.7 32.2 %copy-start.8 = (f32[2,8]{1,0:T(2,128)S(1)}, f32[2,8]{1,0:T(2,128)}, u32[]{:S(2)}) copy-start(f32[2,8]{1,0:T(2,128)} %refs_1_.8) | copy-start | bytes 196
  0.7 32.2 %copy-start.9 = (f32[2,512]{1,0:T(2,128)S(1)}, f32[2,512]{1,0:T(2,128)}, u32[]{:S(2)}) copy-start(f32[2,512]{1,0:T(2,128)} %refs_3_.2) | copy-start | bytes 12292
  33.0 14.7 %copy-start.10 = (s32[192]{0:T(256)S(1)}, s32[192]{0:T(256)}, u32[]{:S(2)}) copy-start(s32[192]{0:T(256)} %refs_5_.4) | copy-start | bytes 2308
  33.0 14.7 %copy-start.11 = (s32[48]{0:T(128)S(1)}, s32[48]{0:T(128)}, u32[]{:S(2)}) copy-start(s32[48]{0:T(128)} %param.17) | copy-start | bytes 580
  34.2 27.5 %copy-start.4 = (bf16[1,3,48,512]{3,2,1,0:T(8,128)(2,1)S(1)}, bf16[1,3,48,512]{3,2,1,0:T(8,128)(2,1)}, u32[]{:S(2)}) copy-start(bf16[1,3,48,512]{3,2,1,0:T(8,128)(2,1)} %param.10) | copy-start | bytes 442372
  49.6 42.9 %copy-start.6 = (bf16[144,512]{1,0:T(8,128)(2,1)S(1)}, bf16[144,512]{1,0:T(8,128)(2,1)}, u32[]{:S(2)}) copy-start(bf16[144,512]{1,0:T(8,128)(2,1)} %get-tuple-element.39.refs_9_) | copy-start | bytes 442372
  94.9 38.9 %copy-start.3 = (bf16[512,640]{1,0:T(8,128)(2,1)S(1)}, bf16[512,640]{1,0:T(8,128)(2,1)}, u32[]{:S(2)}) copy-start(bf16[512,640]{1,0:T(8,128)(2,1)} %get-tuple-element.48.refs_5_) | copy-start | bytes 1966084
  120.5 13.3 %collective-permute-start.1 = (bf16[512,640]{1,0:T(8,128)(2,1)}, bf16[512,640]{1,0:T(8,128)(2,1)S(1)}, u32[]{:S(2)}, u32[]{:S(2)}) collective-permute-start(bf16[512,640]{1,0:T(8,128)(2,1)} %get-tuple-element.45), channel_id=1, source_target_pairs={{0,64},{64,0},{128,192},{192,128},{1,65},{65,1},{129,193},{193,129... | collective-permute-start | bytes 1966088 | tf_op jit(solution)/shard_map/ppermute | solution.py:558
  132.0 1.8 %collective-permute-start = (bf16[512,384]{1,0:T(8,128)(2,1)S(1)}, bf16[512,384]{1,0:T(8,128)(2,1)S(1)}, u32[]{:S(2)}, u32[]{:S(2)}) collective-permute-start(bf16[512,384]{1,0:T(8,128)(2,1)S(1)} %get-tuple-element.44), channel_id=1, source_target_pairs={{0,64},{64,0},{128,192},{192,128},{1,65},{65,1},{129,193},{193,129... | collective-permute-start | bytes 1179656 | tf_op jit(solution)/shard_map/ppermute | solution.py:558
  157.0 19.1 %copy-start.5 = (bf16[144,512]{1,0:T(8,128)(2,1)S(1)}, bf16[144,512]{1,0:T(8,128)(2,1)}, u32[]{:S(2)}) copy-start(bf16[144,512]{1,0:T(8,128)(2,1)} %get-tuple-element.50.refs_2_) | copy-start | bytes 442372
  167.8 4.4 %collective-permute-start.2 = (f32[80,128]{1,0:T(8,128)S(1)}, f32[80,128]{1,0:T(8,128)S(1)}, u32[]{:S(2)}, u32[]{:S(2)}) collective-permute-start(f32[80,128]{1,0:T(8,128)S(1)} %shard_map.139.refs_0_), channel_id=1, source_target_pairs={{0,128},{64,192},{128,0},{192,64},{1,129},{65,193},{129,1},{193,65... | collective-permute-start | bytes 122888 | tf_op jit(solution)/shard_map/ppermute | solution.py:558
  172.3 4.9 %collective-permute-start.3 = (f32[80,128]{1,0:T(8,128)S(1)}, f32[80,128]{1,0:T(8,128)S(1)}, u32[]{:S(2)}, u32[]{:S(2)}) collective-permute-start(f32[80,128]{1,0:T(8,128)S(1)} %shard_map.140.refs_1_), channel_id=1, source_target_pairs={{0,64},{64,0},{128,192},{192,128},{1,65},{65,1},{129,193},{193,129... | collective-permute-start | bytes 122888 | tf_op jit(solution)/shard_map/ppermute | solution.py:558

commit v7 on v6

--- a/solution.py
+++ b/solution.py
@@ -19,6 +19,9 @@
 ROWS_DEV = 3
 PACK = 48
 DEVS = 64
+ORDER = (0, 2, 4, 6, 1, 3, 5, 7)
+MOVED = (0, 2, 4, 6, 7, 5, 3, 1)
+ACROSS = (7, 6, 5, 4, 3, 2, 1, 0)
 VMEM_LIMIT = 24 * 2**20
 EARLY = 3 * HH + 2 * HH
 SHORT = 112
@@ -176,7 +179,7 @@
         cut = jnp.sum((col_ref[...] < label).astype(jnp.int32), 1, keepdims=True)
         col_label = col_label + (column >= cut).astype(jnp.int32)
     blocks = []
-    for source in range(GROUP):
+    for source in MOVED:
         rows = [row_ref[first_row_ref[0] + source * ROWS_DEV + r] for r in range(ROWS_DEV)]
         for r in range(ROWS_DEV):
             row_label = rows[r]
@@ -389,14 +392,14 @@
     for ring in range(8):
         block = gains[:, ring // 2 * 128 : ring // 2 * 128 + 128]
         block = pltpu.roll(block, depth, 1) if ring % 2 else block
-        parts_ref[ring, TILES * depth :] = block.astype(bf16)
+        parts_ref[ACROSS.index(ring), TILES * depth :] = block.astype(bf16)
     late = late_ref[...].astype(f32) + got_late_ref[...].astype(f32)
     early = kept_ref[...].astype(f32) + got_ref[...].astype(f32)
     tile = 0
     for part in (late, early):
         for at in range(0, part.shape[1], 128):
             block = part[:, at : at + 128].astype(bf16).reshape(8, depth, 128)
-            parts_ref[:, tile * depth : (tile + 1) * depth, :] = block
+            parts_ref[:, tile * depth : (tile + 1) * depth, :] = jnp.stack([block[ring] for ring in ACROSS])
             tile += 1
 
 
@@ -406,7 +409,8 @@
     total = total[: TILES * C // 8].reshape(TILES, 8, 8, 128)
     for place in range(8):
         rolled = pltpu.roll(gains, 128 - 8 * place, 1) if place else gains
-        out_ref[place] = jnp.concatenate([total[:, place].reshape(TILES * 8, 128), rolled], 0).astype(bf16)
+        block = jnp.concatenate([total[:, place].reshape(TILES * 8, 128), rolled], 0)
+        out_ref[ORDER.index(place)] = block.astype(bf16)
 
 
 def second_sum_kernel(parts_ref, out_ref):
@@ -530,12 +534,14 @@
     position = lax.axis_index("rows")
     half = GROUP // 2
     rings = range(DEVS // GROUP)
-    aligned = [[GROUP * g + i for i in range(GROUP)] for g in rings]
-    across = [[GROUP * g + i for g in rings] for i in range(GROUP)]
-    moved = [[(GROUP * g + half + i) % DEVS for i in range(GROUP)] for g in rings]
+    aligned = [[GROUP * g + i for i in ORDER] for g in rings]
+    across = [[GROUP * g + i for g in ACROSS] for i in range(GROUP)]
+    moved = [[(GROUP * g + half + i) % DEVS for i in MOVED] for g in rings]
     moved_position = (position + DEVS - half) % DEVS
-    head0 = (position % GROUP).reshape(1)
-    head1 = (moved_position % GROUP).reshape(1)
+    head0, head1 = jnp.zeros((1,), jnp.int32), jnp.zeros((1,), jnp.int32)
+    for h in range(HEADS):
+        head0 = head0 + h * (position % GROUP == ORDER[h])
+        head1 = head1 + h * (moved_position % GROUP == MOVED[h])
     first_row = (moved_position // GROUP * WIN).reshape(1)
     core = (lax.axis_index("dp") % 2).reshape(1)
     image, head0, head1, first_row, core = lax.optimization_barrier((image, head0, head1, first_row, core))

time: 178 us -> 171 us (0.961)
  blocking collectives: 136 us -> 131 us
  starting transfers between devices: 17.5 us -> 15.7 us
    all_to_all x10, blocking collectives: 136 us -> 131 us  [exchange(): lax.all_to_all(array, 'rows', 0, 0, axis_index_groups=groups, tiled=True)]
    ppermute x4, starting transfers between devices: 17.5 us -> 15.7 us  [swap(): return lax.ppermute(array, 'dp', [(i, i ^ apart) for i in range(4)])]
where the time goes in v7:
time: 171 us
  blocking collectives  131 us (77%)
  Pallas kernels  19.9 us (12%)
  starting transfers between devices  15.7 us (9%)
  waiting for transfers between devices  3.33 us (2%)
    all_to_all x10, blocking collectives, exchange(): lax.all_to_all(array, 'rows', 0, 0, axis_index_groups=groups, tiled=True)  131 us
    pallas_call x15, Pallas kernels, call(): pl.pallas_call(wrapped, out_shape=[jax.ShapeDtypeStruct(*out) for out in...  19.9 us
    ppermute x4, starting transfers between devices, swap(): return lax.ppermute(array, 'dp', [(i, i ^ apart) for i in range(4)])  15.7 us
  transfers between devices with their start and end apart: 4, of which 2 were waited for; matrix products, arithmetic and copies ran while one was open for 0% of the time, Pallas kernels for 1%

profile of v7, /device:TPU:1, one launch (start us, length us, event | category | flops | bytes accessed | tf_op | source)
XLA Modules:
  0.0 170.7 jit_solution(1286663676889021732)
XLA Ops:
  0.7 0.0 copy-start
  0.7 0.0 copy-start.1
  0.8 0.0 copy-start.2
  0.8 0.0 copy-start.7
  0.8 0.0 copy-start.8
  0.8 0.0 copy-start.9
  0.8 2.2 %shard_map.128 = bf16[8,112,128]{2,1,0:T(8,128)(2,1)S(1)} custom-call(bf16[144,512]{1,0:T(8,128)(2,1)} %bitcast.9, bf16[2,512,768]{2,1,0:T(8,128)(2,1)} %refs_1_.9, f32[2,8]{1,0:T(2,128)} %refs_1_.8), custom_call_target="tpu_custom_call" | custom-call | tf_op jit(solution)/shard_map/pallas_call | solution.py:515
  3.0 16.3 %all_to_all.50.refs_0_.refs_2_ = bf16[8,112,128]{2,1,0:T(8,128)(2,1)S(1)} all-to-all(bf16[8,112,128]{2,1,0:T(8,128)(2,1)S(1)} %shard_map.128), channel_id=1, replica_groups={{0,2,4,6,1,3,5,7},{8,10,12,14,9,11,13,15},{16,18,20,22,17,19,21,23},{24..., dimensions={0} | all-to-all | bytes 458752 | tf_op jit(solution)/shard_map/all_to_all | solution.py:551
  19.3 1.3 shard_map.129
  20.6 11.7 %all_to_all.51.refs_0_.refs_2_ = bf16[8,48,128]{2,1,0:T(8,128)(2,1)S(1)} all-to-all(bf16[8,48,128]{2,1,0:T(8,128)(2,1)S(1)} %shard_map.129), channel_id=1, replica_groups={{0,2,4,6,1,3,5,7},{8,10,12,14,9,11,13,15},{16,18,20,22,17,19,21,23},{24..., dimensions={0} | all-to-all | bytes 196608 | tf_op jit(solution)/shard_map/all_to_all | solution.py:551
  32.3 0.0 copy-done
  32.3 0.0 copy-done.1
  32.3 0.0 copy-done.2
  32.3 0.0 copy-done.7
  32.3 0.0 copy-done.8
  32.3 0.0 copy-done.9
  32.3 0.0 copy-start.10
  32.3 0.0 copy-start.11
  32.3 1.2 shard_map.130
  33.5 0.0 copy-start.4
  33.5 13.2 %all_to_all.52.refs_0_.refs_2_ = bf16[8,112,128]{2,1,0:T(8,128)(2,1)S(1)} all-to-all(bf16[8,112,128]{2,1,0:T(8,128)(2,1)S(1)} %get-tuple-element.34), channel_id=1, replica_groups={{4,6,8,10,11,9,7,5},{12,14,16,18,19,17,15,13},{20,22,24,26,27,25,23,21}..., dimensions={0} | all-to-all | bytes 458752 | tf_op jit(solution)/shard_map/all_to_all | solution.py:551
  46.7 0.0 copy-done.10
  46.7 0.0 copy-done.11
  46.7 1.9 %shard_map.131 = bf16[8,48,128]{2,1,0:T(8,128)(2,1)S(1)} custom-call(bf16[8,112,128]{2,1,0:T(8,128)(2,1)S(1)} %all_to_all.52.refs_0_.refs_2_, s32[1]{0:T(128)} %bitcast.2.refs_1_.refs_4_, s32[192]{0:T(256)S(1)} %copy-done.10, s32[1,48]{1,0:T(1,128)S(1)} %bitcast.14), custom_call_target="tpu_custom_call" | custom-call | tf_op jit(solution)/shard_map/pallas_call | solution.py:515
  48.6 0.0 copy-start.6
  48.6 12.5 %all_to_all.53.refs_1_ = bf16[8,48,128]{2,1,0:T(8,128)(2,1)S(1)} all-to-all(bf16[8,48,128]{2,1,0:T(8,128)(2,1)S(1)} %shard_map.131), channel_id=1, replica_groups={{4,6,8,10,11,9,7,5},{12,14,16,18,19,17,15,13},{20,22,24,26,27,25,23,21}..., dimensions={0} | all-to-all | bytes 196608 | tf_op jit(solution)/shard_map/all_to_all | solution.py:551
  61.2 0.0 copy-done.4
  61.2 0.9 shard_map.132
  62.0 12.2 %all_to_all.54.refs_3_ = bf16[8,48,128]{2,1,0:T(8,128)(2,1)S(1)} all-to-all(bf16[8,48,128]{2,1,0:T(8,128)(2,1)S(1)} %get-tuple-element.36), channel_id=1, replica_groups={{4,6,8,10,11,9,7,5},{12,14,16,18,19,17,15,13},{20,22,24,26,27,25,23,21}..., dimensions={0} | all-to-all | bytes 196608 | tf_op jit(solution)/shard_map/all_to_all | solution.py:551
  74.2 3.6 %shard_map.133 = bf16[8,112,128]{2,1,0:T(8,128)(2,1)S(1)} custom-call(s32[1]{0:T(128)} %bitcast.1.refs_0_, f32[2,8]{1,0:T(2,128)S(1)} %copy-done.8, bf16[8,112,128]{2,1,0:T(8,128)(2,1)S(1)} %all_to_all.52.refs_0_.refs_2_, bf16[8,48,128]{2,1,0:T(8,128)(2,1)S(1)} %all_to_all.54.refs_3_, s32[1]{0:T(128)} %bitcast.2.refs_1_.refs_4_, s32[192]{0:T(256)S(1)} %copy-done.10, ...), custom_call_target="tpu_custom_call" | custom-call | tf_op jit(solution)/shard_map/pallas_call | solution.py:515
  77.8 13.4 %all_to_all.55.refs_1_ = bf16[8,112,128]{2,1,0:T(8,128)(2,1)S(1)} all-to-all(bf16[8,112,128]{2,1,0:T(8,128)(2,1)S(1)} %shard_map.133), channel_id=1, replica_groups={{4,6,8,10,11,9,7,5},{12,14,16,18,19,17,15,13},{20,22,24,26,27,25,23,21}..., dimensions={0} | all-to-all | bytes 458752 | tf_op jit(solution)/shard_map/all_to_all | solution.py:551
  91.2 0.0 copy-done.6
  91.2 2.4 %shard_map.134 = (bf16[8,48,128]{2,1,0:T(8,128)(2,1)S(1)}, f32[8,512]{1,0:T(8,128)S(1)}, bf16[144,512]{1,0:T(8,128)(2,1)}, bf16[512,640]{1,0:T(8,128)(2,1)}, bf16[512,640]{1,0:T(8,128)(2,1)}) custom-call(s32[1]{0:T(128)} %bitcast.3.refs_0_, bf16[8,112,128]{2,1,0:T(8,128)(2,1)S(1)} %all_to_all.55.refs_1_, bf16[8,48,128]{2,1,0:T(8,128)(2,1)S(1)} %all_to_all.51.refs_0_.refs_2_, ...), custom_call_target="tpu_custom_call" | custom-call | tf_op jit(solution)/shard_map/pallas_call | solution.py:515
  93.6 0.0 copy-start.3
  93.7 10.2 %all_to_all.56.refs_3_ = bf16[8,48,128]{2,1,0:T(8,128)(2,1)S(1)} all-to-all(bf16[8,48,128]{2,1,0:T(8,128)(2,1)S(1)} %get-tuple-element.40), channel_id=1, replica_groups={{0,2,4,6,1,3,5,7},{8,10,12,14,9,11,13,15},{16,18,20,22,17,19,21,23},{24..., dimensions={0} | all-to-all | bytes 196608 | tf_op jit(solution)/shard_map/all_to_all | solution.py:551
  103.8 3.4 %shard_map.135 = bf16[8,112,128]{2,1,0:T(8,128)(2,1)S(1)} custom-call(s32[1]{0:T(128)} %bitcast.refs_0_, f32[2,8]{1,0:T(2,128)S(1)} %copy-done.8, bf16[8,112,128]{2,1,0:T(8,128)(2,1)S(1)} %all_to_all.50.refs_0_.refs_2_, bf16[8,48,128]{2,1,0:T(8,128)(2,1)S(1)} %all_to_all.56.refs_3_), custom_call_target="tpu_custom_call" | custom-call | tf_op jit(solution)/shard_map/pallas_call | solution.py:515
  107.3 9.9 %all_to_all.57.refs_1_.refs_0_ = bf16[8,112,128]{2,1,0:T(8,128)(2,1)S(1)} all-to-all(bf16[8,112,128]{2,1,0:T(8,128)(2,1)S(1)} %shard_map.135), channel_id=1, replica_groups={{0,2,4,6,1,3,5,7},{8,10,12,14,9,11,13,15},{16,18,20,22,17,19,21,23},{24..., dimensions={0} | all-to-all | bytes 458752 | tf_op jit(solution)/shard_map/all_to_all | solution.py:551
  117.1 9.5 %collective-permute-start.1 = (bf16[512,640]{1,0:T(8,128)(2,1)}, bf16[512,640]{1,0:T(8,128)(2,1)S(1)}, u32[]{:S(2)}, u32[]{:S(2)}) collective-permute-start(bf16[512,640]{1,0:T(8,128)(2,1)} %get-tuple-element.45), channel_id=1, source_target_pairs={{0,64},{64,0},{128,192},{192,128},{1,65},{65,1},{129,193},{193,129... | collective-permute-start | bytes 1966088 | tf_op jit(solution)/shard_map/ppermute | solution.py:564
  126.6 0.7 shard_map.136
  127.3 0.1 collective-permute-start
  127.4 1.7 %collective-permute-done.refs_1_ = bf16[512,384]{1,0:T(8,128)(2,1)S(1)} collective-permute-done((bf16[512,384]{1,0:T(8,128)(2,1)S(1)}, bf16[512,384]{1,0:T(8,128)(2,1)S(1)}, u32[]{:S(2)}, u32[]{:S(2)}) %collective-permute-start) | collective-permute-done | bytes 393248 | tf_op jit(solution)/shard_map/ppermute | solution.py:564
  129.1 0.0 collective-permute-done.1.refs_2_
  129.1 0.0 copy-done.3
  129.1 0.4 shard_map.137
  129.6 21.4 %all_to_all.58.refs_0_ = bf16[8,528,128]{2,1,0:T(8,128)(2,1)S(1)} all-to-all(bf16[8,528,128]{2,1,0:T(8,128)(2,1)S(1)} %shard_map.137), channel_id=1, replica_groups={{56,48,40,32,24,16,8,0},{57,49,41,33,25,17,9,1},{58,50,42,34,26,18,10,2..., dimensions={0} | all-to-all | bytes 2162688 | tf_op jit(solution)/shard_map/all_to_all | solution.py:551
  150.9 0.0 copy-start.5
  150.9 0.2 shard_map.138
  151.1 10.1 %all_to_all.59.refs_0_ = bf16[8,80,128]{2,1,0:T(8,128)(2,1)S(1)} all-to-all(bf16[8,80,128]{2,1,0:T(8,128)(2,1)S(1)} %shard_map.138), channel_id=1, replica_groups={{0,2,4,6,1,3,5,7},{8,10,12,14,9,11,13,15},{16,18,20,22,17,19,21,23},{24..., dimensions={0} | all-to-all | bytes 327680 | tf_op jit(solution)/shard_map/all_to_all | solution.py:551
  161.3 2.8 %collective-permute-start.2 = (f32[80,128]{1,0:T(8,128)S(1)}, f32[80,128]{1,0:T(8,128)S(1)}, u32[]{:S(2)}, u32[]{:S(2)}) collective-permute-start(f32[80,128]{1,0:T(8,128)S(1)} %shard_map.139.refs_0_), channel_id=1, source_target_pairs={{0,128},{64,192},{128,0},{192,64},{1,129},{65,193},{129,1},{193,65... | collective-permute-start | bytes 122888 | tf_op jit(solution)/shard_map/ppermute | solution.py:564
  164.1 1.6 collective-permute-done.2.refs_1_
  165.8 3.3 %collective-permute-start.3 = (f32[80,128]{1,0:T(8,128)S(1)}, f32[80,128]{1,0:T(8,128)S(1)}, u32[]{:S(2)}, u32[]{:S(2)}) collective-permute-start(f32[80,128]{1,0:T(8,128)S(1)} %shard_map.140.refs_1_), channel_id=1, source_target_pairs={{0,64},{64,0},{128,192},{192,128},{1,65},{65,1},{129,193},{193,129... | collective-permute-start | bytes 122888 | tf_op jit(solution)/shard_map/ppermute | solution.py:564
  169.0 0.0 copy-done.5
  169.0 1.1 shard_map.141
  170.1 0.0 collective-permute-done.3.refs_2_
  170.1 0.6 shard_map.142
  (2 shorter events, 0.0 us)
Async XLA Ops:
  0.7 31.5 %copy-start = (bf16[2,512,768]{2,1,0:T(8,128)(2,1)S(1)}, bf16[2,512,768]{2,1,0:T(8,128)(2,1)}, u32[]{:S(2)}) copy-start(bf16[2,512,768]{2,1,0:T(8,128)(2,1)} %refs_1_.9) | copy-start | bytes 4718596
  0.7 31.5 %copy-start.1 = (bf16[2,256,512]{2,1,0:T(8,128)(2,1)S(1)}, bf16[2,256,512]{2,1,0:T(8,128)(2,1)}, u32[]{:S(2)}) copy-start(bf16[2,256,512]{2,1,0:T(8,128)(2,1)} %refs_5_.5) | copy-start | bytes 1572868
  0.8 31.5 %copy-start.2 = (bf16[1,3,48,512]{3,2,1,0:T(8,128)(2,1)S(1)}, bf16[1,3,48,512]{3,2,1,0:T(8,128)(2,1)}, u32[]{:S(2)}) copy-start(bf16[1,3,48,512]{3,2,1,0:T(8,128)(2,1)} %param.9) | copy-start | bytes 442372
  0.8 31.5 %copy-start.7 = (f32[2,512]{1,0:T(2,128)S(1)}, f32[2,512]{1,0:T(2,128)}, u32[]{:S(2)}) copy-start(f32[2,512]{1,0:T(2,128)} %refs_3_.3) | copy-start | bytes 12292
  0.8 31.5 %copy-start.8 = (f32[2,8]{1,0:T(2,128)S(1)}, f32[2,8]{1,0:T(2,128)}, u32[]{:S(2)}) copy-start(f32[2,8]{1,0:T(2,128)} %refs_1_.8) | copy-start | bytes 196
  0.8 31.5 %copy-start.9 = (f32[2,512]{1,0:T(2,128)S(1)}, f32[2,512]{1,0:T(2,128)}, u32[]{:S(2)}) copy-start(f32[2,512]{1,0:T(2,128)} %refs_3_.2) | copy-start | bytes 12292
  32.3 14.4 %copy-start.10 = (s32[192]{0:T(256)S(1)}, s32[192]{0:T(256)}, u32[]{:S(2)}) copy-start(s32[192]{0:T(256)} %refs_5_.4) | copy-start | bytes 2308
  32.3 14.4 %copy-start.11 = (s32[48]{0:T(128)S(1)}, s32[48]{0:T(128)}, u32[]{:S(2)}) copy-start(s32[48]{0:T(128)} %param.17) | copy-start | bytes 580
  33.5 27.6 %copy-start.4 = (bf16[1,3,48,512]{3,2,1,0:T(8,128)(2,1)S(1)}, bf16[1,3,48,512]{3,2,1,0:T(8,128)(2,1)}, u32[]{:S(2)}) copy-start(bf16[1,3,48,512]{3,2,1,0:T(8,128)(2,1)} %param.10) | copy-start | bytes 442372
  48.6 42.6 %copy-start.6 = (bf16[144,512]{1,0:T(8,128)(2,1)S(1)}, bf16[144,512]{1,0:T(8,128)(2,1)}, u32[]{:S(2)}) copy-start(bf16[144,512]{1,0:T(8,128)(2,1)} %get-tuple-element.39.refs_9_) | copy-start | bytes 442372
  93.6 35.5 %copy-start.3 = (bf16[512,640]{1,0:T(8,128)(2,1)S(1)}, bf16[512,640]{1,0:T(8,128)(2,1)}, u32[]{:S(2)}) copy-start(bf16[512,640]{1,0:T(8,128)(2,1)} %get-tuple-element.48.refs_5_) | copy-start | bytes 1966084
  117.1 12.0 %collective-permute-start.1 = (bf16[512,640]{1,0:T(8,128)(2,1)}, bf16[512,640]{1,0:T(8,128)(2,1)S(1)}, u32[]{:S(2)}, u32[]{:S(2)}) collective-permute-start(bf16[512,640]{1,0:T(8,128)(2,1)} %get-tuple-element.45), channel_id=1, source_target_pairs={{0,64},{64,0},{128,192},{192,128},{1,65},{65,1},{129,193},{193,129... | collective-permute-start | bytes 1966088 | tf_op jit(solution)/shard_map/ppermute | solution.py:564
  127.3 1.8 %collective-permute-start = (bf16[512,384]{1,0:T(8,128)(2,1)S(1)}, bf16[512,384]{1,0:T(8,128)(2,1)S(1)}, u32[]{:S(2)}, u32[]{:S(2)}) collective-permute-start(bf16[512,384]{1,0:T(8,128)(2,1)S(1)} %get-tuple-element.44), channel_id=1, source_target_pairs={{0,64},{64,0},{128,192},{192,128},{1,65},{65,1},{129,193},{193,129... | collective-permute-start | bytes 1179656 | tf_op jit(solution)/shard_map/ppermute | solution.py:564
  150.9 18.1 %copy-start.5 = (bf16[144,512]{1,0:T(8,128)(2,1)S(1)}, bf16[144,512]{1,0:T(8,128)(2,1)}, u32[]{:S(2)}) copy-start(bf16[144,512]{1,0:T(8,128)(2,1)} %get-tuple-element.50.refs_2_) | copy-start | bytes 442372
  161.3 4.4 %collective-permute-start.2 = (f32[80,128]{1,0:T(8,128)S(1)}, f32[80,128]{1,0:T(8,128)S(1)}, u32[]{:S(2)}, u32[]{:S(2)}) collective-permute-start(f32[80,128]{1,0:T(8,128)S(1)} %shard_map.139.refs_0_), channel_id=1, source_target_pairs={{0,128},{64,192},{128,0},{192,64},{1,129},{65,193},{129,1},{193,65... | collective-permute-start | bytes 122888 | tf_op jit(solution)/shard_map/ppermute | solution.py:564
  165.8 4.4 %collective-permute-start.3 = (f32[80,128]{1,0:T(8,128)S(1)}, f32[80,128]{1,0:T(8,128)S(1)}, u32[]{:S(2)}, u32[]{:S(2)}) collective-permute-start(f32[80,128]{1,0:T(8,128)S(1)} %shard_map.140.refs_1_), channel_id=1, source_target_pairs={{0,64},{64,0},{128,192},{192,128},{1,65},{65,1},{129,193},{193,129... | collective-permute-start | bytes 122888 | tf_op jit(solution)/shard_map/ppermute | solution.py:564

commit v8 on v7

--- a/solution.py
+++ b/solution.py
@@ -17,7 +17,8 @@
 TOK = 144
 CELLS = WIN * WIN
 ROWS_DEV = 3
-PACK = 48
+PACK = 40
+RUNS = ((0, 40), (40, 80), (80, 112), (112, 144))
 DEVS = 64
 ORDER = (0, 2, 4, 6, 1, 3, 5, 7)
 MOVED = (0, 2, 4, 6, 7, 5, 3, 1)
@@ -109,19 +110,27 @@
 
 
 def unpack_heads(packed_ref):
-    packed = [packed_ref[h].astype(f32) for h in range(HEADS)]
+    packed = packed_ref[...].astype(f32)
     rows = [
-        jnp.concatenate([lane_slice(packed[h], r * HD) for h in range(HEADS)], 1)
-        for r in range(ROWS_DEV)
+        jnp.concatenate([lane_slice(packed[h, : stop - start], run * HD) for h in range(HEADS)], 1)
+        for run, (start, stop) in enumerate(RUNS)
     ]
     return jnp.concatenate(rows, 0).astype(bf16)
 
 
+def padded(run):
+    missing = PACK - run.shape[-2]
+    if not missing:
+        return run
+    return jnp.concatenate([run, jnp.zeros((*run.shape[:-2], missing, run.shape[-1]), f32)], -2)
+
+
 def pack_heads(array, out_ref):
-    zeros = jnp.zeros((PACK, HD), f32)
+    heads = []
     for h in range(HEADS):
-        parts = [lane_slice(array[r * PACK : (r + 1) * PACK], h * HD) for r in range(ROWS_DEV)]
-        out_ref[h] = jnp.concatenate(parts + [zeros], 1).astype(bf16)
+        parts = [padded(lane_slice(array[start:stop], h * HD)) for start, stop in RUNS]
+        heads.append(jnp.concatenate(parts, 1))
+    out_ref[...] = jnp.stack(heads).astype(bf16)
 
 
 def to_windows(array):
@@ -229,13 +238,14 @@
         summed = dot(weights, value)
         yield
         attended = jnp.where(lane < HD, summed * (1.0 / summed[:, HD : HD + 1]), 0.0)
-        per_window[w] = attended.reshape(GROUP, ROWS_DEV, WIN, 128)
+        per_window[w] = attended
 
     together(attend(w, cells) for w, cells in enumerate(to_windows(unpack_cells(x_ref))))
+    cells = from_windows(per_window)
     total = 0.0
-    for r in range(ROWS_DEV):
-        rows = jnp.concatenate([part[:, r] for part in per_window], 1).reshape(GROUP * PACK, 128)
-        total = total + (rows if r == 0 else pltpu.roll(rows, r * HD, 1))
+    for run, (start, stop) in enumerate(RUNS):
+        rows = padded(cells[:, start:stop]).reshape(GROUP * PACK, 128)
+        total = total + (pltpu.roll(rows, run * HD, 1) if run else rows)
     out_ref[...] = total.astype(bf16).reshape(GROUP, PACK, 128)
 
 
@@ -248,9 +258,11 @@
     scale_row = jnp.exp(jnp.full((1, 128), scale_ref[block, head_ref[0]], f32))
     unscale_row = 1.0 / scale_row
     packed = grad_ref[...].astype(f32).reshape(GROUP * PACK, 128)
-    rolled = [packed if r == 0 else pltpu.roll(packed, 128 - r * HD, 1) for r in range(ROWS_DEV)]
-    rolled = [part.reshape(GROUP, 1, 2, WIN, 128) for part in rolled]
-    grads = jnp.concatenate(rolled, 1)
+    rolled = [pltpu.roll(packed, 128 - run * HD, 1) if run else packed for run in range(len(RUNS))]
+    rolled = [
+        part.reshape(GROUP, PACK, 128)[:, : stop - start] for part, (start, stop) in zip(rolled, RUNS)
+    ]
+    grads = to_windows(jnp.concatenate(rolled, 1))
     factors = to_windows(unpack_factors(x_ref))
     results = [None, None]
 
@@ -260,7 +272,7 @@
         query_t = (jnp.concatenate([turned[:HD], turned[96:]], 0) if masks else turned[:HD]).astype(bf16)
         key_t = turned[HD : 2 * HD].astype(bf16)
         value_t = turned[2 * HD : 3 * HD]
-        grad_t = grads[:, :, w].reshape(CELLS, 128).T[:HD]
+        grad_t = grads[w].T[:HD]
         key = with_tags(cells, HD, True) if masks else cells[:, HD : 2 * HD].astype(bf16)
         yield
         scores = dot(key, query_t)

time: 171 us -> 171 us (level)
  no operation moved by 1% of the time
where the time goes in v8:
time: 171 us; the launch traced here: 170 us
  blocking collectives  130 us (76%)
  Pallas kernels  19.8 us (12%)
  starting transfers between devices  15.6 us (9%)
  waiting for transfers between devices  3.35 us (2%)
    all_to_all x10, blocking collectives, exchange(): lax.all_to_all(array, 'rows', 0, 0, axis_index_groups=groups, tiled=True)  130 us
    pallas_call x15, Pallas kernels, call(): pl.pallas_call(wrapped, out_shape=[jax.ShapeDtypeStruct(*out) for out in...  19.8 us
    ppermute x4, starting transfers between devices, swap(): return lax.ppermute(array, 'dp', [(i, i ^ apart) for i in range(4)])  15.6 us
  transfers between devices with their start and end apart: 4, of which 2 were waited for; matrix products, arithmetic and copies ran while one was open for 0% of the time, Pallas kernels for 1%

profile of v8, /device:TPU:1, one launch (start us, length us, event | category | flops | bytes accessed | tf_op | source)
XLA Modules:
  0.0 170.1 jit_solution(13010488868967623043)
XLA Ops:
  0.7 0.0 copy-start
  0.7 0.0 copy-start.1
  0.8 0.0 copy-start.2
  0.8 0.0 copy-start.7
  0.8 0.0 copy-start.8
  0.8 0.0 copy-start.9
  0.8 2.2 %shard_map.128 = bf16[8,112,128]{2,1,0:T(8,128)(2,1)S(1)} custom-call(bf16[144,512]{1,0:T(8,128)(2,1)} %bitcast.9, bf16[2,512,768]{2,1,0:T(8,128)(2,1)} %refs_1_.9, f32[2,8]{1,0:T(2,128)} %refs_1_.8), custom_call_target="tpu_custom_call" | custom-call | tf_op jit(solution)/shard_map/pallas_call | solution.py:527
  3.0 16.3 %all_to_all.50.refs_0_.refs_2_ = bf16[8,112,128]{2,1,0:T(8,128)(2,1)S(1)} all-to-all(bf16[8,112,128]{2,1,0:T(8,128)(2,1)S(1)} %shard_map.128), channel_id=1, replica_groups={{0,2,4,6,1,3,5,7},{8,10,12,14,9,11,13,15},{16,18,20,22,17,19,21,23},{24..., dimensions={0} | all-to-all | bytes 458752 | tf_op jit(solution)/shard_map/all_to_all | solution.py:563
  19.3 1.3 shard_map.129
  20.6 11.5 %all_to_all.51.refs_0_.refs_2_ = bf16[8,40,128]{2,1,0:T(8,128)(2,1)S(1)} all-to-all(bf16[8,40,128]{2,1,0:T(8,128)(2,1)S(1)} %shard_map.129), channel_id=1, replica_groups={{0,2,4,6,1,3,5,7},{8,10,12,14,9,11,13,15},{16,18,20,22,17,19,21,23},{24..., dimensions={0} | all-to-all | bytes 163840 | tf_op jit(solution)/shard_map/all_to_all | solution.py:563
  32.1 0.0 copy-done
  32.1 0.0 copy-done.1
  32.1 0.0 copy-done.2
  32.1 0.0 copy-done.7
  32.1 0.0 copy-done.8
  32.1 0.0 copy-done.9
  32.1 0.0 copy-start.10
  32.1 0.0 copy-start.11
  32.1 0.0 copy-start.4
  32.1 1.2 shard_map.130
  33.4 13.0 %all_to_all.52.refs_0_.refs_2_ = bf16[8,112,128]{2,1,0:T(8,128)(2,1)S(1)} all-to-all(bf16[8,112,128]{2,1,0:T(8,128)(2,1)S(1)} %get-tuple-element.34), channel_id=1, replica_groups={{4,6,8,10,11,9,7,5},{12,14,16,18,19,17,15,13},{20,22,24,26,27,25,23,21}..., dimensions={0} | all-to-all | bytes 458752 | tf_op jit(solution)/shard_map/all_to_all | solution.py:563
  46.4 0.0 copy-done.10
  46.4 0.0 copy-done.11
  46.4 1.9 %shard_map.131 = bf16[8,40,128]{2,1,0:T(8,128)(2,1)S(1)} custom-call(bf16[8,112,128]{2,1,0:T(8,128)(2,1)S(1)} %all_to_all.52.refs_0_.refs_2_, s32[1]{0:T(128)} %bitcast.2.refs_1_.refs_4_, s32[192]{0:T(256)S(1)} %copy-done.10, s32[1,48]{1,0:T(1,128)S(1)} %bitcast.14), custom_call_target="tpu_custom_call" | custom-call | tf_op jit(solution)/shard_map/pallas_call | solution.py:527
  48.3 0.0 copy-start.6
  48.3 12.4 %all_to_all.53.refs_1_ = bf16[8,40,128]{2,1,0:T(8,128)(2,1)S(1)} all-to-all(bf16[8,40,128]{2,1,0:T(8,128)(2,1)S(1)} %shard_map.131), channel_id=1, replica_groups={{4,6,8,10,11,9,7,5},{12,14,16,18,19,17,15,13},{20,22,24,26,27,25,23,21}..., dimensions={0} | all-to-all | bytes 163840 | tf_op jit(solution)/shard_map/all_to_all | solution.py:563
  60.8 0.0 copy-done.4
  60.8 0.9 shard_map.132
  61.6 12.2 %all_to_all.54.refs_3_ = bf16[8,40,128]{2,1,0:T(8,128)(2,1)S(1)} all-to-all(bf16[8,40,128]{2,1,0:T(8,128)(2,1)S(1)} %get-tuple-element.36), channel_id=1, replica_groups={{4,6,8,10,11,9,7,5},{12,14,16,18,19,17,15,13},{20,22,24,26,27,25,23,21}..., dimensions={0} | all-to-all | bytes 163840 | tf_op jit(solution)/shard_map/all_to_all | solution.py:563
  73.8 3.6 %shard_map.133 = bf16[8,112,128]{2,1,0:T(8,128)(2,1)S(1)} custom-call(s32[1]{0:T(128)} %bitcast.1.refs_0_, f32[2,8]{1,0:T(2,128)S(1)} %copy-done.8, bf16[8,112,128]{2,1,0:T(8,128)(2,1)S(1)} %all_to_all.52.refs_0_.refs_2_, bf16[8,40,128]{2,1,0:T(8,128)(2,1)S(1)} %all_to_all.54.refs_3_, s32[1]{0:T(128)} %bitcast.2.refs_1_.refs_4_, s32[192]{0:T(256)S(1)} %copy-done.10, ...), custom_call_target="tpu_custom_call" | custom-call | tf_op jit(solution)/shard_map/pallas_call | solution.py:527
  77.4 13.4 %all_to_all.55.refs_1_ = bf16[8,112,128]{2,1,0:T(8,128)(2,1)S(1)} all-to-all(bf16[8,112,128]{2,1,0:T(8,128)(2,1)S(1)} %shard_map.133), channel_id=1, replica_groups={{4,6,8,10,11,9,7,5},{12,14,16,18,19,17,15,13},{20,22,24,26,27,25,23,21}..., dimensions={0} | all-to-all | bytes 458752 | tf_op jit(solution)/shard_map/all_to_all | solution.py:563
  90.8 0.0 copy-done.6
  90.9 2.4 %shard_map.134 = (bf16[8,40,128]{2,1,0:T(8,128)(2,1)S(1)}, f32[8,512]{1,0:T(8,128)S(1)}, bf16[144,512]{1,0:T(8,128)(2,1)}, bf16[512,640]{1,0:T(8,128)(2,1)}, bf16[512,640]{1,0:T(8,128)(2,1)}) custom-call(s32[1]{0:T(128)} %bitcast.3.refs_0_, bf16[8,112,128]{2,1,0:T(8,128)(2,1)S(1)} %all_to_all.55.refs_1_, bf16[8,40,128]{2,1,0:T(8,128)(2,1)S(1)} %all_to_all.51.refs_0_.refs_2_, ...), custom_call_target="tpu_custom_call" | custom-call | tf_op jit(solution)/shard_map/pallas_call | solution.py:527
  93.2 0.0 copy-start.3
  93.2 10.1 %all_to_all.56.refs_3_ = bf16[8,40,128]{2,1,0:T(8,128)(2,1)S(1)} all-to-all(bf16[8,40,128]{2,1,0:T(8,128)(2,1)S(1)} %get-tuple-element.40), channel_id=1, replica_groups={{0,2,4,6,1,3,5,7},{8,10,12,14,9,11,13,15},{16,18,20,22,17,19,21,23},{24..., dimensions={0} | all-to-all | bytes 163840 | tf_op jit(solution)/shard_map/all_to_all | solution.py:563
  103.3 3.4 %shard_map.135 = bf16[8,112,128]{2,1,0:T(8,128)(2,1)S(1)} custom-call(s32[1]{0:T(128)} %bitcast.refs_0_, f32[2,8]{1,0:T(2,128)S(1)} %copy-done.8, bf16[8,112,128]{2,1,0:T(8,128)(2,1)S(1)} %all_to_all.50.refs_0_.refs_2_, bf16[8,40,128]{2,1,0:T(8,128)(2,1)S(1)} %all_to_all.56.refs_3_), custom_call_target="tpu_custom_call" | custom-call | tf_op jit(solution)/shard_map/pallas_call | solution.py:527
  106.7 9.9 %all_to_all.57.refs_1_.refs_0_ = bf16[8,112,128]{2,1,0:T(8,128)(2,1)S(1)} all-to-all(bf16[8,112,128]{2,1,0:T(8,128)(2,1)S(1)} %shard_map.135), channel_id=1, replica_groups={{0,2,4,6,1,3,5,7},{8,10,12,14,9,11,13,15},{16,18,20,22,17,19,21,23},{24..., dimensions={0} | all-to-all | bytes 458752 | tf_op jit(solution)/shard_map/all_to_all | solution.py:563
  116.6 9.4 %collective-permute-start.1 = (bf16[512,640]{1,0:T(8,128)(2,1)}, bf16[512,640]{1,0:T(8,128)(2,1)S(1)}, u32[]{:S(2)}, u32[]{:S(2)}) collective-permute-start(bf16[512,640]{1,0:T(8,128)(2,1)} %get-tuple-element.45), channel_id=1, source_target_pairs={{0,64},{64,0},{128,192},{192,128},{1,65},{65,1},{129,193},{193,129... | collective-permute-start | bytes 1966088 | tf_op jit(solution)/shard_map/ppermute | solution.py:576
  126.1 0.7 shard_map.136
  126.7 0.1 collective-permute-start
  126.8 1.7 %collective-permute-done.refs_1_ = bf16[512,384]{1,0:T(8,128)(2,1)S(1)} collective-permute-done((bf16[512,384]{1,0:T(8,128)(2,1)S(1)}, bf16[512,384]{1,0:T(8,128)(2,1)S(1)}, u32[]{:S(2)}, u32[]{:S(2)}) %collective-permute-start) | collective-permute-done | bytes 393248 | tf_op jit(solution)/shard_map/ppermute | solution.py:576
  128.5 0.0 collective-permute-done.1.refs_2_
  128.5 0.0 copy-done.3
  128.6 0.4 shard_map.137
  129.0 21.4 %all_to_all.58.refs_0_ = bf16[8,528,128]{2,1,0:T(8,128)(2,1)S(1)} all-to-all(bf16[8,528,128]{2,1,0:T(8,128)(2,1)S(1)} %shard_map.137), channel_id=1, replica_groups={{56,48,40,32,24,16,8,0},{57,49,41,33,25,17,9,1},{58,50,42,34,26,18,10,2..., dimensions={0} | all-to-all | bytes 2162688 | tf_op jit(solution)/shard_map/all_to_all | solution.py:563
  150.3 0.0 copy-start.5
  150.3 0.2 shard_map.138
  150.6 10.1 %all_to_all.59.refs_0_ = bf16[8,80,128]{2,1,0:T(8,128)(2,1)S(1)} all-to-all(bf16[8,80,128]{2,1,0:T(8,128)(2,1)S(1)} %shard_map.138), channel_id=1, replica_groups={{0,2,4,6,1,3,5,7},{8,10,12,14,9,11,13,15},{16,18,20,22,17,19,21,23},{24..., dimensions={0} | all-to-all | bytes 327680 | tf_op jit(solution)/shard_map/all_to_all | solution.py:563
  160.7 2.8 %collective-permute-start.2 = (f32[80,128]{1,0:T(8,128)S(1)}, f32[80,128]{1,0:T(8,128)S(1)}, u32[]{:S(2)}, u32[]{:S(2)}) collective-permute-start(f32[80,128]{1,0:T(8,128)S(1)} %shard_map.139.refs_0_), channel_id=1, source_target_pairs={{0,128},{64,192},{128,0},{192,64},{1,129},{65,193},{129,1},{193,65... | collective-permute-start | bytes 122888 | tf_op jit(solution)/shard_map/ppermute | solution.py:576
  163.5 1.6 collective-permute-done.2.refs_1_
  165.1 3.3 %collective-permute-start.3 = (f32[80,128]{1,0:T(8,128)S(1)}, f32[80,128]{1,0:T(8,128)S(1)}, u32[]{:S(2)}, u32[]{:S(2)}) collective-permute-start(f32[80,128]{1,0:T(8,128)S(1)} %shard_map.140.refs_1_), channel_id=1, source_target_pairs={{0,64},{64,0},{128,192},{192,128},{1,65},{65,1},{129,193},{193,129... | collective-permute-start | bytes 122888 | tf_op jit(solution)/shard_map/ppermute | solution.py:576
  168.4 0.0 copy-done.5
  168.4 1.1 shard_map.141
  169.5 0.0 collective-permute-done.3.refs_2_
  169.5 0.6 shard_map.142
  (2 shorter events, 0.0 us)
Async XLA Ops:
  0.7 31.3 %copy-start = (bf16[2,512,768]{2,1,0:T(8,128)(2,1)S(1)}, bf16[2,512,768]{2,1,0:T(8,128)(2,1)}, u32[]{:S(2)}) copy-start(bf16[2,512,768]{2,1,0:T(8,128)(2,1)} %refs_1_.9) | copy-start | bytes 4718596
  0.7 31.3 %copy-start.1 = (bf16[2,256,512]{2,1,0:T(8,128)(2,1)S(1)}, bf16[2,256,512]{2,1,0:T(8,128)(2,1)}, u32[]{:S(2)}) copy-start(bf16[2,256,512]{2,1,0:T(8,128)(2,1)} %refs_5_.5) | copy-start | bytes 1572868
  0.8 31.3 %copy-start.2 = (bf16[1,3,48,512]{3,2,1,0:T(8,128)(2,1)S(1)}, bf16[1,3,48,512]{3,2,1,0:T(8,128)(2,1)}, u32[]{:S(2)}) copy-start(bf16[1,3,48,512]{3,2,1,0:T(8,128)(2,1)} %param.9) | copy-start | bytes 442372
  0.8 31.3 %copy-start.7 = (f32[2,512]{1,0:T(2,128)S(1)}, f32[2,512]{1,0:T(2,128)}, u32[]{:S(2)}) copy-start(f32[2,512]{1,0:T(2,128)} %refs_3_.3) | copy-start | bytes 12292
  0.8 31.3 %copy-start.8 = (f32[2,8]{1,0:T(2,128)S(1)}, f32[2,8]{1,0:T(2,128)}, u32[]{:S(2)}) copy-start(f32[2,8]{1,0:T(2,128)} %refs_1_.8) | copy-start | bytes 196
  0.8 31.3 %copy-start.9 = (f32[2,512]{1,0:T(2,128)S(1)}, f32[2,512]{1,0:T(2,128)}, u32[]{:S(2)}) copy-start(f32[2,512]{1,0:T(2,128)} %refs_3_.2) | copy-start | bytes 12292
  32.1 14.3 %copy-start.10 = (s32[192]{0:T(256)S(1)}, s32[192]{0:T(256)}, u32[]{:S(2)}) copy-start(s32[192]{0:T(256)} %refs_5_.4) | copy-start | bytes 2308
  32.1 14.3 %copy-start.11 = (s32[48]{0:T(128)S(1)}, s32[48]{0:T(128)}, u32[]{:S(2)}) copy-start(s32[48]{0:T(128)} %param.17) | copy-start | bytes 580
  32.1 28.6 %copy-start.4 = (bf16[1,3,48,512]{3,2,1,0:T(8,128)(2,1)S(1)}, bf16[1,3,48,512]{3,2,1,0:T(8,128)(2,1)}, u32[]{:S(2)}) copy-start(bf16[1,3,48,512]{3,2,1,0:T(8,128)(2,1)} %param.10) | copy-start | bytes 442372
  48.3 42.5 %copy-start.6 = (bf16[144,512]{1,0:T(8,128)(2,1)S(1)}, bf16[144,512]{1,0:T(8,128)(2,1)}, u32[]{:S(2)}) copy-start(bf16[144,512]{1,0:T(8,128)(2,1)} %get-tuple-element.39.refs_9_) | copy-start | bytes 442372
  93.2 35.3 %copy-start.3 = (bf16[512,640]{1,0:T(8,128)(2,1)S(1)}, bf16[512,640]{1,0:T(8,128)(2,1)}, u32[]{:S(2)}) copy-start(bf16[512,640]{1,0:T(8,128)(2,1)} %get-tuple-element.48.refs_5_) | copy-start | bytes 1966084
  116.6 11.9 %collective-permute-start.1 = (bf16[512,640]{1,0:T(8,128)(2,1)}, bf16[512,640]{1,0:T(8,128)(2,1)S(1)}, u32[]{:S(2)}, u32[]{:S(2)}) collective-permute-start(bf16[512,640]{1,0:T(8,128)(2,1)} %get-tuple-element.45), channel_id=1, source_target_pairs={{0,64},{64,0},{128,192},{192,128},{1,65},{65,1},{129,193},{193,129... | collective-permute-start | bytes 1966088 | tf_op jit(solution)/shard_map/ppermute | solution.py:576
  126.7 1.8 %collective-permute-start = (bf16[512,384]{1,0:T(8,128)(2,1)S(1)}, bf16[512,384]{1,0:T(8,128)(2,1)S(1)}, u32[]{:S(2)}, u32[]{:S(2)}) collective-permute-start(bf16[512,384]{1,0:T(8,128)(2,1)S(1)} %get-tuple-element.44), channel_id=1, source_target_pairs={{0,64},{64,0},{128,192},{192,128},{1,65},{65,1},{129,193},{193,129... | collective-permute-start | bytes 1179656 | tf_op jit(solution)/shard_map/ppermute | solution.py:576
  150.3 18.0 %copy-start.5 = (bf16[144,512]{1,0:T(8,128)(2,1)S(1)}, bf16[144,512]{1,0:T(8,128)(2,1)}, u32[]{:S(2)}) copy-start(bf16[144,512]{1,0:T(8,128)(2,1)} %get-tuple-element.50.refs_2_) | copy-start | bytes 442372
  160.7 4.4 %collective-permute-start.2 = (f32[80,128]{1,0:T(8,128)S(1)}, f32[80,128]{1,0:T(8,128)S(1)}, u32[]{:S(2)}, u32[]{:S(2)}) collective-permute-start(f32[80,128]{1,0:T(8,128)S(1)} %shard_map.139.refs_0_), channel_id=1, source_target_pairs={{0,128},{64,192},{128,0},{192,64},{1,129},{65,193},{129,1},{193,65... | collective-permute-start | bytes 122888 | tf_op jit(solution)/shard_map/ppermute | solution.py:576
  165.1 4.4 %collective-permute-start.3 = (f32[80,128]{1,0:T(8,128)S(1)}, f32[80,128]{1,0:T(8,128)S(1)}, u32[]{:S(2)}, u32[]{:S(2)}) collective-permute-start(f32[80,128]{1,0:T(8,128)S(1)} %shard_map.140.refs_1_), channel_id=1, source_target_pairs={{0,64},{64,0},{128,192},{192,128},{1,65},{65,1},{129,193},{193,129... | collective-permute-start | bytes 122888 | tf_op jit(solution)/shard_map/ppermute | solution.py:576

commit v9 on v8

--- a/solution.py
+++ b/solution.py
@@ -388,10 +388,9 @@
     out_ref[...] = (grad_ref[...].astype(f32) + dot_t(gather_qkv(qkv_ref), w_ref[...])).astype(bf16)
 
 
-def last_kernel(core_ref, qkv_ref, tokens_ref, kept_ref, given_ref):
-    kept, given = halves(gather_qkv(qkv_ref), core_ref[0])
-    given_ref[...] = dot_0(tokens_ref[...], given).astype(bf16)
-    kept_ref[...] = dot_0(tokens_ref[...], kept).astype(bf16)
+def late_kernel(given, core_ref, qkv_ref, tokens_ref, out_ref):
+    half = halves(gather_qkv(qkv_ref), core_ref[0])[given]
+    out_ref[...] = dot_0(tokens_ref[...], half).astype(bf16)
 
 
 def parts_kernel(late_ref, got_late_ref, got_ref, gains0_ref, gains1_ref, kept_ref, parts_ref):
@@ -418,6 +417,8 @@
 def first_sum_kernel(parts_ref, out_ref):
     total = jnp.sum(parts_ref[...].astype(f32), 0)
     gains = total[TILES * C // 8 :]
+    high, low = split_two(gains + pltpu.roll(gains, 15, 0))
+    gains = jnp.where(iota(gains.shape, 0) % 2 == 0, high, pltpu.roll(low, 1, 0))
     total = total[: TILES * C // 8].reshape(TILES, 8, 8, 128)
     for place in range(8):
         rolled = pltpu.roll(gains, 128 - 8 * place, 1) if place else gains
@@ -448,7 +449,7 @@
 
 
 def pieces_of(shape):
-    return 4 if shape[0] % 64 == 0 and shape[0] * shape[1] >= 2**18 else 1
+    return 2 if shape[0] % 64 == 0 and shape[0] * shape[1] >= 2**18 else 1
 
 
 def copies_of(source, target, sems, first):
@@ -612,8 +613,10 @@
     qkv0 = exchange(qkv0, aligned)
     qkv0, given = lax.optimization_barrier((qkv0, given))
     got = swap(given, 1)
-    late, given_late = call(last_kernel, [half_late, half_late], (core,), (qkv0, tokens0))
+    (given_late,) = call(functools.partial(late_kernel, 1), [half_late], (core,), (qkv0, tokens0))
     got_late = swap(given_late, 1)
+    qkv0, given_late = lax.optimization_barrier((qkv0, given_late))
+    (late,) = call(functools.partial(late_kernel, 0), [half_late], (core,), (qkv0, tokens0))
     (parts,) = call(
         parts_kernel,
         [((8, SENT, 128), bf16)],

time: 171 us -> 170 us (level)
    pallas_call x15 -> x16, Pallas kernels: 19.8 us -> 20.2 us  [call(): pl.pallas_call(wrapped, out_shape=[jax.ShapeDtypeStruct(*out) for out in...]
where the time goes in v9:
time: 170 us
  blocking collectives  130 us (76%)
  Pallas kernels  20.2 us (12%)
  starting transfers between devices  15.6 us (9%)
  waiting for transfers between devices  2.79 us (2%)
    all_to_all x10, blocking collectives, exchange(): lax.all_to_all(array, 'rows', 0, 0, axis_index_groups=groups, tiled=True)  130 us
    pallas_call x16, Pallas kernels, call(): pl.pallas_call(wrapped, out_shape=[jax.ShapeDtypeStruct(*out) for out in...  20.2 us
    ppermute x4, starting transfers between devices, swap(): return lax.ppermute(array, 'dp', [(i, i ^ apart) for i in range(4)])  15.6 us
  transfers between devices with their start and end apart: 4, of which 2 were waited for; matrix products, arithmetic and copies ran while one was open for 0% of the time, Pallas kernels for 1%

profile of v9, /device:TPU:1, one launch (start us, length us, event | category | flops | bytes accessed | tf_op | source)
XLA Modules:
  0.0 170.0 jit_solution(12551695155971417232)
XLA Ops:
  0.7 0.0 copy-start
  0.7 0.0 copy-start.1
  0.8 0.0 copy-start.2
  0.8 0.0 copy-start.7
  0.8 0.0 copy-start.8
  0.8 0.0 copy-start.9
  0.8 2.1 %shard_map.128 = bf16[8,112,128]{2,1,0:T(8,128)(2,1)S(1)} custom-call(bf16[144,512]{1,0:T(8,128)(2,1)} %bitcast.9, bf16[2,512,768]{2,1,0:T(8,128)(2,1)} %refs_1_.9, f32[2,8]{1,0:T(2,128)} %refs_1_.8), custom_call_target="tpu_custom_call" | custom-call | tf_op jit(solution)/shard_map/pallas_call | solution.py:528
  2.9 16.3 %all_to_all.50.refs_0_.refs_2_ = bf16[8,112,128]{2,1,0:T(8,128)(2,1)S(1)} all-to-all(bf16[8,112,128]{2,1,0:T(8,128)(2,1)S(1)} %shard_map.128), channel_id=1, replica_groups={{0,2,4,6,1,3,5,7},{8,10,12,14,9,11,13,15},{16,18,20,22,17,19,21,23},{24..., dimensions={0} | all-to-all | bytes 458752 | tf_op jit(solution)/shard_map/all_to_all | solution.py:564
  19.2 1.3 shard_map.129
  20.5 11.5 %all_to_all.51.refs_0_.refs_2_ = bf16[8,40,128]{2,1,0:T(8,128)(2,1)S(1)} all-to-all(bf16[8,40,128]{2,1,0:T(8,128)(2,1)S(1)} %shard_map.129), channel_id=1, replica_groups={{0,2,4,6,1,3,5,7},{8,10,12,14,9,11,13,15},{16,18,20,22,17,19,21,23},{24..., dimensions={0} | all-to-all | bytes 163840 | tf_op jit(solution)/shard_map/all_to_all | solution.py:564
  32.0 0.0 copy-done
  32.0 0.0 copy-done.1
  32.0 0.0 copy-done.2
  32.0 0.0 copy-done.7
  32.0 0.0 copy-done.8
  32.0 0.0 copy-done.9
  32.0 0.0 copy-start.10
  32.0 0.0 copy-start.11
  32.1 0.0 copy-start.4
  32.1 1.2 shard_map.130
  33.3 13.0 %all_to_all.52.refs_0_.refs_2_ = bf16[8,112,128]{2,1,0:T(8,128)(2,1)S(1)} all-to-all(bf16[8,112,128]{2,1,0:T(8,128)(2,1)S(1)} %get-tuple-element.33), channel_id=1, replica_groups={{4,6,8,10,11,9,7,5},{12,14,16,18,19,17,15,13},{20,22,24,26,27,25,23,21}..., dimensions={0} | all-to-all | bytes 458752 | tf_op jit(solution)/shard_map/all_to_all | solution.py:564
  46.3 0.0 copy-done.10
  46.3 0.0 copy-done.11
  46.3 1.9 %shard_map.131 = bf16[8,40,128]{2,1,0:T(8,128)(2,1)S(1)} custom-call(bf16[8,112,128]{2,1,0:T(8,128)(2,1)S(1)} %all_to_all.52.refs_0_.refs_2_, s32[1]{0:T(128)} %bitcast.2.refs_1_.refs_4_, s32[192]{0:T(256)S(1)} %copy-done.10, s32[1,48]{1,0:T(1,128)S(1)} %bitcast.15), custom_call_target="tpu_custom_call" | custom-call | tf_op jit(solution)/shard_map/pallas_call | solution.py:528
  48.2 0.0 copy-start.6
  48.2 12.4 %all_to_all.53.refs_1_ = bf16[8,40,128]{2,1,0:T(8,128)(2,1)S(1)} all-to-all(bf16[8,40,128]{2,1,0:T(8,128)(2,1)S(1)} %shard_map.131), channel_id=1, replica_groups={{4,6,8,10,11,9,7,5},{12,14,16,18,19,17,15,13},{20,22,24,26,27,25,23,21}..., dimensions={0} | all-to-all | bytes 163840 | tf_op jit(solution)/shard_map/all_to_all | solution.py:564
  60.7 0.0 copy-done.4
  60.7 0.9 shard_map.132
  61.6 12.1 %all_to_all.54.refs_3_ = bf16[8,40,128]{2,1,0:T(8,128)(2,1)S(1)} all-to-all(bf16[8,40,128]{2,1,0:T(8,128)(2,1)S(1)} %get-tuple-element.35), channel_id=1, replica_groups={{4,6,8,10,11,9,7,5},{12,14,16,18,19,17,15,13},{20,22,24,26,27,25,23,21}..., dimensions={0} | all-to-all | bytes 163840 | tf_op jit(solution)/shard_map/all_to_all | solution.py:564
  73.7 3.6 %shard_map.133 = bf16[8,112,128]{2,1,0:T(8,128)(2,1)S(1)} custom-call(s32[1]{0:T(128)} %bitcast.1.refs_0_, f32[2,8]{1,0:T(2,128)S(1)} %copy-done.8, bf16[8,112,128]{2,1,0:T(8,128)(2,1)S(1)} %all_to_all.52.refs_0_.refs_2_, bf16[8,40,128]{2,1,0:T(8,128)(2,1)S(1)} %all_to_all.54.refs_3_, s32[1]{0:T(128)} %bitcast.2.refs_1_.refs_4_, s32[192]{0:T(256)S(1)} %copy-done.10, ...), custom_call_target="tpu_custom_call" | custom-call | tf_op jit(solution)/shard_map/pallas_call | solution.py:528
  77.3 13.4 %all_to_all.55.refs_1_ = bf16[8,112,128]{2,1,0:T(8,128)(2,1)S(1)} all-to-all(bf16[8,112,128]{2,1,0:T(8,128)(2,1)S(1)} %shard_map.133), channel_id=1, replica_groups={{4,6,8,10,11,9,7,5},{12,14,16,18,19,17,15,13},{20,22,24,26,27,25,23,21}..., dimensions={0} | all-to-all | bytes 458752 | tf_op jit(solution)/shard_map/all_to_all | solution.py:564
  90.8 0.0 copy-done.6
  90.8 2.4 %shard_map.134 = (bf16[8,40,128]{2,1,0:T(8,128)(2,1)S(1)}, f32[8,512]{1,0:T(8,128)S(1)}, bf16[144,512]{1,0:T(8,128)(2,1)}, bf16[512,640]{1,0:T(8,128)(2,1)}, bf16[512,640]{1,0:T(8,128)(2,1)}) custom-call(s32[1]{0:T(128)} %bitcast.3.refs_0_, bf16[8,112,128]{2,1,0:T(8,128)(2,1)S(1)} %all_to_all.55.refs_1_, bf16[8,40,128]{2,1,0:T(8,128)(2,1)S(1)} %all_to_all.51.refs_0_.refs_2_, ...), custom_call_target="tpu_custom_call" | custom-call | tf_op jit(solution)/shard_map/pallas_call | solution.py:528
  93.1 0.0 copy-start.12
  93.2 10.1 %all_to_all.56.refs_3_ = bf16[8,40,128]{2,1,0:T(8,128)(2,1)S(1)} all-to-all(bf16[8,40,128]{2,1,0:T(8,128)(2,1)S(1)} %get-tuple-element.39), channel_id=1, replica_groups={{0,2,4,6,1,3,5,7},{8,10,12,14,9,11,13,15},{16,18,20,22,17,19,21,23},{24..., dimensions={0} | all-to-all | bytes 163840 | tf_op jit(solution)/shard_map/all_to_all | solution.py:564
  103.2 3.4 %shard_map.135 = bf16[8,112,128]{2,1,0:T(8,128)(2,1)S(1)} custom-call(s32[1]{0:T(128)} %bitcast.refs_0_, f32[2,8]{1,0:T(2,128)S(1)} %copy-done.8, bf16[8,112,128]{2,1,0:T(8,128)(2,1)S(1)} %all_to_all.50.refs_0_.refs_2_, bf16[8,40,128]{2,1,0:T(8,128)(2,1)S(1)} %all_to_all.56.refs_3_), custom_call_target="tpu_custom_call" | custom-call | tf_op jit(solution)/shard_map/pallas_call | solution.py:528
  106.7 0.0 copy-start.3
  106.7 10.0 %all_to_all.57.refs_1_.refs_0_ = bf16[8,112,128]{2,1,0:T(8,128)(2,1)S(1)} all-to-all(bf16[8,112,128]{2,1,0:T(8,128)(2,1)S(1)} %shard_map.135), channel_id=1, replica_groups={{0,2,4,6,1,3,5,7},{8,10,12,14,9,11,13,15},{16,18,20,22,17,19,21,23},{24..., dimensions={0} | all-to-all | bytes 458752 | tf_op jit(solution)/shard_map/all_to_all | solution.py:564
  116.7 0.0 copy-done.12
  116.7 9.4 %collective-permute-start.1 = (bf16[512,640]{1,0:T(8,128)(2,1)S(1)}, bf16[512,640]{1,0:T(8,128)(2,1)S(1)}, u32[]{:S(2)}, u32[]{:S(2)}) collective-permute-start(bf16[512,640]{1,0:T(8,128)(2,1)S(1)} %copy-done.12), channel_id=1, source_target_pairs={{0,64},{64,0},{128,192},{192,128},{1,65},{65,1},{129,193},{193,129... | collective-permute-start | bytes 1966088 | tf_op jit(solution)/shard_map/ppermute | solution.py:577
  126.1 0.5 shard_map.136
  126.7 0.1 collective-permute-start
  126.8 0.5 shard_map.137.refs_0_
  127.3 1.2 collective-permute-done.refs_1_
  128.5 0.0 collective-permute-done.1.refs_2_
  128.5 0.0 copy-done.3
  128.5 0.4 shard_map.138
  128.9 21.3 %all_to_all.58.refs_0_ = bf16[8,528,128]{2,1,0:T(8,128)(2,1)S(1)} all-to-all(bf16[8,528,128]{2,1,0:T(8,128)(2,1)S(1)} %shard_map.138), channel_id=1, replica_groups={{56,48,40,32,24,16,8,0},{57,49,41,33,25,17,9,1},{58,50,42,34,26,18,10,2..., dimensions={0} | all-to-all | bytes 2162688 | tf_op jit(solution)/shard_map/all_to_all | solution.py:564
  150.3 0.0 copy-start.5
  150.3 0.2 shard_map.139
  150.5 10.1 %all_to_all.59.refs_0_ = bf16[8,80,128]{2,1,0:T(8,128)(2,1)S(1)} all-to-all(bf16[8,80,128]{2,1,0:T(8,128)(2,1)S(1)} %shard_map.139), channel_id=1, replica_groups={{0,2,4,6,1,3,5,7},{8,10,12,14,9,11,13,15},{16,18,20,22,17,19,21,23},{24..., dimensions={0} | all-to-all | bytes 327680 | tf_op jit(solution)/shard_map/all_to_all | solution.py:564
  160.6 2.8 %collective-permute-start.2 = (f32[80,128]{1,0:T(8,128)S(1)}, f32[80,128]{1,0:T(8,128)S(1)}, u32[]{:S(2)}, u32[]{:S(2)}) collective-permute-start(f32[80,128]{1,0:T(8,128)S(1)} %shard_map.140.refs_0_), channel_id=1, source_target_pairs={{0,128},{64,192},{128,0},{192,64},{1,129},{65,193},{129,1},{193,65... | collective-permute-start | bytes 122888 | tf_op jit(solution)/shard_map/ppermute | solution.py:577
  163.4 1.6 collective-permute-done.2.refs_1_
  165.0 3.2 %collective-permute-start.3 = (f32[80,128]{1,0:T(8,128)S(1)}, f32[80,128]{1,0:T(8,128)S(1)}, u32[]{:S(2)}, u32[]{:S(2)}) collective-permute-start(f32[80,128]{1,0:T(8,128)S(1)} %shard_map.141.refs_1_), channel_id=1, source_target_pairs={{0,64},{64,0},{128,192},{192,128},{1,65},{65,1},{129,193},{193,129... | collective-permute-start | bytes 122888 | tf_op jit(solution)/shard_map/ppermute | solution.py:577
  168.3 0.0 copy-done.5
  168.3 1.1 shard_map.142
  169.4 0.0 collective-permute-done.3.refs_2_
  169.4 0.6 shard_map.143
  (2 shorter events, 0.0 us)
Async XLA Ops:
  0.7 31.3 %copy-start = (bf16[2,512,768]{2,1,0:T(8,128)(2,1)S(1)}, bf16[2,512,768]{2,1,0:T(8,128)(2,1)}, u32[]{:S(2)}) copy-start(bf16[2,512,768]{2,1,0:T(8,128)(2,1)} %refs_1_.9) | copy-start | bytes 4718596
  0.7 31.2 %copy-start.1 = (bf16[2,256,512]{2,1,0:T(8,128)(2,1)S(1)}, bf16[2,256,512]{2,1,0:T(8,128)(2,1)}, u32[]{:S(2)}) copy-start(bf16[2,256,512]{2,1,0:T(8,128)(2,1)} %refs_5_.5) | copy-start | bytes 1572868
  0.8 31.2 %copy-start.2 = (bf16[1,3,48,512]{3,2,1,0:T(8,128)(2,1)S(1)}, bf16[1,3,48,512]{3,2,1,0:T(8,128)(2,1)}, u32[]{:S(2)}) copy-start(bf16[1,3,48,512]{3,2,1,0:T(8,128)(2,1)} %param.9) | copy-start | bytes 442372
  0.8 31.2 %copy-start.7 = (f32[2,512]{1,0:T(2,128)S(1)}, f32[2,512]{1,0:T(2,128)}, u32[]{:S(2)}) copy-start(f32[2,512]{1,0:T(2,128)} %refs_3_.3) | copy-start | bytes 12292
  0.8 31.2 %copy-start.8 = (f32[2,8]{1,0:T(2,128)S(1)}, f32[2,8]{1,0:T(2,128)}, u32[]{:S(2)}) copy-start(f32[2,8]{1,0:T(2,128)} %refs_1_.8) | copy-start | bytes 196
  0.8 31.2 %copy-start.9 = (f32[2,512]{1,0:T(2,128)S(1)}, f32[2,512]{1,0:T(2,128)}, u32[]{:S(2)}) copy-start(f32[2,512]{1,0:T(2,128)} %refs_3_.2) | copy-start | bytes 12292
  32.0 14.3 %copy-start.10 = (s32[192]{0:T(256)S(1)}, s32[192]{0:T(256)}, u32[]{:S(2)}) copy-start(s32[192]{0:T(256)} %refs_5_.4) | copy-start | bytes 2308
  32.0 14.3 %copy-start.11 = (s32[48]{0:T(128)S(1)}, s32[48]{0:T(128)}, u32[]{:S(2)}) copy-start(s32[48]{0:T(128)} %param.17) | copy-start | bytes 580
  32.1 28.6 %copy-start.4 = (bf16[1,3,48,512]{3,2,1,0:T(8,128)(2,1)S(1)}, bf16[1,3,48,512]{3,2,1,0:T(8,128)(2,1)}, u32[]{:S(2)}) copy-start(bf16[1,3,48,512]{3,2,1,0:T(8,128)(2,1)} %param.10) | copy-start | bytes 442372
  48.2 42.5 %copy-start.6 = (bf16[144,512]{1,0:T(8,128)(2,1)S(1)}, bf16[144,512]{1,0:T(8,128)(2,1)}, u32[]{:S(2)}) copy-start(bf16[144,512]{1,0:T(8,128)(2,1)} %get-tuple-element.38.refs_9_) | copy-start | bytes 442372
  93.1 23.6 %copy-start.12 = (bf16[512,640]{1,0:T(8,128)(2,1)S(1)}, bf16[512,640]{1,0:T(8,128)(2,1)}, u32[]{:S(2)}) copy-start(bf16[512,640]{1,0:T(8,128)(2,1)} %get-tuple-element.43) | copy-start | bytes 1966084
  106.7 21.8 %copy-start.3 = (bf16[512,640]{1,0:T(8,128)(2,1)S(1)}, bf16[512,640]{1,0:T(8,128)(2,1)}, u32[]{:S(2)}) copy-start(bf16[512,640]{1,0:T(8,128)(2,1)} %get-tuple-element.46.refs_5_) | copy-start | bytes 1966084
  116.7 11.8 %collective-permute-start.1 = (bf16[512,640]{1,0:T(8,128)(2,1)S(1)}, bf16[512,640]{1,0:T(8,128)(2,1)S(1)}, u32[]{:S(2)}, u32[]{:S(2)}) collective-permute-start(bf16[512,640]{1,0:T(8,128)(2,1)S(1)} %copy-done.12), channel_id=1, source_target_pairs={{0,64},{64,0},{128,192},{192,128},{1,65},{65,1},{129,193},{193,129... | collective-permute-start | bytes 1966088 | tf_op jit(solution)/shard_map/ppermute | solution.py:577
  126.7 1.8 %collective-permute-start = (bf16[512,384]{1,0:T(8,128)(2,1)S(1)}, bf16[512,384]{1,0:T(8,128)(2,1)S(1)}, u32[]{:S(2)}, u32[]{:S(2)}) collective-permute-start(bf16[512,384]{1,0:T(8,128)(2,1)S(1)} %shard_map.136), channel_id=1, source_target_pairs={{0,64},{64,0},{128,192},{192,128},{1,65},{65,1},{129,193},{193,129... | collective-permute-start | bytes 1179656 | tf_op jit(solution)/shard_map/ppermute | solution.py:577
  150.3 18.0 %copy-start.5 = (bf16[144,512]{1,0:T(8,128)(2,1)S(1)}, bf16[144,512]{1,0:T(8,128)(2,1)}, u32[]{:S(2)}) copy-start(bf16[144,512]{1,0:T(8,128)(2,1)} %get-tuple-element.48.refs_2_) | copy-start | bytes 442372
  160.6 4.4 %collective-permute-start.2 = (f32[80,128]{1,0:T(8,128)S(1)}, f32[80,128]{1,0:T(8,128)S(1)}, u32[]{:S(2)}, u32[]{:S(2)}) collective-permute-start(f32[80,128]{1,0:T(8,128)S(1)} %shard_map.140.refs_0_), channel_id=1, source_target_pairs={{0,128},{64,192},{128,0},{192,64},{1,129},{65,193},{129,1},{193,65... | collective-permute-start | bytes 122888 | tf_op jit(solution)/shard_map/ppermute | solution.py:577
  165.0 4.3 %collective-permute-start.3 = (f32[80,128]{1,0:T(8,128)S(1)}, f32[80,128]{1,0:T(8,128)S(1)}, u32[]{:S(2)}, u32[]{:S(2)}) collective-permute-start(f32[80,128]{1,0:T(8,128)S(1)} %shard_map.141.refs_1_), channel_id=1, source_target_pairs={{0,64},{64,0},{128,192},{192,128},{1,65},{65,1},{129,193},{193,129... | collective-permute-start | bytes 122888 | tf_op jit(solution)/shard_map/ppermute | solution.py:577

commit v10 on v9

--- a/solution.py
+++ b/solution.py
@@ -449,7 +449,7 @@
 
 
 def pieces_of(shape):
-    return 2 if shape[0] % 64 == 0 and shape[0] * shape[1] >= 2**18 else 1
+    return 4 if shape[0] % 64 == 0 and shape[0] * shape[1] >= 2**18 else 1
 
 
 def copies_of(source, target, sems, first):

time: 170 us -> 171 us (level)
  no operation moved by 1% of the time
where the time goes in v10:
time: 171 us; the launch traced here: 170 us
  blocking collectives  130 us (76%)
  Pallas kernels  20.3 us (12%)
  starting transfers between devices  15.6 us (9%)
  waiting for transfers between devices  2.8 us (2%)
    all_to_all x10, blocking collectives, exchange(): lax.all_to_all(array, 'rows', 0, 0, axis_index_groups=groups, tiled=True)  130 us
    pallas_call x16, Pallas kernels, call(): pl.pallas_call(wrapped, out_shape=[jax.ShapeDtypeStruct(*out) for out in...  20.3 us
    ppermute x4, starting transfers between devices, swap(): return lax.ppermute(array, 'dp', [(i, i ^ apart) for i in range(4)])  15.6 us
  transfers between devices with their start and end apart: 4, of which 2 were waited for; matrix products, arithmetic and copies ran while one was open for 0% of the time, Pallas kernels for 1%

profile of v10, /device:TPU:1, one launch (start us, length us, event | category | flops | bytes accessed | tf_op | source)
XLA Modules:
  0.0 170.1 jit_solution(11911452567818101600)
XLA Ops:
  0.7 0.0 copy-start
  0.7 0.0 copy-start.1
  0.8 0.0 copy-start.2
  0.8 0.0 copy-start.7
  0.8 0.0 copy-start.8
  0.8 0.0 copy-start.9
  0.8 2.2 %shard_map.128 = bf16[8,112,128]{2,1,0:T(8,128)(2,1)S(1)} custom-call(bf16[144,512]{1,0:T(8,128)(2,1)} %bitcast.9, bf16[2,512,768]{2,1,0:T(8,128)(2,1)} %refs_1_.9, f32[2,8]{1,0:T(2,128)} %refs_1_.8), custom_call_target="tpu_custom_call" | custom-call | tf_op jit(solution)/shard_map/pallas_call | solution.py:528
  3.0 16.3 %all_to_all.50.refs_0_.refs_2_ = bf16[8,112,128]{2,1,0:T(8,128)(2,1)S(1)} all-to-all(bf16[8,112,128]{2,1,0:T(8,128)(2,1)S(1)} %shard_map.128), channel_id=1, replica_groups={{0,2,4,6,1,3,5,7},{8,10,12,14,9,11,13,15},{16,18,20,22,17,19,21,23},{24..., dimensions={0} | all-to-all | bytes 458752 | tf_op jit(solution)/shard_map/all_to_all | solution.py:564
  19.3 1.3 shard_map.129
  20.6 11.5 %all_to_all.51.refs_0_.refs_2_ = bf16[8,40,128]{2,1,0:T(8,128)(2,1)S(1)} all-to-all(bf16[8,40,128]{2,1,0:T(8,128)(2,1)S(1)} %shard_map.129), channel_id=1, replica_groups={{0,2,4,6,1,3,5,7},{8,10,12,14,9,11,13,15},{16,18,20,22,17,19,21,23},{24..., dimensions={0} | all-to-all | bytes 163840 | tf_op jit(solution)/shard_map/all_to_all | solution.py:564
  32.1 0.0 copy-done
  32.1 0.0 copy-done.1
  32.1 0.0 copy-done.2
  32.1 0.0 copy-done.7
  32.1 0.0 copy-done.8
  32.1 0.0 copy-done.9
  32.1 0.0 copy-start.10
  32.1 0.0 copy-start.11
  32.1 0.0 copy-start.4
  32.1 1.2 shard_map.130
  33.4 13.0 %all_to_all.52.refs_0_.refs_2_ = bf16[8,112,128]{2,1,0:T(8,128)(2,1)S(1)} all-to-all(bf16[8,112,128]{2,1,0:T(8,128)(2,1)S(1)} %get-tuple-element.33), channel_id=1, replica_groups={{4,6,8,10,11,9,7,5},{12,14,16,18,19,17,15,13},{20,22,24,26,27,25,23,21}..., dimensions={0} | all-to-all | bytes 458752 | tf_op jit(solution)/shard_map/all_to_all | solution.py:564
  46.4 0.0 copy-done.10
  46.4 0.0 copy-done.11
  46.4 1.9 %shard_map.131 = bf16[8,40,128]{2,1,0:T(8,128)(2,1)S(1)} custom-call(bf16[8,112,128]{2,1,0:T(8,128)(2,1)S(1)} %all_to_all.52.refs_0_.refs_2_, s32[1]{0:T(128)} %bitcast.2.refs_1_.refs_4_, s32[192]{0:T(256)S(1)} %copy-done.10, s32[1,48]{1,0:T(1,128)S(1)} %bitcast.15), custom_call_target="tpu_custom_call" | custom-call | tf_op jit(solution)/shard_map/pallas_call | solution.py:528
  48.3 0.0 copy-start.6
  48.3 12.4 %all_to_all.53.refs_1_ = bf16[8,40,128]{2,1,0:T(8,128)(2,1)S(1)} all-to-all(bf16[8,40,128]{2,1,0:T(8,128)(2,1)S(1)} %shard_map.131), channel_id=1, replica_groups={{4,6,8,10,11,9,7,5},{12,14,16,18,19,17,15,13},{20,22,24,26,27,25,23,21}..., dimensions={0} | all-to-all | bytes 163840 | tf_op jit(solution)/shard_map/all_to_all | solution.py:564
  60.8 0.0 copy-done.4
  60.8 0.9 shard_map.132
  61.6 12.1 %all_to_all.54.refs_3_ = bf16[8,40,128]{2,1,0:T(8,128)(2,1)S(1)} all-to-all(bf16[8,40,128]{2,1,0:T(8,128)(2,1)S(1)} %get-tuple-element.35), channel_id=1, replica_groups={{4,6,8,10,11,9,7,5},{12,14,16,18,19,17,15,13},{20,22,24,26,27,25,23,21}..., dimensions={0} | all-to-all | bytes 163840 | tf_op jit(solution)/shard_map/all_to_all | solution.py:564
  73.8 3.6 %shard_map.133 = bf16[8,112,128]{2,1,0:T(8,128)(2,1)S(1)} custom-call(s32[1]{0:T(128)} %bitcast.1.refs_0_, f32[2,8]{1,0:T(2,128)S(1)} %copy-done.8, bf16[8,112,128]{2,1,0:T(8,128)(2,1)S(1)} %all_to_all.52.refs_0_.refs_2_, bf16[8,40,128]{2,1,0:T(8,128)(2,1)S(1)} %all_to_all.54.refs_3_, s32[1]{0:T(128)} %bitcast.2.refs_1_.refs_4_, s32[192]{0:T(256)S(1)} %copy-done.10, ...), custom_call_target="tpu_custom_call" | custom-call | tf_op jit(solution)/shard_map/pallas_call | solution.py:528
  77.4 13.5 %all_to_all.55.refs_1_ = bf16[8,112,128]{2,1,0:T(8,128)(2,1)S(1)} all-to-all(bf16[8,112,128]{2,1,0:T(8,128)(2,1)S(1)} %shard_map.133), channel_id=1, replica_groups={{4,6,8,10,11,9,7,5},{12,14,16,18,19,17,15,13},{20,22,24,26,27,25,23,21}..., dimensions={0} | all-to-all | bytes 458752 | tf_op jit(solution)/shard_map/all_to_all | solution.py:564
  90.9 0.0 copy-done.6
  90.9 2.4 %shard_map.134 = (bf16[8,40,128]{2,1,0:T(8,128)(2,1)S(1)}, f32[8,512]{1,0:T(8,128)S(1)}, bf16[144,512]{1,0:T(8,128)(2,1)}, bf16[512,640]{1,0:T(8,128)(2,1)}, bf16[512,640]{1,0:T(8,128)(2,1)}) custom-call(s32[1]{0:T(128)} %bitcast.3.refs_0_, bf16[8,112,128]{2,1,0:T(8,128)(2,1)S(1)} %all_to_all.55.refs_1_, bf16[8,40,128]{2,1,0:T(8,128)(2,1)S(1)} %all_to_all.51.refs_0_.refs_2_, ...), custom_call_target="tpu_custom_call" | custom-call | tf_op jit(solution)/shard_map/pallas_call | solution.py:528
  93.2 0.0 copy-start.12
  93.2 10.1 %all_to_all.56.refs_3_ = bf16[8,40,128]{2,1,0:T(8,128)(2,1)S(1)} all-to-all(bf16[8,40,128]{2,1,0:T(8,128)(2,1)S(1)} %get-tuple-element.39), channel_id=1, replica_groups={{0,2,4,6,1,3,5,7},{8,10,12,14,9,11,13,15},{16,18,20,22,17,19,21,23},{24..., dimensions={0} | all-to-all | bytes 163840 | tf_op jit(solution)/shard_map/all_to_all | solution.py:564
  103.3 3.4 %shard_map.135 = bf16[8,112,128]{2,1,0:T(8,128)(2,1)S(1)} custom-call(s32[1]{0:T(128)} %bitcast.refs_0_, f32[2,8]{1,0:T(2,128)S(1)} %copy-done.8, bf16[8,112,128]{2,1,0:T(8,128)(2,1)S(1)} %all_to_all.50.refs_0_.refs_2_, bf16[8,40,128]{2,1,0:T(8,128)(2,1)S(1)} %all_to_all.56.refs_3_), custom_call_target="tpu_custom_call" | custom-call | tf_op jit(solution)/shard_map/pallas_call | solution.py:528
  106.8 0.0 copy-start.3
  106.8 10.0 %all_to_all.57.refs_1_.refs_0_ = bf16[8,112,128]{2,1,0:T(8,128)(2,1)S(1)} all-to-all(bf16[8,112,128]{2,1,0:T(8,128)(2,1)S(1)} %shard_map.135), channel_id=1, replica_groups={{0,2,4,6,1,3,5,7},{8,10,12,14,9,11,13,15},{16,18,20,22,17,19,21,23},{24..., dimensions={0} | all-to-all | bytes 458752 | tf_op jit(solution)/shard_map/all_to_all | solution.py:564
  116.8 0.0 copy-done.12
  116.8 9.4 %collective-permute-start.1 = (bf16[512,640]{1,0:T(8,128)(2,1)S(1)}, bf16[512,640]{1,0:T(8,128)(2,1)S(1)}, u32[]{:S(2)}, u32[]{:S(2)}) collective-permute-start(bf16[512,640]{1,0:T(8,128)(2,1)S(1)} %copy-done.12), channel_id=1, source_target_pairs={{0,64},{64,0},{128,192},{192,128},{1,65},{65,1},{129,193},{193,129... | collective-permute-start | bytes 1966088 | tf_op jit(solution)/shard_map/ppermute | solution.py:577
  126.2 0.5 shard_map.136
  126.7 0.1 collective-permute-start
  126.8 0.5 shard_map.137.refs_0_
  127.4 1.2 collective-permute-done.refs_1_
  128.6 0.0 collective-permute-done.1.refs_2_
  128.6 0.0 copy-done.3
  128.6 0.4 shard_map.138
  129.0 21.3 %all_to_all.58.refs_0_ = bf16[8,528,128]{2,1,0:T(8,128)(2,1)S(1)} all-to-all(bf16[8,528,128]{2,1,0:T(8,128)(2,1)S(1)} %shard_map.138), channel_id=1, replica_groups={{56,48,40,32,24,16,8,0},{57,49,41,33,25,17,9,1},{58,50,42,34,26,18,10,2..., dimensions={0} | all-to-all | bytes 2162688 | tf_op jit(solution)/shard_map/all_to_all | solution.py:564
  150.3 0.0 copy-start.5
  150.3 0.2 shard_map.139
  150.5 10.1 %all_to_all.59.refs_0_ = bf16[8,80,128]{2,1,0:T(8,128)(2,1)S(1)} all-to-all(bf16[8,80,128]{2,1,0:T(8,128)(2,1)S(1)} %shard_map.139), channel_id=1, replica_groups={{0,2,4,6,1,3,5,7},{8,10,12,14,9,11,13,15},{16,18,20,22,17,19,21,23},{24..., dimensions={0} | all-to-all | bytes 327680 | tf_op jit(solution)/shard_map/all_to_all | solution.py:564
  160.7 2.8 %collective-permute-start.2 = (f32[80,128]{1,0:T(8,128)S(1)}, f32[80,128]{1,0:T(8,128)S(1)}, u32[]{:S(2)}, u32[]{:S(2)}) collective-permute-start(f32[80,128]{1,0:T(8,128)S(1)} %shard_map.140.refs_0_), channel_id=1, source_target_pairs={{0,128},{64,192},{128,0},{192,64},{1,129},{65,193},{129,1},{193,65... | collective-permute-start | bytes 122888 | tf_op jit(solution)/shard_map/ppermute | solution.py:577
  163.5 1.6 collective-permute-done.2.refs_1_
  165.1 3.2 %collective-permute-start.3 = (f32[80,128]{1,0:T(8,128)S(1)}, f32[80,128]{1,0:T(8,128)S(1)}, u32[]{:S(2)}, u32[]{:S(2)}) collective-permute-start(f32[80,128]{1,0:T(8,128)S(1)} %shard_map.141.refs_1_), channel_id=1, source_target_pairs={{0,64},{64,0},{128,192},{192,128},{1,65},{65,1},{129,193},{193,129... | collective-permute-start | bytes 122888 | tf_op jit(solution)/shard_map/ppermute | solution.py:577
  168.4 0.0 copy-done.5
  168.4 1.1 shard_map.142
  169.4 0.0 collective-permute-done.3.refs_2_
  169.5 0.6 shard_map.143
  (2 shorter events, 0.0 us)
Async XLA Ops:
  0.7 31.3 %copy-start = (bf16[2,512,768]{2,1,0:T(8,128)(2,1)S(1)}, bf16[2,512,768]{2,1,0:T(8,128)(2,1)}, u32[]{:S(2)}) copy-start(bf16[2,512,768]{2,1,0:T(8,128)(2,1)} %refs_1_.9) | copy-start | bytes 4718596
  0.7 31.3 %copy-start.1 = (bf16[2,256,512]{2,1,0:T(8,128)(2,1)S(1)}, bf16[2,256,512]{2,1,0:T(8,128)(2,1)}, u32[]{:S(2)}) copy-start(bf16[2,256,512]{2,1,0:T(8,128)(2,1)} %refs_5_.5) | copy-start | bytes 1572868
  0.8 31.3 %copy-start.2 = (bf16[1,3,48,512]{3,2,1,0:T(8,128)(2,1)S(1)}, bf16[1,3,48,512]{3,2,1,0:T(8,128)(2,1)}, u32[]{:S(2)}) copy-start(bf16[1,3,48,512]{3,2,1,0:T(8,128)(2,1)} %param.9) | copy-start | bytes 442372
  0.8 31.3 %copy-start.7 = (f32[2,512]{1,0:T(2,128)S(1)}, f32[2,512]{1,0:T(2,128)}, u32[]{:S(2)}) copy-start(f32[2,512]{1,0:T(2,128)} %refs_3_.3) | copy-start | bytes 12292
  0.8 31.3 %copy-start.8 = (f32[2,8]{1,0:T(2,128)S(1)}, f32[2,8]{1,0:T(2,128)}, u32[]{:S(2)}) copy-start(f32[2,8]{1,0:T(2,128)} %refs_1_.8) | copy-start | bytes 196
  0.8 31.3 %copy-start.9 = (f32[2,512]{1,0:T(2,128)S(1)}, f32[2,512]{1,0:T(2,128)}, u32[]{:S(2)}) copy-start(f32[2,512]{1,0:T(2,128)} %refs_3_.2) | copy-start | bytes 12292
  32.1 14.3 %copy-start.10 = (s32[192]{0:T(256)S(1)}, s32[192]{0:T(256)}, u32[]{:S(2)}) copy-start(s32[192]{0:T(256)} %refs_5_.4) | copy-start | bytes 2308
  32.1 14.3 %copy-start.11 = (s32[48]{0:T(128)S(1)}, s32[48]{0:T(128)}, u32[]{:S(2)}) copy-start(s32[48]{0:T(128)} %param.17) | copy-start | bytes 580
  32.1 28.6 %copy-start.4 = (bf16[1,3,48,512]{3,2,1,0:T(8,128)(2,1)S(1)}, bf16[1,3,48,512]{3,2,1,0:T(8,128)(2,1)}, u32[]{:S(2)}) copy-start(bf16[1,3,48,512]{3,2,1,0:T(8,128)(2,1)} %param.10) | copy-start | bytes 442372
  48.3 42.5 %copy-start.6 = (bf16[144,512]{1,0:T(8,128)(2,1)S(1)}, bf16[144,512]{1,0:T(8,128)(2,1)}, u32[]{:S(2)}) copy-start(bf16[144,512]{1,0:T(8,128)(2,1)} %get-tuple-element.38.refs_9_) | copy-start | bytes 442372
  93.2 23.6 %copy-start.12 = (bf16[512,640]{1,0:T(8,128)(2,1)S(1)}, bf16[512,640]{1,0:T(8,128)(2,1)}, u32[]{:S(2)}) copy-start(bf16[512,640]{1,0:T(8,128)(2,1)} %get-tuple-element.43) | copy-start | bytes 1966084
  106.8 21.8 %copy-start.3 = (bf16[512,640]{1,0:T(8,128)(2,1)S(1)}, bf16[512,640]{1,0:T(8,128)(2,1)}, u32[]{:S(2)}) copy-start(bf16[512,640]{1,0:T(8,128)(2,1)} %get-tuple-element.46.refs_5_) | copy-start | bytes 1966084
  116.8 11.8 %collective-permute-start.1 = (bf16[512,640]{1,0:T(8,128)(2,1)S(1)}, bf16[512,640]{1,0:T(8,128)(2,1)S(1)}, u32[]{:S(2)}, u32[]{:S(2)}) collective-permute-start(bf16[512,640]{1,0:T(8,128)(2,1)S(1)} %copy-done.12), channel_id=1, source_target_pairs={{0,64},{64,0},{128,192},{192,128},{1,65},{65,1},{129,193},{193,129... | collective-permute-start | bytes 1966088 | tf_op jit(solution)/shard_map/ppermute | solution.py:577
  126.7 1.8 %collective-permute-start = (bf16[512,384]{1,0:T(8,128)(2,1)S(1)}, bf16[512,384]{1,0:T(8,128)(2,1)S(1)}, u32[]{:S(2)}, u32[]{:S(2)}) collective-permute-start(bf16[512,384]{1,0:T(8,128)(2,1)S(1)} %shard_map.136), channel_id=1, source_target_pairs={{0,64},{64,0},{128,192},{192,128},{1,65},{65,1},{129,193},{193,129... | collective-permute-start | bytes 1179656 | tf_op jit(solution)/shard_map/ppermute | solution.py:577
  150.3 18.0 %copy-start.5 = (bf16[144,512]{1,0:T(8,128)(2,1)S(1)}, bf16[144,512]{1,0:T(8,128)(2,1)}, u32[]{:S(2)}) copy-start(bf16[144,512]{1,0:T(8,128)(2,1)} %get-tuple-element.48.refs_2_) | copy-start | bytes 442372
  160.7 4.4 %collective-permute-start.2 = (f32[80,128]{1,0:T(8,128)S(1)}, f32[80,128]{1,0:T(8,128)S(1)}, u32[]{:S(2)}, u32[]{:S(2)}) collective-permute-start(f32[80,128]{1,0:T(8,128)S(1)} %shard_map.140.refs_0_), channel_id=1, source_target_pairs={{0,128},{64,192},{128,0},{192,64},{1,129},{65,193},{129,1},{193,65... | collective-permute-start | bytes 122888 | tf_op jit(solution)/shard_map/ppermute | solution.py:577
  165.1 4.3 %collective-permute-start.3 = (f32[80,128]{1,0:T(8,128)S(1)}, f32[80,128]{1,0:T(8,128)S(1)}, u32[]{:S(2)}, u32[]{:S(2)}) collective-permute-start(f32[80,128]{1,0:T(8,128)S(1)} %shard_map.141.refs_1_), channel_id=1, source_target_pairs={{0,64},{64,0},{128,192},{192,128},{1,65},{65,1},{129,193},{193,129... | collective-permute-start | bytes 122888 | tf_op jit(solution)/shard_map/ppermute | solution.py:577
